TPU v7x, 128 devices: a whole 4x4x4 slice. The times are simulated.
128 devices in a mesh: aux: 8 (over z, core), bas: 16 (over y, x).
Axes of the slice: x: 4, y: 4, z: 4, core: 2. Of those that a mesh axis runs over, the one named last changes fastest.
Arguments:
- three_index: bfloat16 [6144, 32, 4096], P(('aux', 'bas')), may hold values from -6 to 6
- block_size: int32 [32], replicated, may hold values from 64 to 128, as said below
- screen: int32 [32, 5], replicated, may hold values from 0 to 1, as said below
Outputs:
- exchange_band: float32 [4096, 1152], P(('bas', 'aux'))
Inputs may be any that keep to these rules, and one draw needn't show every extreme that they name: `block_size`: block sizes lie between 64 and 128; some block is full. screen[a, 0] = 1 for every block a; screen[a, d] = 0 wherever a + d >= 32.
All inputs are finite; a program needn't handle non-finite values.
Results may differ from a plain program's by a relative error of at most 0.0038.
Values may be sent and summed in bfloat16 or wider, within the bound.
No kernel may reach another device: no remote copies, remote signals or barrier semaphores. Data moves between devices by JAX's collectives and lax.ppermute only.
A program may use at most 448 MiB of HBM per device.

v0:
```python
import math

import jax
import jax.numpy as jnp
from jax import lax
from jax.sharding import PartitionSpec as P

AUX = 6144
OCC = 32
BW = 128
BLK_DEV = 2
BAND = 5


def from_behind(value, axis, steps):
    count = lax.axis_size(axis)
    initial, last = (max(0, -steps), min(count, count - steps))
    return lax.ppermute(value, axis, [(source, source + steps) for source in range(initial, last)])


def masked_tile(left_block, right_block, left_size, right_size, kept_flag, factor):

    def compute(unused):
        product = lax.dot_general(
            left_block,
            right_block,
            (((0, 1), (0, 1)), ((), ())),
            preferred_element_type=jnp.float32,
        )
        position = jnp.arange(left_block.shape[2], dtype=jnp.int32)
        row_mask = (position < left_size).astype(jnp.float32)
        col_mask = (position < right_size).astype(jnp.float32)
        return product * factor * row_mask[:, None] * col_mask[None, :]

    def skipped(unused):
        return jnp.zeros((left_block.shape[2], right_block.shape[2]), jnp.float32)

    return lax.cond(kept_flag > 0, compute, skipped, 0)


def assemble_band(upper_tiles):
    slot_count = 2 * BAND - 1
    zero_tile = jnp.zeros((BW, BW), jnp.float32)
    panel_tiles = [[zero_tile for slot in range(slot_count)] for local_row in range(BLK_DEV)]
    outgoing = [
        [[zero_tile for slot in range(BAND - 1)] for local_row in range(BLK_DEV)]
        for section in range(2)
    ]
    for local_row in range(BLK_DEV):
        for offset in range(BAND):
            tile = upper_tiles[local_row][offset]
            panel_tiles[local_row][BAND - 1 + offset] = tile
            if offset > 0:
                window_slot = local_row + offset
                section = window_slot // BLK_DEV
                target = window_slot - section * BLK_DEV
                if section == 0:
                    panel_tiles[target][BAND - 1 - offset] = tile.T
                else:
                    outgoing[section - 1][target][BAND - 1 - offset] = tile.T
    row_panel = jnp.concatenate(
        [jnp.concatenate(panel_tiles[local_row], axis=1) for local_row in range(BLK_DEV)], axis=0
    )
    to_next = jnp.concatenate(
        [jnp.concatenate(outgoing[0][local_row], axis=1) for local_row in range(BLK_DEV)], axis=0
    )
    to_second = jnp.concatenate(
        [jnp.concatenate(outgoing[1][local_row], axis=1) for local_row in range(BLK_DEV)], axis=0
    )
    from_previous = from_behind(to_next.astype(jnp.bfloat16), "bas", 1).astype(to_next.dtype)
    from_second = from_behind(to_second.astype(jnp.bfloat16), "bas", 2).astype(to_second.dtype)
    lower_tiles = from_previous + from_second
    filler = jnp.zeros((lower_tiles.shape[0], BAND * BW), jnp.float32)
    return row_panel + jnp.concatenate([lower_tiles, filler], axis=1)


def owner_upper(window, block_size, screen, owner_index, factor):
    total_blocks = screen.shape[0]
    first_block = owner_index * BLK_DEV
    upper_tiles = []
    for local_row in range(BLK_DEV):
        row_block = first_block + local_row
        left_block = window[:, :, local_row * BW : (local_row + 1) * BW]
        row_tiles = []
        for offset in range(BAND):
            window_slot = local_row + offset
            clamped = jnp.minimum(row_block + offset, total_blocks - 1)
            right_block = window[:, :, window_slot * BW : (window_slot + 1) * BW]
            row_tiles.append(
                masked_tile(
                    left_block,
                    right_block,
                    block_size[row_block],
                    block_size[clamped],
                    screen[row_block, offset],
                    factor,
                )
            )
        upper_tiles.append(row_tiles)
    return upper_tiles


def local(three_index, block_size, screen):
    factor = 1.0 / math.sqrt(AUX * OCC)
    owner_index = lax.axis_index("bas")
    owned_blocks = lax.all_to_all(three_index, "bas", split_axis=2, concat_axis=0, tiled=True)
    following = from_behind(owned_blocks, "bas", -1)
    beyond = from_behind(owned_blocks, "bas", -2)
    window = jnp.concatenate([owned_blocks, following, beyond], axis=2)
    upper_tiles = owner_upper(window, block_size, screen, owner_index, factor)
    row_panel = assemble_band(upper_tiles)
    return lax.psum_scatter(row_panel, "aux", scatter_dimension=0, tiled=True)


def solution(mesh):
    in_specs = (P(("aux", "bas"), None, None), P(), P())
    out_specs = P(("bas", "aux"), None)
    return jax.shard_map(local, mesh=mesh, in_specs=in_specs, out_specs=out_specs, check_vma=False)
```

profile of v0, /device:TPU:1, one launch (start us, length us, event | category | flops | bytes accessed | tf_op | source)
XLA Modules:
  0.0 1017.5 jit_solution(5132597096739234014)
XLA Ops:
  6.5 55.4 %copy.113 = bf16[48,32,4096]{0,1,2:T(8,128)(2,1)} copy(bf16[48,32,4096]{2,1,0:T(8,128)(2,1)} %param.23) | data formatting | bytes 25165824 | tf_op args[0]
  62.0 51.7 %reshape.160 = bf16[16,2,196608]{2,1,0:T(2,128)(2,1)} reshape(bf16[4096,32,48]{2,1,0:T(8,128)(2,1)} %bitcast.128) | data formatting | bytes 25165824
  113.7 147.4 %all_to_all.18 = bf16[16,2,196608]{2,1,0:T(2,128)(2,1)} all-to-all(bf16[16,2,196608]{2,1,0:T(2,128)(2,1)} %reshape.160), channel_id=1, replica_groups=mesh['aux'=8,'bas'=16] {'bas'}, dimensions={0} | all-to-all | bytes 25165824 | tf_op jit(solution)/shard_map/all_to_all | solution.py:106
  261.1 33.7 %reshape.161 = bf16[4096,32,48]{2,1,0:T(8,128)(2,1)} reshape(bf16[16,2,196608]{2,1,0:T(2,128)(2,1)} %all_to_all.18) | data formatting | bytes 25165824
  294.8 45.2 %copy.115 = bf16[16,48,32,256]{3,2,1,0:T(8,128)(2,1)} copy(bf16[16,48,32,256]{1,2,3,0:T(8,128)(2,1)} %bitcast.127) | data formatting | bytes 25165824 | tf_op jit(solution)/shard_map/all_to_all | solution.py:106
  340.0 1.3 collective-permute-start
  341.3 1.3 collective-permute-start.1
  342.6 0.7 constant_dynamic-slice_fusion.1
  349.4 0.7 fusion.33
  350.1 11.1 %fusion.32 = (bf16[768,32,128]{2,1,0:T(8,128)(2,1)}, bf16[768,32,128]{2,1,0:T(8,128)(2,1)}) fusion(bf16[768,32,256]{2,1,0:T(8,128)(2,1)} %bitcast.131), kind=kLoop, calls=%fused_computation.89 | loop fusion | bytes 25165824 | tf_op jit(solution)/shard_map/slice | solution.py:88
  361.2 7.7 conditional.11
  361.2 0.6 compare_convert_fusion.1
  361.8 0.6 compare_select_fusion.1
  362.4 6.5 fusion.3
  369.0 8.7 conditional.10
  369.2 0.6 dynamic_slice.11
  369.8 0.6 compare_convert_fusion
  370.4 0.6 compare_select_fusion
  371.1 6.6 fusion.1
  377.6 7.8 conditional.15
  377.7 0.6 compare_convert_fusion.5
  378.9 6.6 fusion.11
  385.5 226.5 %collective-permute-done = bf16[768,32,256]{2,1,0:T(8,128)(2,1)} collective-permute-done((bf16[768,32,256]{2,1,0:T(8,128)(2,1)}, bf16[768,32,256]{2,1,0:T(8,128)(2,1)}, u32[]{:S(2)}, u32[]{:S(2)}) %collective-permute-start) | collective-permute-done | bytes 12582944 | tf_op jit(solution)/shard_map/ppermute | solution.py:18
  612.0 10.9 %fusion.31 = (bf16[768,32,128]{2,1,0:T(8,128)(2,1)}, bf16[768,32,128]{2,1,0:T(8,128)(2,1)}) fusion(bf16[768,32,256]{2,1,0:T(8,128)(2,1)} %collective-permute-done), kind=kLoop, calls=%fused_computation.88 | loop fusion | bytes 25165824 | tf_op jit(solution)/shard_map/slice | solution.py:88
  623.0 6.5 slice.36
  629.4 7.7 conditional.12
  629.4 0.6 compare_convert_fusion.2
  630.1 0.6 compare_select_fusion.2
  630.7 6.5 fusion.5
  637.3 7.7 conditional.13
  637.9 0.6 compare_select_fusion.3
  638.5 6.5 fusion.7
  645.1 7.7 conditional.16
  645.1 0.6 compare_convert_fusion.6
  646.3 6.5 fusion.13
  652.9 7.8 conditional.17
  654.3 6.5 fusion.15
  660.9 23.9 %conditional.19 = (f32[128,128]{1,0:T(8,128)S(1)}) conditional(s32[]{:T(128)} %bitcast.33, () %tuple.90, (bf16[768,32,256]{2,1,0:T(8,128)(2,1)}, bf16[768,32,128]{2,1,0:T(8,128)(2,1)}, s32[]{:T(128)}, s32[]{:T(128)}, s32[32]{0:T(128)S(1)}) %tuple.181), branch_computations={%region_18.0_spmd, %region_19.0_spmd} | conditional | flops 805339648 | bytes 50399316 | solution.py:38
  660.9 9.0 copy.133
  669.9 3.8 slice.31
  673.7 0.6 dynamic_slice.12
  674.4 0.7 compare_convert_fusion.9
  675.6 9.2 fusion.26
  685.5 1.3 collective-permute-start.3
  686.8 275.4 %collective-permute-start.2 = (bf16[256,512]{1,0:T(8,128)(2,1)S(1)}, bf16[256,512]{1,0:T(8,128)(2,1)S(1)}, u32[]{:S(2)}, u32[]{:S(2)}) collective-permute-start(bf16[256,512]{1,0:T(8,128)(2,1)S(1)} %get-tuple-element.411), channel_id=1, source_target_pairs={{0,1},{1,2},{2,3},{3,4},{4,5},{5,6},{6,7},{7,8},{8,9},{9,10},{10,1... | collective-permute-start | bytes 786440 | tf_op jit(solution)/shard_map/ppermute | solution.py:18
  962.3 3.2 collective-permute-done.2
  965.6 1.1 maximum_add_fusion
  966.8 43.4 %reduce-scatter.2.cloned.1.call-done = f32[32,1152]{1,0:T(8,128)} async-done(((f32[256,1152]{1,0:T(8,128)}), f32[32,1152]{1,0:T(8,128)}) %reduce-scatter.2.cloned.1.call-update) | async-done | bytes 147472 | tf_op jit(solution)/shard_map/reduce_scatter | solution.py:112
  (42 shorter events, 4.8 us)
Async XLA Ops:
  6.5 1003.6 %reduce-scatter.2.cloned.1.call-start = ((), (), s32[]{:S(2)}) async-start(), calls=%async_computation.2 | async-start | bytes 1327104 | tf_op jit(solution)/shard_map/reduce_scatter | solution.py:112
  294.8 47.8 %copy-start.1 = (s32[32,5]{0,1:T(8,128)S(1)}, s32[32,5]{0,1:T(8,128)}, u32[]{:S(2)}) copy-start(s32[32,5]{0,1:T(8,128)} %param.25) | copy-start | bytes 1924
  294.8 54.6 %copy-start = (s32[32]{0:T(128)S(1)}, s32[32]{0:T(128)}, u32[]{:S(2)}) copy-start(s32[32]{0:T(128)} %param.24) | copy-start | bytes 388
  340.0 272.0 %collective-permute-start = (bf16[768,32,256]{2,1,0:T(8,128)(2,1)}, bf16[768,32,256]{2,1,0:T(8,128)(2,1)}, u32[]{:S(2)}, u32[]{:S(2)}) collective-permute-start(bf16[768,32,256]{2,1,0:T(8,128)(2,1)} %bitcast.129), channel_id=1, source_target_pairs={{1,0},{2,1},{3,2},{4,3},{5,4},{6,5},{7,6},{8,7},{9,8},{10,9},{11,1... | collective-permute-start | bytes 37748744 | tf_op jit(solution)/shard_map/ppermute | solution.py:18
  341.3 281.7 %collective-permute-start.1 = (bf16[768,32,256]{2,1,0:T(8,128)(2,1)}, bf16[768,32,256]{2,1,0:T(8,128)(2,1)}, u32[]{:S(2)}, u32[]{:S(2)}) collective-permute-start(bf16[768,32,256]{2,1,0:T(8,128)(2,1)} %bitcast.130), channel_id=1, source_target_pairs={{2,0},{3,1},{4,2},{5,3},{6,4},{7,5},{8,6},{9,7},{10,8},{11,9},{12,... | collective-permute-start | bytes 37748744 | tf_op jit(solution)/shard_map/ppermute | solution.py:18
  685.5 276.8 %collective-permute-start.3 = (bf16[256,512]{1,0:T(8,128)(2,1)S(1)}, bf16[256,512]{1,0:T(8,128)(2,1)S(1)}, u32[]{:S(2)}, u32[]{:S(2)}) collective-permute-start(bf16[256,512]{1,0:T(8,128)(2,1)S(1)} %get-tuple-element.412), channel_id=1, source_target_pairs={{0,2},{1,3},{2,4},{3,5},{4,6},{5,7},{6,8},{7,9},{8,10},{9,11},{10,... | collective-permute-start | bytes 786440 | tf_op jit(solution)/shard_map/ppermute | solution.py:18
  686.8 278.7 %collective-permute-start.2 = (bf16[256,512]{1,0:T(8,128)(2,1)S(1)}, bf16[256,512]{1,0:T(8,128)(2,1)S(1)}, u32[]{:S(2)}, u32[]{:S(2)}) collective-permute-start(bf16[256,512]{1,0:T(8,128)(2,1)S(1)} %get-tuple-element.411), channel_id=1, source_target_pairs={{0,1},{1,2},{2,3},{3,4},{4,5},{5,6},{6,7},{7,8},{8,9},{9,10},{10,1... | collective-permute-start | bytes 786440 | tf_op jit(solution)/shard_map/ppermute | solution.py:18
Sparse Core Ops, SparseCore 0:
  966.9 43.2 reduce-scatter.1
where the time goes:
time: 1030 us; the launch traced here: 1020 us
  starting transfers between devices  279 us (27%)
  waiting for transfers between devices  273 us (27%)
  local copies, waits for them, and re-layouts  231 us (22%)
  blocking collectives  147 us (14%)
  matrix products  54.6 us (5%)
  between operations  20.2 us (2%)
  other arithmetic  11 us (1%)
    ppermute x4, starting transfers between devices, from_behind(): lax.ppermute(value, axis, [(source, source + steps) for source in range(i...  279 us
    ppermute x4, waiting for transfers between devices, from_behind(): lax.ppermute(value, axis, [(source, source + steps) for source in range(i...  230 us
    all_to_all x1, blocking collectives, local(): lax.all_to_all(three_index, 'bas', split_axis=2, concat_axis=0, tiled=True)  147 us
    unnamed x18, local copies, waits for them, and re-layouts  141 us
    dot_general x8, matrix products, compute(): lax.dot_general(left_block, right_block, (((0, 1), (0, 1)), ((), ())), pr...  54.6 us
    all_to_all x1, local copies, waits for them, and re-layouts, local(): lax.all_to_all(three_index, 'bas', split_axis=2, concat_axis=0, tiled=True)  45.2 us
    reduce_scatter x1, waiting for transfers between devices, local(): return lax.psum_scatter(row_panel, 'aux', scatter_dimension=0, tiled=True)  43.4 us
    slice x4, local copies, waits for them, and re-layouts, owner_upper(): right_block = window[:, :, window_slot * BW:(window_slot + 1) * BW]  32.3 us
  transfers between devices with their start and end apart: 5, of which 3 were waited for; matrix products, arithmetic and copies ran while one was open for 5% of the time, Pallas kernels for 0%

commit v1 on v0

v1 whole, which is shorter than its diff:
```python
import functools
import math

import jax
import jax.numpy as jnp
from jax import lax
from jax.experimental import pallas as pl
from jax.experimental.pallas import tpu as pltpu
from jax.sharding import PartitionSpec as P

AUX = 6144
OCC = 32
BW = 128
BAND = 5
NB = 32
OWNERS = 16
PAIR = 2 * BW
AXES = ("aux", "bas")
F32 = jnp.float32
BF16 = jnp.bfloat16

TILES = (
    ((0, 0), (0, 2), (0, 3), (1, 1), (1, 2)),
    ((1, 0), (0, 1), (0, 4), (1, 3), (1, 4)),
)
PANEL = {
    (0, 0): ((0, 1, 2, 5, 7), (4, 6, 7, 2, 3)),
    (1, 0): ((1, 2, 6, 7), (5, 8, 0, 1)),
    (0, 1): ((3, 4, 6, 8), (5, 6, 1, 2)),
    (1, 1): ((0, 3, 4, 5, 8), (4, 7, 8, 3, 0)),
}
GROUPS = (
    ((1, 0), (1, 1), (1, 2), (1, 3), (0, 1), (2, 1), (3, 1)),
    ((3, 0), (3, 2), (3, 3), (0, 3), (2, 3)),
    ((2, 0), (2, 2), (0, 2)),
    ((0, 0),),
)


def device(z, c, y, x):
    return (z * 2 + c) * 16 + y * 4 + x


EVERY = [(z, c, y, x) for z in range(4) for c in range(2) for y in range(4) for x in range(4)]


def core_pairs():
    return [(device(z, c, y, x), device(z, 1 - c, y, x)) for z, c, y, x in EVERY]


def plane_pairs(step, first):
    pairs = []
    for z, c, y, x in EVERY:
        if (c == 0) == first:
            target = device(z, c, (y + step) % 4, x)
        else:
            target = device(z, c, y, (x + step) % 4)
        pairs.append((device(z, c, y, x), target))
    return pairs


def mirror_pairs():
    pairs = []
    for z, c, y, x in EVERY:
        owner = y * 4 + x + 1 + c
        if owner < OWNERS:
            pairs.append((device(z, c, y, x), device(z, c, owner // 4, owner % 4)))
    return pairs


def z_pairs(step):
    return [(device(z, c, y, x), device((z + step) % 4, c, y, x)) for z, c, y, x in EVERY]


def send(value, pairs):
    return lax.ppermute(value, AXES, pairs)


def tiles_kernel(owner_ref, place_ref, core_ref, left_ref, next_ref, beyond_ref, mine_ref, theirs_ref):
    left = left_ref[...]
    products = [
        lax.dot_general(left, right, (((0,), (0,)), ((), ())), preferred_element_type=F32)
        for right in (left, next_ref[...], beyond_ref[...])
    ]

    def tile(row, offset):
        slot = row + offset
        part = products[slot // 2]
        return part[row * BW : (row + 1) * BW, (slot % 2) * BW : (slot % 2 + 1) * BW].astype(BF16)

    def put(mine, theirs):
        for place in range(BAND):
            mine_ref[0, place] = tile(*TILES[mine][place])
            theirs_ref[0, place] = tile(*TILES[theirs][place])

    core = core_ref[0]

    @pl.when(core == 0)
    def _():
        put(0, 1)

    @pl.when(core != 0)
    def _():
        put(1, 0)


def partial_tiles(flat, owners, places, core):
    count = len(places)
    depth = flat.shape[0]

    def column(ahead):
        return pl.BlockSpec(
            (depth, PAIR), lambda i, owner, place, core: (0, jnp.minimum(owner[i] + ahead, OWNERS - 1))
        )

    shape = jax.ShapeDtypeStruct((count, BAND, BW, BW), BF16)
    return pl.pallas_call(
        tiles_kernel,
        grid_spec=pltpu.PrefetchScalarGridSpec(
            num_scalar_prefetch=3,
            grid=(count,),
            in_specs=[column(0), column(1), column(2)],
            out_specs=[
                pl.BlockSpec((1, BAND, BW, BW), lambda i, owner, place, core: (i, 0, 0, 0)),
                pl.BlockSpec((1, BAND, BW, BW), lambda i, owner, place, core: (place[i], 0, 0, 0)),
            ],
        ),
        out_shape=[shape, shape],
        compiler_params=pltpu.CompilerParams(vmem_limit_bytes=32 << 20),
        cost_estimate=pl.CostEstimate(
            flops=count * 2 * PAIR * 3 * PAIR * depth,
            bytes_accessed=count * (3 * depth * PAIR * 2 + 10 * BW * BW * 2),
            transcendentals=0,
        ),
    )(owners, jnp.array(places, jnp.int32), core, flat, flat, flat)


def pack_kernel(where_ref, upper_ref, lower_ref, out_ref):
    core = where_ref[0]
    z = where_ref[1]
    for mine in range(2):

        @pl.when(core == mine)
        def _():
            for row in range(2):
                tiles = PANEL[(mine, row)][0]
                for place in range(BAND):
                    if place >= len(tiles):
                        value = jnp.zeros((BW, BW), F32)
                    elif tiles[place] < BAND:
                        value = upper_ref[tiles[place]]
                    elif mine == 1 and tiles[place] == BAND:
                        value = upper_ref[1].T
                    else:
                        value = lower_ref[tiles[place] - BAND].astype(F32).T
                    for half in range(2):
                        step = lax.rem(row * 2 + half - z + 4, 4)
                        out_ref[step, place] = value[half * 64 : (half + 1) * 64]


def pack(where, upper, lower):
    return pl.pallas_call(
        pack_kernel,
        grid_spec=pltpu.PrefetchScalarGridSpec(
            num_scalar_prefetch=1,
            grid=(1,),
            in_specs=[
                pl.BlockSpec((BAND, BW, BW), lambda i, where: (0, 0, 0)),
                pl.BlockSpec((BAND - 1, BW, BW), lambda i, where: (0, 0, 0)),
            ],
            out_specs=pl.BlockSpec((4, BAND, 64, BW), lambda i, where: (0, 0, 0, 0)),
        ),
        out_shape=jax.ShapeDtypeStruct((4, BAND, 64, BW), F32),
    )(where, upper, lower)


def split_kernel(where_ref, own_ref, first_ref, second_ref, third_ref, out_ref):
    total = (own_ref[0] + first_ref[...]) + (second_ref[...] + third_ref[...])
    core = where_ref[0]
    for mine in range(2):

        @pl.when(core == mine)
        def _():
            out_ref[0] = total[:, 32 * mine : 32 * mine + 32]
            out_ref[1] = total[:, 32 - 32 * mine : 64 - 32 * mine]


def split(where, packed, received):
    part = pl.BlockSpec((BAND, 64, BW), lambda i, where: (0, 0, 0))
    return pl.pallas_call(
        split_kernel,
        grid_spec=pltpu.PrefetchScalarGridSpec(
            num_scalar_prefetch=1,
            grid=(1,),
            in_specs=[
                pl.BlockSpec((1, BAND, 64, BW), lambda i, where: (0, 0, 0, 0)),
                part,
                part,
                part,
            ],
            out_specs=pl.BlockSpec((2, BAND, 32, BW), lambda i, where: (0, 0, 0, 0)),
        ),
        out_shape=jax.ShapeDtypeStruct((2, BAND, 32, BW), F32),
    )(where, packed, *received)


def final_kernel(where_ref, size_ref, screen_ref, own_ref, other_ref, out_ref, *, factor):
    core = where_ref[0]
    z = where_ref[1]
    owner = where_ref[2]
    for row in range(2):
        for mine in range(2):

            @pl.when(jnp.logical_and(core == mine, z // 2 == row))
            def _():
                block = owner * 2 + row
                start = (z % 2) * 64 + mine * 32
                rows = lax.broadcasted_iota(jnp.int32, (32, BW), 0) + start
                columns = lax.broadcasted_iota(jnp.int32, (32, BW), 1)
                row_mask = rows < size_ref[block]
                for half in range(2):
                    source = own_ref if half == mine else other_ref
                    for place, slot in enumerate(PANEL[(half, row)][1]):
                        offset = slot - (BAND - 1)
                        partner = jnp.clip(block + offset, 0, NB - 1)
                        first = jnp.minimum(block, partner)
                        inside = jnp.logical_and(block + offset >= 0, block + offset < NB)
                        kept = jnp.where(inside, screen_ref[first, abs(offset)], 0)
                        limit = jnp.where(kept > 0, size_ref[partner], 0)
                        mask = jnp.logical_and(row_mask, columns < limit)
                        value = source[place] if half != mine else source[0, place]
                        out_ref[:, slot * BW : (slot + 1) * BW] = jnp.where(mask, value * factor, 0.0)


def final(where, block_size, screen, pieces, other):
    factor = 1.0 / math.sqrt(AUX * OCC)
    return pl.pallas_call(
        functools.partial(final_kernel, factor=factor),
        grid_spec=pltpu.PrefetchScalarGridSpec(
            num_scalar_prefetch=3,
            grid=(1,),
            in_specs=[
                pl.BlockSpec((1, BAND, 32, BW), lambda i, *scalars: (0, 0, 0, 0)),
                pl.BlockSpec((BAND, 32, BW), lambda i, *scalars: (0, 0, 0)),
            ],
            out_specs=pl.BlockSpec((32, (2 * BAND - 1) * BW), lambda i, *scalars: (0, 0)),
        ),
        out_shape=jax.ShapeDtypeStruct((32, (2 * BAND - 1) * BW), F32),
    )(where, block_size, screen, pieces, other)


def local(three_index, block_size, screen):
    aux = lax.axis_index("aux")
    bas = lax.axis_index("bas")
    z, core = aux // 2, aux % 2
    y, x = bas // 4, bas % 4
    where = jnp.stack([core, z, bas]).astype(jnp.int32)
    flat = three_index.reshape(-1, three_index.shape[2])

    kept, received = {}, {}
    for group in GROUPS:
        pairs = jnp.array(group, jnp.int32)
        dy = jnp.where(core == 0, pairs[:, 0], pairs[:, 1])
        dx = jnp.where(core == 0, pairs[:, 1], pairs[:, 0])
        owners = ((y + dy) % 4) * 4 + (x + dx) % 4
        places = [group.index((second, first)) for first, second in group]
        mine, theirs = partial_tiles(flat, owners, places, where[:1])
        other = send(theirs, core_pairs())
        for index, key in enumerate(group):
            kept[key] = mine[index]
            received[key] = other[index]

    def chunk(step):
        own = jnp.stack([kept[(step, other)] for other in range(4)])
        other = jnp.stack([received[(step, other)] for other in range(4)])
        return own.astype(F32) + other.astype(F32)

    arrived = [send(chunk(step).astype(BF16), plane_pairs(step, True)) for step in (1, 3, 2)]
    total = chunk(0)
    for piece in arrived:
        total = total + piece.astype(F32)
    arrived = [send(total[step].astype(BF16), plane_pairs(step, False)) for step in (1, 3, 2)]
    upper = total[0]
    for piece in arrived:
        upper = upper + piece.astype(F32)

    lower = send(upper[1:].astype(BF16), mirror_pairs())
    packed = pack(where, upper, lower)
    arrived = [send(packed[step], z_pairs(step)) for step in (1, 3, 2)]
    pieces = split(where, packed, arrived)
    other = send(pieces[1], core_pairs())
    return final(where, block_size, screen, pieces, other)


def solution(mesh):
    in_specs = (P(("aux", "bas"), None, None), P(), P())
    out_specs = P(("bas", "aux"), None)
    return jax.shard_map(local, mesh=mesh, in_specs=in_specs, out_specs=out_specs, check_vma=False)
```

time: 1030 us -> 94.2 us (0.09); the launches traced: 1020 us -> 92.6 us
  starting transfers between devices: 279 us -> 24.7 us
  waiting for transfers between devices: 273 us -> 26.1 us
  local copies, waits for them, and re-layouts: 231 us -> 10.3 us
  blocking collectives: 147 us -> 0 us
  matrix products: 54.6 us -> 0 us
  Pallas kernels: 0 us -> 28.6 us
  between operations: 20.2 us -> 0.29 us
    ppermute x4 -> x15, starting transfers between devices: 279 us -> 24.7 us  [send(): return lax.ppermute(value, AXES, pairs)]
    ppermute x4 -> x15, waiting for transfers between devices: 230 us -> 26.1 us  [send(): return lax.ppermute(value, AXES, pairs)]
    all_to_all x1 -> x0, blocking collectives: 147 us -> none  [local(): lax.all_to_all(three_index, 'bas', split_axis=2, concat_axis=0, tiled=True)]
    unnamed x18 -> x33, local copies, waits for them, and re-layouts: 141 us -> 7.91 us
    dot_general x8 -> x0, matrix products: 54.6 us -> none  [compute(): lax.dot_general(left_block, right_block, (((0, 1), (0, 1)), ((), ())), pr...]
    all_to_all x1 -> x0, local copies, waits for them, and re-layouts: 45.2 us -> none  [local(): lax.all_to_all(three_index, 'bas', split_axis=2, concat_axis=0, tiled=True)]
    reduce_scatter x1 -> x0, waiting for transfers between devices: 43.4 us -> none  [local(): return lax.psum_scatter(row_panel, 'aux', scatter_dimension=0, tiled=True)]
    slice x4 -> x8, local copies, waits for them, and re-layouts: 32.3 us -> 0.3 us  [the longest x3 0.15 us: local(): kept[key] = mine[index]]
  transfers between devices with their start and end apart: 5 -> 15, of which waited for: 3 -> 10; matrix products, arithmetic and copies ran while one was open for 5% -> 2% of each run, Pallas kernels for 0% -> 13%
where the time goes in v1:
time: 94.2 us; the launch traced here: 92.6 us
  Pallas kernels  28.6 us (30%)
  waiting for transfers between devices  26.1 us (28%)
  starting transfers between devices  24.7 us (26%)
  local copies, waits for them, and re-layouts  10.3 us (11%)
  other arithmetic  2.66 us (3%)
    ppermute x15, waiting for transfers between devices, send(): return lax.ppermute(value, AXES, pairs)  26.1 us
    ppermute x15, starting transfers between devices, send(): return lax.ppermute(value, AXES, pairs)  24.7 us
    pallas_call x4, Pallas kernels, partial_tiles(): pl.pallas_call(tiles_kernel, grid_spec=pltpu.PrefetchScalarGridSpec(num_s...  20.8 us
    unnamed x33, local copies, waits for them, and re-layouts  7.91 us
    pallas_call x1, Pallas kernels, pack(): pl.pallas_call(pack_kernel, grid_spec=pltpu.PrefetchScalarGridSpec(num_sc...  2.65 us
    pallas_call x1, Pallas kernels, final(): pl.pallas_call(functools.partial(final_kernel, factor=factor), grid_spec=...  2.58 us
    pallas_call x1, Pallas kernels, split(): pl.pallas_call(split_kernel, grid_spec=pltpu.PrefetchScalarGridSpec(num_s...  2.54 us
  transfers between devices with their start and end apart: 15, of which 10 were waited for; matrix products, arithmetic and copies ran while one was open for 2% of the time, Pallas kernels for 13%

profile of v1, /device:TPU:1, one launch (start us, length us, event | category | flops | bytes accessed | tf_op | source)
XLA Modules:
  0.0 92.6 jit_solution(11048442025984179911)
XLA Ops:
  0.0 0.7 fusion.3.owner_ref
  0.7 4.6 %copy-done = bf16[48,32,4096]{2,1,0:T(8,128)(2,1)S(1)} copy-done((bf16[48,32,4096]{2,1,0:T(8,128)(2,1)S(1)}, bf16[48,32,4096]{2,1,0:T(8,128)(2,1)}, u32[]{:S(2)}) %copy-start) | copy-done | bytes 12582936
  5.3 0.7 copy-done.4
  5.9 9.1 %shard_map.110 = (bf16[7,5,128,128]{3,2,1,0:T(8,128)(2,1)S(1)}, bf16[7,5,128,128]{3,2,1,0:T(8,128)(2,1)S(1)}) custom-call(s32[7]{0:T(128)S(1)} %fusion.3.owner_ref, s32[7]{0:T(128)S(1)} %copy-done.4, s32[1]{0:T(128)} %bitcast.core_ref, bf16[1536,4096]{1,0:T(8,128)(2,1)S(1)} %bitcast.52, bf16[1536,4096]{1,0:T(8,128)(2,1)S(1)} %bitcast.53, ...), custom_call_target="tpu_custom_call" | custom-call | flops 4227858432 | bytes 18808832 | tf_op jit(solution)/shard_map/pallas_call | solution.py:117
  15.0 1.5 %collective-permute-start.1 = (bf16[7,5,128,128]{3,2,1,0:T(8,128)(2,1)S(1)}, bf16[7,5,128,128]{3,2,1,0:T(8,128)(2,1)S(1)}, u32[]{:S(2)}, u32[]{:S(2)}) collective-permute-start(bf16[7,5,128,128]{3,2,1,0:T(8,128)(2,1)S(1)} %get-tuple-element.18), channel_id=1, source_target_pairs={{0,16},{1,17},{2,18},{3,19},{4,20},{5,21},{6,22},{7,23},{8,24},{9,... | collective-permute-start | bytes 3440648 | tf_op jit(solution)/shard_map/ppermute | solution.py:76
  16.6 6.7 %shard_map.112 = (bf16[5,5,128,128]{3,2,1,0:T(8,128)(2,1)S(1)}, bf16[5,5,128,128]{3,2,1,0:T(8,128)(2,1)S(1)}) custom-call(s32[5]{0:T(128)S(1)} %fusion.5.owner_ref, s32[5]{0:T(128)S(1)} %copy-done.3, s32[1]{0:T(128)} %bitcast.core_ref, bf16[1536,4096]{1,0:T(8,128)(2,1)S(1)} %bitcast.55, bf16[1536,4096]{1,0:T(8,128)(2,1)S(1)} %bitcast.56, ...), custom_call_target="tpu_custom_call" | custom-call | flops 3019898880 | bytes 13434880 | tf_op jit(solution)/shard_map/pallas_call | solution.py:117
  23.3 0.1 collective-permute-start.3
  23.4 4.2 %shard_map.111 = (bf16[3,5,128,128]{3,2,1,0:T(8,128)(2,1)S(1)}, bf16[3,5,128,128]{3,2,1,0:T(8,128)(2,1)S(1)}) custom-call(s32[3]{0:T(128)S(1)} %fusion.4.owner_ref, s32[3]{0:T(128)S(1)} %copy-done.2, s32[1]{0:T(128)} %bitcast.core_ref, bf16[1536,4096]{1,0:T(8,128)(2,1)S(1)} %bitcast.58, bf16[1536,4096]{1,0:T(8,128)(2,1)S(1)} %bitcast.59, ...), custom_call_target="tpu_custom_call" | custom-call | flops 1811939328 | bytes 8060928 | tf_op jit(solution)/shard_map/pallas_call | solution.py:117
  27.7 0.6 collective-permute-start.2
  28.3 0.1 fusion.28
  28.4 1.3 %collective-permute-done.2 = bf16[3,5,128,128]{3,2,1,0:T(8,128)(2,1)S(1)} collective-permute-done((bf16[3,5,128,128]{3,2,1,0:T(8,128)(2,1)S(1)}, bf16[3,5,128,128]{3,2,1,0:T(8,128)(2,1)S(1)}, u32[]{:S(2)}, u32[]{:S(2)}) %collective-permute-start.2) | collective-permute-done | bytes 491552 | tf_op jit(solution)/shard_map/ppermute | solution.py:76
  29.9 0.2 add_convert_fusion.1
  30.1 2.3 %collective-permute-start.5 = (bf16[4,5,128,128]{3,2,1,0:T(8,128)(2,1)S(1)}, bf16[4,5,128,128]{3,2,1,0:T(8,128)(2,1)S(1)}, u32[]{:S(2)}, u32[]{:S(2)}) collective-permute-start(bf16[4,5,128,128]{3,2,1,0:T(8,128)(2,1)S(1)} %add_convert_fusion.1), channel_id=1, source_target_pairs={{0,12},{1,13},{2,14},{3,15},{4,0},{5,1},{6,2},{7,3},{8,4},{9,5},{1... | collective-permute-start | bytes 1966088 | tf_op jit(solution)/shard_map/ppermute | solution.py:76
  32.4 0.3 add_convert_fusion
  32.7 0.8 collective-permute-start.6
  33.5 0.2 add_convert_fusion.2
  33.7 0.7 collective-permute-start.4
  34.4 0.9 shard_map.109
  35.3 1.2 %collective-permute-start = (bf16[1,5,128,128]{3,2,1,0:T(8,128)(2,1)S(1)}, bf16[1,5,128,128]{3,2,1,0:T(8,128)(2,1)S(1)}, u32[]{:S(2)}, u32[]{:S(2)}) collective-permute-start(bf16[1,5,128,128]{3,2,1,0:T(8,128)(2,1)S(1)} %get-tuple-element.17), channel_id=1, source_target_pairs={{0,16},{1,17},{2,18},{3,19},{4,20},{5,21},{6,22},{7,23},{8,24},{9,... | collective-permute-start | bytes 491528 | tf_op jit(solution)/shard_map/ppermute | solution.py:76
  36.5 1.0 %collective-permute-done = bf16[1,5,128,128]{3,2,1,0:T(8,128)(2,1)S(1)} collective-permute-done((bf16[1,5,128,128]{3,2,1,0:T(8,128)(2,1)S(1)}, bf16[1,5,128,128]{3,2,1,0:T(8,128)(2,1)S(1)}, u32[]{:S(2)}, u32[]{:S(2)}) %collective-permute-start) | collective-permute-done | bytes 163872 | tf_op jit(solution)/shard_map/ppermute | solution.py:76
  37.6 9.4 %collective-permute-done.5 = bf16[4,5,128,128]{3,2,1,0:T(8,128)(2,1)S(1)} collective-permute-done((bf16[4,5,128,128]{3,2,1,0:T(8,128)(2,1)S(1)}, bf16[4,5,128,128]{3,2,1,0:T(8,128)(2,1)S(1)}, u32[]{:S(2)}, u32[]{:S(2)}) %collective-permute-start.5) | collective-permute-done | bytes 655392 | tf_op jit(solution)/shard_map/ppermute | solution.py:76
  47.0 4.1 %collective-permute-done.4 = bf16[4,5,128,128]{3,2,1,0:T(8,128)(2,1)S(1)} collective-permute-done((bf16[4,5,128,128]{3,2,1,0:T(8,128)(2,1)S(1)}, bf16[4,5,128,128]{3,2,1,0:T(8,128)(2,1)S(1)}, u32[]{:S(2)}, u32[]{:S(2)}) %collective-permute-start.4) | collective-permute-done | bytes 655392 | tf_op jit(solution)/shard_map/ppermute | solution.py:76
  51.1 0.5 fusion.27
  51.6 1.3 %collective-permute-start.7 = (bf16[5,128,128]{2,1,0:T(8,128)(2,1)S(1)}, bf16[5,128,128]{2,1,0:T(8,128)(2,1)S(1)}, u32[]{:S(2)}, u32[]{:S(2)}) collective-permute-start(bf16[5,128,128]{2,1,0:T(8,128)(2,1)S(1)} %get-tuple-element.38), channel_id=1, source_target_pairs={{0,1},{1,2},{2,3},{3,0},{4,5},{5,6},{6,7},{7,4},{8,9},{9,10},{10,1... | collective-permute-start | bytes 491528 | tf_op jit(solution)/shard_map/ppermute | solution.py:76
  52.9 1.6 %collective-permute-start.8 = (bf16[5,128,128]{2,1,0:T(8,128)(2,1)S(1)}, bf16[5,128,128]{2,1,0:T(8,128)(2,1)S(1)}, u32[]{:S(2)}, u32[]{:S(2)}) collective-permute-start(bf16[5,128,128]{2,1,0:T(8,128)(2,1)S(1)} %get-tuple-element.40), channel_id=1, source_target_pairs={{0,3},{1,0},{2,1},{3,2},{4,7},{5,4},{6,5},{7,6},{8,11},{9,8},{10,9... | collective-permute-start | bytes 491528 | tf_op jit(solution)/shard_map/ppermute | solution.py:76
  54.5 1.4 %collective-permute-start.9 = (bf16[5,128,128]{2,1,0:T(8,128)(2,1)S(1)}, bf16[5,128,128]{2,1,0:T(8,128)(2,1)S(1)}, u32[]{:S(2)}, u32[]{:S(2)}) collective-permute-start(bf16[5,128,128]{2,1,0:T(8,128)(2,1)S(1)} %get-tuple-element.39), channel_id=1, source_target_pairs={{0,2},{1,3},{2,0},{3,1},{4,6},{5,7},{6,4},{7,5},{8,10},{9,11},{10,... | collective-permute-start | bytes 491528 | tf_op jit(solution)/shard_map/ppermute | solution.py:76
  56.0 1.2 %collective-permute-done.7 = bf16[5,128,128]{2,1,0:T(8,128)(2,1)S(1)} collective-permute-done((bf16[5,128,128]{2,1,0:T(8,128)(2,1)S(1)}, bf16[5,128,128]{2,1,0:T(8,128)(2,1)S(1)}, u32[]{:S(2)}, u32[]{:S(2)}) %collective-permute-start.7) | collective-permute-done | bytes 163872 | tf_op jit(solution)/shard_map/ppermute | solution.py:76
  57.2 3.0 %collective-permute-done.9 = bf16[5,128,128]{2,1,0:T(8,128)(2,1)S(1)} collective-permute-done((bf16[5,128,128]{2,1,0:T(8,128)(2,1)S(1)}, bf16[5,128,128]{2,1,0:T(8,128)(2,1)S(1)}, u32[]{:S(2)}, u32[]{:S(2)}) %collective-permute-start.9) | collective-permute-done | bytes 163872 | tf_op jit(solution)/shard_map/ppermute | solution.py:76
  60.2 0.1 fusion.2.upper_ref
  60.3 2.7 %collective-permute-start.10 = (bf16[4,128,128]{2,1,0:T(8,128)(2,1)S(1)}, bf16[4,128,128]{2,1,0:T(8,128)(2,1)S(1)}, u32[]{:S(2)}, u32[]{:S(2)}) collective-permute-start(bf16[4,128,128]{2,1,0:T(8,128)(2,1)S(1)} %slice.217), channel_id=1, source_target_pairs={{0,1},{1,2},{2,3},{3,4},{4,5},{5,6},{6,7},{7,8},{8,9},{9,10},{10,1... | collective-permute-start | bytes 393224 | tf_op jit(solution)/shard_map/ppermute | solution.py:76
  63.1 0.7 pad_add_fusion.where_ref
  63.7 1.3 %collective-permute-done.10.lower_ref = bf16[4,128,128]{2,1,0:T(8,128)(2,1)S(1)} collective-permute-done((bf16[4,128,128]{2,1,0:T(8,128)(2,1)S(1)}, bf16[4,128,128]{2,1,0:T(8,128)(2,1)S(1)}, u32[]{:S(2)}, u32[]{:S(2)}) %collective-permute-start.10) | collective-permute-done | bytes 131104 | tf_op jit(solution)/shard_map/ppermute | solution.py:76
  65.0 0.7 copy-done.9
  65.6 2.6 %shard_map.113.own_ref = f32[4,5,64,128]{3,2,1,0:T(8,128)} custom-call(s32[3]{0:T(128)} %pad_add_fusion.where_ref, f32[5,128,128]{2,1,0:T(8,128)} %copy-done.5, bf16[4,128,128]{2,1,0:T(8,128)(2,1)} %copy-done.9), custom_call_target="tpu_custom_call" | custom-call | tf_op jit(solution)/shard_map/pallas_call | solution.py:162
  68.3 1.1 %slice_bitcast_fusion.1 = (f32[5,64,128]{2,1,0:T(8,128)S(1)}, f32[5,64,128]{2,1,0:T(8,128)S(1)}, f32[5,64,128]{2,1,0:T(8,128)S(1)}) fusion(f32[4,5,64,128]{3,2,1,0:T(8,128)} %shard_map.113.own_ref), kind=kLoop, calls=%fused_computation.9 | loop fusion | bytes 983040 | tf_op jit(solution)/shard_map/squeeze | solution.py:289
  69.4 1.7 %collective-permute-start.11 = (f32[5,64,128]{2,1,0:T(8,128)S(1)}, f32[5,64,128]{2,1,0:T(8,128)S(1)}, u32[]{:S(2)}, u32[]{:S(2)}) collective-permute-start(f32[5,64,128]{2,1,0:T(8,128)S(1)} %get-tuple-element.37), channel_id=1, source_target_pairs={{0,32},{1,33},{2,34},{3,35},{4,36},{5,37},{6,38},{7,39},{8,40},{9,... | collective-permute-start | bytes 491528 | tf_op jit(solution)/shard_map/ppermute | solution.py:76
  71.1 2.2 %collective-permute-start.12 = (f32[5,64,128]{2,1,0:T(8,128)S(1)}, f32[5,64,128]{2,1,0:T(8,128)S(1)}, u32[]{:S(2)}, u32[]{:S(2)}) collective-permute-start(f32[5,64,128]{2,1,0:T(8,128)S(1)} %get-tuple-element.36), channel_id=1, source_target_pairs={{0,96},{1,97},{2,98},{3,99},{4,100},{5,101},{6,102},{7,103},{8,104... | collective-permute-start | bytes 491528 | tf_op jit(solution)/shard_map/ppermute | solution.py:76
  73.3 1.2 %collective-permute-start.13 = (f32[5,64,128]{2,1,0:T(8,128)S(1)}, f32[5,64,128]{2,1,0:T(8,128)S(1)}, u32[]{:S(2)}, u32[]{:S(2)}) collective-permute-start(f32[5,64,128]{2,1,0:T(8,128)S(1)} %get-tuple-element.35), channel_id=1, source_target_pairs={{0,64},{1,65},{2,66},{3,67},{4,68},{5,69},{6,70},{7,71},{8,72},{9,... | collective-permute-start | bytes 491528 | tf_op jit(solution)/shard_map/ppermute | solution.py:76
  74.5 1.4 %collective-permute-done.11.first_ref = f32[5,64,128]{2,1,0:T(8,128)S(1)} collective-permute-done((f32[5,64,128]{2,1,0:T(8,128)S(1)}, f32[5,64,128]{2,1,0:T(8,128)S(1)}, u32[]{:S(2)}, u32[]{:S(2)}) %collective-permute-start.11) | collective-permute-done | bytes 163872 | tf_op jit(solution)/shard_map/ppermute | solution.py:76
  76.0 3.1 %collective-permute-done.13.third_ref = f32[5,64,128]{2,1,0:T(8,128)S(1)} collective-permute-done((f32[5,64,128]{2,1,0:T(8,128)S(1)}, f32[5,64,128]{2,1,0:T(8,128)S(1)}, u32[]{:S(2)}, u32[]{:S(2)}) %collective-permute-start.13) | collective-permute-done | bytes 163872 | tf_op jit(solution)/shard_map/ppermute | solution.py:76
  79.1 0.7 copy-done.8
  79.7 2.5 %shard_map.114.own_ref = f32[2,5,32,128]{3,2,1,0:T(8,128)} custom-call(s32[3]{0:T(128)} %pad_add_fusion.where_ref, f32[4,5,64,128]{3,2,1,0:T(8,128)} %shard_map.113.own_ref, f32[5,64,128]{2,1,0:T(8,128)} %copy-done.6, f32[5,64,128]{2,1,0:T(8,128)} %copy-done.7, f32[5,64,128]{2,1,0:T(8,128)} %copy-done.8), custom_call_target="tpu_custom_call" | custom-call | tf_op jit(solution)/shard_map/pallas_call | solution.py:190
  82.3 0.9 slice_bitcast_fusion.7
  83.2 5.3 %collective-permute-start.14 = (f32[5,32,128]{2,1,0:T(8,128)S(1)}, f32[5,32,128]{2,1,0:T(8,128)S(1)}, u32[]{:S(2)}, u32[]{:S(2)}) collective-permute-start(f32[5,32,128]{2,1,0:T(8,128)S(1)} %slice_bitcast_fusion.7), channel_id=1, source_target_pairs={{0,16},{1,17},{2,18},{3,19},{4,20},{5,21},{6,22},{7,23},{8,24},{9,... | collective-permute-start | bytes 245768 | tf_op jit(solution)/shard_map/ppermute | solution.py:76
  88.5 0.7 copy.12.screen_ref
  89.2 0.2 collective-permute-done.14.other_ref
  89.4 0.6 copy-done.10
  90.1 2.6 %shard_map.115 = f32[32,1152]{1,0:T(8,128)} custom-call(s32[3]{0:T(128)} %pad_add_fusion.where_ref, s32[32]{0:T(128)} %size_ref.1, s32[32,5]{1,0:T(8,128)} %copy.12.screen_ref, f32[2,5,32,128]{3,2,1,0:T(8,128)} %shard_map.114.own_ref, f32[5,32,128]{2,1,0:T(8,128)} %copy-done.10), custom_call_target="tpu_custom_call" | custom-call | tf_op jit(solution)/shard_map/pallas_call | solution.py:237
  (42 shorter events, 0.3 us)
Async XLA Ops:
  0.7 4.6 %copy-start = (bf16[48,32,4096]{2,1,0:T(8,128)(2,1)S(1)}, bf16[48,32,4096]{2,1,0:T(8,128)(2,1)}, u32[]{:S(2)}) copy-start(bf16[48,32,4096]{2,1,0:T(8,128)(2,1)} %param.11) | copy-start | bytes 37748740
  5.3 0.7 copy-start.4
  5.9 10.6 %copy-start.14 = (s32[5,1]{0,1:T(1,128)S(1)}, s32[5,1]{0,1:T(1,128)}, u32[]{:S(2)}) copy-start(s32[5,1]{0,1:T(1,128)} %constant.147) | copy-start | bytes 64
  5.9 10.6 %copy-start.15 = (s32[5,1]{0,1:T(1,128)S(1)}, s32[5,1]{0,1:T(1,128)}, u32[]{:S(2)}) copy-start(s32[5,1]{0,1:T(1,128)} %constant.148) | copy-start | bytes 64
  5.9 10.6 %copy-start.1 = (bf16[48,32,4096]{2,1,0:T(8,128)(2,1)S(1)}, bf16[48,32,4096]{2,1,0:T(8,128)(2,1)}, u32[]{:S(2)}) copy-start(bf16[48,32,4096]{2,1,0:T(8,128)(2,1)} %param.11) | copy-start | bytes 37748740
  5.9 10.6 %copy-start.3 = (s32[5]{0:T(128)S(1)}, s32[5]{0:T(128)}, u32[]{:S(2)}) copy-start(s32[5]{0:T(128)} %constant.136.clone.place_ref) | copy-start | bytes 64
  15.0 14.8 %collective-permute-start.1 = (bf16[7,5,128,128]{3,2,1,0:T(8,128)(2,1)S(1)}, bf16[7,5,128,128]{3,2,1,0:T(8,128)(2,1)S(1)}, u32[]{:S(2)}, u32[]{:S(2)}) collective-permute-start(bf16[7,5,128,128]{3,2,1,0:T(8,128)(2,1)S(1)} %get-tuple-element.18), channel_id=1, source_target_pairs={{0,16},{1,17},{2,18},{3,19},{4,20},{5,21},{6,22},{7,23},{8,24},{9,... | collective-permute-start | bytes 3440648 | tf_op jit(solution)/shard_map/ppermute | solution.py:76
  16.6 6.8 %copy-start.12 = (s32[3,1]{0,1:T(1,128)S(1)}, s32[3,1]{0,1:T(1,128)}, u32[]{:S(2)}) copy-start(s32[3,1]{0,1:T(1,128)} %constant.145) | copy-start | bytes 40
  16.6 6.8 %copy-start.13 = (s32[3,1]{0,1:T(1,128)S(1)}, s32[3,1]{0,1:T(1,128)}, u32[]{:S(2)}) copy-start(s32[3,1]{0,1:T(1,128)} %constant.146) | copy-start | bytes 40
  16.6 6.8 %copy-start.2 = (s32[3]{0:T(128)S(1)}, s32[3]{0:T(128)}, u32[]{:S(2)}) copy-start(s32[3]{0:T(128)} %constant.138.clone.place_ref) | copy-start | bytes 40
  23.3 6.5 %collective-permute-start.3 = (bf16[5,5,128,128]{3,2,1,0:T(8,128)(2,1)S(1)}, bf16[5,5,128,128]{3,2,1,0:T(8,128)(2,1)S(1)}, u32[]{:S(2)}, u32[]{:S(2)}) collective-permute-start(bf16[5,5,128,128]{3,2,1,0:T(8,128)(2,1)S(1)} %get-tuple-element.20), channel_id=1, source_target_pairs={{0,16},{1,17},{2,18},{3,19},{4,20},{5,21},{6,22},{7,23},{8,24},{9,... | collective-permute-start | bytes 2457608 | tf_op jit(solution)/shard_map/ppermute | solution.py:76
  27.7 2.0 %collective-permute-start.2 = (bf16[3,5,128,128]{3,2,1,0:T(8,128)(2,1)S(1)}, bf16[3,5,128,128]{3,2,1,0:T(8,128)(2,1)S(1)}, u32[]{:S(2)}, u32[]{:S(2)}) collective-permute-start(bf16[3,5,128,128]{3,2,1,0:T(8,128)(2,1)S(1)} %get-tuple-element.19), channel_id=1, source_target_pairs={{0,16},{1,17},{2,18},{3,19},{4,20},{5,21},{6,22},{7,23},{8,24},{9,... | collective-permute-start | bytes 1474568 | tf_op jit(solution)/shard_map/ppermute | solution.py:76
  30.1 16.9 %collective-permute-start.5 = (bf16[4,5,128,128]{3,2,1,0:T(8,128)(2,1)S(1)}, bf16[4,5,128,128]{3,2,1,0:T(8,128)(2,1)S(1)}, u32[]{:S(2)}, u32[]{:S(2)}) collective-permute-start(bf16[4,5,128,128]{3,2,1,0:T(8,128)(2,1)S(1)} %add_convert_fusion.1), channel_id=1, source_target_pairs={{0,12},{1,13},{2,14},{3,15},{4,0},{5,1},{6,2},{7,3},{8,4},{9,5},{1... | collective-permute-start | bytes 1966088 | tf_op jit(solution)/shard_map/ppermute | solution.py:76
  32.7 14.3 %collective-permute-start.6 = (bf16[4,5,128,128]{3,2,1,0:T(8,128)(2,1)S(1)}, bf16[4,5,128,128]{3,2,1,0:T(8,128)(2,1)S(1)}, u32[]{:S(2)}, u32[]{:S(2)}) collective-permute-start(bf16[4,5,128,128]{3,2,1,0:T(8,128)(2,1)S(1)} %add_convert_fusion), channel_id=1, source_target_pairs={{0,8},{1,9},{2,10},{3,11},{4,12},{5,13},{6,14},{7,15},{8,0},{9,1},... | collective-permute-start | bytes 1966088 | tf_op jit(solution)/shard_map/ppermute | solution.py:76
  33.7 17.3 %collective-permute-start.4 = (bf16[4,5,128,128]{3,2,1,0:T(8,128)(2,1)S(1)}, bf16[4,5,128,128]{3,2,1,0:T(8,128)(2,1)S(1)}, u32[]{:S(2)}, u32[]{:S(2)}) collective-permute-start(bf16[4,5,128,128]{3,2,1,0:T(8,128)(2,1)S(1)} %add_convert_fusion.2), channel_id=1, source_target_pairs={{0,4},{1,5},{2,6},{3,7},{4,8},{5,9},{6,10},{7,11},{8,12},{9,13},{1... | collective-permute-start | bytes 1966088 | tf_op jit(solution)/shard_map/ppermute | solution.py:76
  35.3 2.3 %collective-permute-start = (bf16[1,5,128,128]{3,2,1,0:T(8,128)(2,1)S(1)}, bf16[1,5,128,128]{3,2,1,0:T(8,128)(2,1)S(1)}, u32[]{:S(2)}, u32[]{:S(2)}) collective-permute-start(bf16[1,5,128,128]{3,2,1,0:T(8,128)(2,1)S(1)} %get-tuple-element.17), channel_id=1, source_target_pairs={{0,16},{1,17},{2,18},{3,19},{4,20},{5,21},{6,22},{7,23},{8,24},{9,... | collective-permute-start | bytes 491528 | tf_op jit(solution)/shard_map/ppermute | solution.py:76
  51.6 5.5 %collective-permute-start.7 = (bf16[5,128,128]{2,1,0:T(8,128)(2,1)S(1)}, bf16[5,128,128]{2,1,0:T(8,128)(2,1)S(1)}, u32[]{:S(2)}, u32[]{:S(2)}) collective-permute-start(bf16[5,128,128]{2,1,0:T(8,128)(2,1)S(1)} %get-tuple-element.38), channel_id=1, source_target_pairs={{0,1},{1,2},{2,3},{3,0},{4,5},{5,6},{6,7},{7,4},{8,9},{9,10},{10,1... | collective-permute-start | bytes 491528 | tf_op jit(solution)/shard_map/ppermute | solution.py:76
  52.9 4.3 %collective-permute-start.8 = (bf16[5,128,128]{2,1,0:T(8,128)(2,1)S(1)}, bf16[5,128,128]{2,1,0:T(8,128)(2,1)S(1)}, u32[]{:S(2)}, u32[]{:S(2)}) collective-permute-start(bf16[5,128,128]{2,1,0:T(8,128)(2,1)S(1)} %get-tuple-element.40), channel_id=1, source_target_pairs={{0,3},{1,0},{2,1},{3,2},{4,7},{5,4},{6,5},{7,6},{8,11},{9,8},{10,9... | collective-permute-start | bytes 491528 | tf_op jit(solution)/shard_map/ppermute | solution.py:76
  54.5 5.7 %collective-permute-start.9 = (bf16[5,128,128]{2,1,0:T(8,128)(2,1)S(1)}, bf16[5,128,128]{2,1,0:T(8,128)(2,1)S(1)}, u32[]{:S(2)}, u32[]{:S(2)}) collective-permute-start(bf16[5,128,128]{2,1,0:T(8,128)(2,1)S(1)} %get-tuple-element.39), channel_id=1, source_target_pairs={{0,2},{1,3},{2,0},{3,1},{4,6},{5,7},{6,4},{7,5},{8,10},{9,11},{10,... | collective-permute-start | bytes 491528 | tf_op jit(solution)/shard_map/ppermute | solution.py:76
  60.3 4.7 %copy-start.5 = (f32[5,128,128]{2,1,0:T(8,128)}, f32[5,128,128]{2,1,0:T(8,128)S(1)}, u32[]{:S(2)}) copy-start(f32[5,128,128]{2,1,0:T(8,128)S(1)} %fusion.2.upper_ref) | copy-start | bytes 983044
  60.3 4.7 %collective-permute-start.10 = (bf16[4,128,128]{2,1,0:T(8,128)(2,1)S(1)}, bf16[4,128,128]{2,1,0:T(8,128)(2,1)S(1)}, u32[]{:S(2)}, u32[]{:S(2)}) collective-permute-start(bf16[4,128,128]{2,1,0:T(8,128)(2,1)S(1)} %slice.217), channel_id=1, source_target_pairs={{0,1},{1,2},{2,3},{3,4},{4,5},{5,6},{6,7},{7,8},{8,9},{9,10},{10,1... | collective-permute-start | bytes 393224 | tf_op jit(solution)/shard_map/ppermute | solution.py:76
  65.0 0.7 copy-start.9
  68.3 20.2 %copy-start.11 = (s32[32,5]{0,1:T(8,128)S(1)}, s32[32,5]{0,1:T(8,128)}, u32[]{:S(2)}) copy-start(s32[32,5]{0,1:T(8,128)} %param.13) | copy-start | bytes 1924
  69.4 6.5 %collective-permute-start.11 = (f32[5,64,128]{2,1,0:T(8,128)S(1)}, f32[5,64,128]{2,1,0:T(8,128)S(1)}, u32[]{:S(2)}, u32[]{:S(2)}) collective-permute-start(f32[5,64,128]{2,1,0:T(8,128)S(1)} %get-tuple-element.37), channel_id=1, source_target_pairs={{0,32},{1,33},{2,34},{3,35},{4,36},{5,37},{6,38},{7,39},{8,40},{9,... | collective-permute-start | bytes 491528 | tf_op jit(solution)/shard_map/ppermute | solution.py:76
  71.1 4.8 %collective-permute-start.12 = (f32[5,64,128]{2,1,0:T(8,128)S(1)}, f32[5,64,128]{2,1,0:T(8,128)S(1)}, u32[]{:S(2)}, u32[]{:S(2)}) collective-permute-start(f32[5,64,128]{2,1,0:T(8,128)S(1)} %get-tuple-element.36), channel_id=1, source_target_pairs={{0,96},{1,97},{2,98},{3,99},{4,100},{5,101},{6,102},{7,103},{8,104... | collective-permute-start | bytes 491528 | tf_op jit(solution)/shard_map/ppermute | solution.py:76
  73.3 5.7 %collective-permute-start.13 = (f32[5,64,128]{2,1,0:T(8,128)S(1)}, f32[5,64,128]{2,1,0:T(8,128)S(1)}, u32[]{:S(2)}, u32[]{:S(2)}) collective-permute-start(f32[5,64,128]{2,1,0:T(8,128)S(1)} %get-tuple-element.35), channel_id=1, source_target_pairs={{0,64},{1,65},{2,66},{3,67},{4,68},{5,69},{6,70},{7,71},{8,72},{9,... | collective-permute-start | bytes 491528 | tf_op jit(solution)/shard_map/ppermute | solution.py:76
  75.9 3.1 %copy-start.6 = (f32[5,64,128]{2,1,0:T(8,128)}, f32[5,64,128]{2,1,0:T(8,128)S(1)}, u32[]{:S(2)}) copy-start(f32[5,64,128]{2,1,0:T(8,128)S(1)} %collective-permute-done.11.first_ref) | copy-start | bytes 491524
  75.9 3.1 %copy-start.7 = (f32[5,64,128]{2,1,0:T(8,128)}, f32[5,64,128]{2,1,0:T(8,128)S(1)}, u32[]{:S(2)}) copy-start(f32[5,64,128]{2,1,0:T(8,128)S(1)} %collective-permute-done.12.second_ref) | copy-start | bytes 491524
  79.1 0.7 copy-start.8
  83.2 6.3 %collective-permute-start.14 = (f32[5,32,128]{2,1,0:T(8,128)S(1)}, f32[5,32,128]{2,1,0:T(8,128)S(1)}, u32[]{:S(2)}, u32[]{:S(2)}) collective-permute-start(f32[5,32,128]{2,1,0:T(8,128)S(1)} %slice_bitcast_fusion.7), channel_id=1, source_target_pairs={{0,16},{1,17},{2,18},{3,19},{4,20},{5,21},{6,22},{7,23},{8,24},{9,... | collective-permute-start | bytes 245768 | tf_op jit(solution)/shard_map/ppermute | solution.py:76
  89.4 0.6 copy-start.10

commit v2 on v0

v2 whole, which is shorter than its diff:
```python
import functools
import math

import jax
import jax.numpy as jnp
from jax import lax
from jax.experimental import pallas as pl
from jax.experimental.pallas import tpu as pltpu
from jax.sharding import PartitionSpec as P

AUX = 6144
OCC = 32
BW = 128
BAND = 5
NB = 32
OWNERS = 16
PAIR = 2 * BW
AXES = ("aux", "bas")
F32 = jnp.float32
BF16 = jnp.bfloat16

TILES = (
    ((0, 0), (0, 2), (0, 3), (1, 1), (1, 2)),
    ((1, 0), (0, 1), (0, 4), (1, 3), (1, 4)),
)
PANEL = {
    (0, 0): ((0, 1, 2, 5, 7), (4, 6, 7, 2, 3)),
    (1, 0): ((1, 2, 6, 7), (5, 8, 0, 1)),
    (0, 1): ((3, 4, 6, 8), (5, 6, 1, 2)),
    (1, 1): ((0, 3, 4, 5, 8), (4, 7, 8, 3, 0)),
}
STEPS = (2, 1, 3, 0)


def device(z, c, y, x):
    return (z * 2 + c) * 16 + y * 4 + x


EVERY = [(z, c, y, x) for z in range(4) for c in range(2) for y in range(4) for x in range(4)]


def core_pairs():
    return [(device(z, c, y, x), device(z, 1 - c, y, x)) for z, c, y, x in EVERY]


def plane_pairs(step, first):
    pairs = []
    for z, c, y, x in EVERY:
        if (c == 0) == first:
            target = device(z, c, (y + step) % 4, x)
        else:
            target = device(z, c, y, (x + step) % 4)
        pairs.append((device(z, c, y, x), target))
    return pairs


def mirror_pairs():
    pairs = []
    for z, c, y, x in EVERY:
        owner = (y * 4 + x + 1 + c) % OWNERS
        pairs.append((device(z, c, y, x), device(z, c, owner // 4, owner % 4)))
    return pairs


def z_pairs(step):
    return [(device(z, c, y, x), device((z + step) % 4, c, y, x)) for z, c, y, x in EVERY]


def send(value, pairs):
    return lax.ppermute(value, AXES, pairs)


def place_here():
    aux = lax.axis_index("aux")
    bas = lax.axis_index("bas")
    return aux // 2, aux % 2, bas


def panel(ref, block, depth):
    return ref[depth, pl.ds(pl.multiple_of(block * PAIR, PAIR), PAIR)]


def gram(left, right):
    return lax.dot_general(left, right, (((0,), (0,)), ((), ())), preferred_element_type=F32)


def set_products(flat_ref, step, bas, depth):
    y, x = bas // 4, bas % 4
    for other in range(4):
        owner = ((y + step) % 4) * 4 + (x + other) % 4
        left = panel(flat_ref, owner, depth)
        right = panel(flat_ref, jnp.minimum(owner + 1, OWNERS - 1), depth)
        zero = gram(left[:, :BW], left[:, :BW]), gram(left, right)
        owner = ((y + other) % 4) * 4 + (x + step) % 4
        left = panel(flat_ref, owner, depth)
        right = panel(flat_ref, jnp.minimum(owner + 2, OWNERS - 1), depth)
        yield zero + (gram(left, left), gram(left, right))


def put_tiles(parts, position, core, mine_ref, theirs_ref):
    low, high = slice(0, BW), slice(BW, PAIR)
    diagonal, near, block, far = parts
    zero = diagonal, near[low, low], near[low, high], near[high, low], near[high, high]
    one = block[high, high], block[low, high], far[low, low], far[high, low], far[high, high]
    for place in range(BAND):
        first, second = zero[place].astype(BF16), one[place].astype(BF16)
        mine_ref[position, place] = jnp.where(core == 0, first, second)
        theirs_ref[0, place] = jnp.where(core == 0, second, first)


def depth_parts(depth):
    sizes = (depth // 3, depth // 3, depth // 6, depth // 6)
    return [pl.ds(sum(sizes[:index]), size) for index, size in enumerate(sizes)]


def first_kernel(flat_hbm, mine_ref, theirs_ref, flat_ref, small_ref, sums_ref, sems, *, step):
    z, core, bas = place_here()
    depths = depth_parts(flat_ref.shape[0])
    copies = [
        pltpu.make_async_copy(flat_hbm.at[depth], flat_ref.at[depth], sems.at[index])
        for index, depth in enumerate(depths)
    ]
    for copy in copies:
        copy.start()
    for index, (copy, depth) in enumerate(zip(copies, depths)):
        copy.wait()
        for position, parts in enumerate(set_products(flat_ref, step, bas, depth)):
            if index > 0:
                before = (small_ref[position], *(sums_ref[position, place] for place in range(3)))
                parts = [total + part for total, part in zip(before, parts)]
            if index < len(depths) - 1:
                small_ref[position] = parts[0]
                for place, part in enumerate(parts[1:]):
                    sums_ref[position, place] = part
            else:
                put_tiles(parts, position, core, mine_ref, theirs_ref.at[pl.ds(position, 1)])


def later_kernel(flat_ref, after_ref, mine_ref, *theirs_refs, step):
    z, core, bas = place_here()
    for position, parts in enumerate(set_products(flat_ref, step, bas, pl.ds(0, flat_ref.shape[0]))):
        size = 4 // len(theirs_refs)
        theirs_ref = theirs_refs[position // size].at[pl.ds(position % size, 1)]
        put_tiles(parts, position, core, mine_ref, theirs_ref)


VMEM = pl.BlockSpec(memory_space=pltpu.VMEM)
ANYWHERE = pl.BlockSpec(memory_space=pl.ANY)
SMALL = pltpu.CompilerParams(vmem_limit_bytes=4 << 20)
SCALARS = pl.BlockSpec(memory_space=pltpu.SMEM)


SET = jax.ShapeDtypeStruct((4, BAND, BW, BW), BF16)


def cost(depth, moved=0):
    return pl.CostEstimate(
        flops=4 * 13 * PAIR * PAIR * depth // 2, bytes_accessed=moved, transcendentals=0
    )


def first_tiles(flat, step):
    depth = flat.shape[0]
    return pl.pallas_call(
        functools.partial(first_kernel, step=step),
        in_specs=[ANYWHERE],
        out_specs=[VMEM, VMEM, VMEM],
        out_shape=[SET, SET, pltpu.VMEM(flat.shape, BF16)],
        scratch_shapes=[
            pltpu.VMEM((4, BW, BW), F32),
            pltpu.VMEM((4, 3, PAIR, PAIR), F32),
            pltpu.SemaphoreType.DMA((4,)),
        ],
        compiler_params=pltpu.CompilerParams(vmem_limit_bytes=20 << 20),
        cost_estimate=cost(depth, flat.size * 2),
    )(pltpu.with_memory_space_constraint(flat, pltpu.HBM))


def later_tiles(flat, after, step, pieces=1):
    return pl.pallas_call(
        functools.partial(later_kernel, step=step),
        in_specs=[VMEM, ANYWHERE],
        out_specs=[VMEM] * (1 + pieces),
        out_shape=[SET] + [jax.ShapeDtypeStruct((4 // pieces, BAND, BW, BW), BF16)] * pieces,
        compiler_params=pltpu.CompilerParams(vmem_limit_bytes=16 << 20),
        cost_estimate=cost(flat.shape[0]),
    )(flat, after)


def total_kernel(*refs):
    mine_ref, other_ref, *arrived, own_ref, first_ref, second_ref, third_ref = refs
    for position, out_ref in enumerate((own_ref, first_ref, second_ref, third_ref)):
        total = mine_ref[position].astype(F32) + other_ref[position].astype(F32)
        for ref in arrived:
            total = total + ref[position].astype(F32)
        out_ref[...] = total.astype(out_ref.dtype)


def first_total(mine, other, arrived):
    sent = jax.ShapeDtypeStruct((BAND, BW, BW), BF16)
    return pl.pallas_call(
        total_kernel,
        in_specs=[VMEM] * 5,
        out_specs=[VMEM] * 4,
        out_shape=[jax.ShapeDtypeStruct((BAND, BW, BW), F32), sent, sent, sent],
        compiler_params=SMALL,
    )(mine, other, *arrived)


def pair_sum(mine, other):
    return (mine.astype(F32) + other.astype(F32)).astype(BF16)


def pack_kernel(upper_ref, lower_ref, own_ref, *sent_refs):
    z, core, _ = place_here()
    for mine in range(2):
        for row in range(2):
            tiles = PANEL[(mine, row)][0]
            for half in range(2):
                target = row * 2 + half
                rows = pl.ds(half * 64, 64)

                def value(index):
                    if index < BAND:
                        return upper_ref[index, rows]
                    if mine == 1 and index == BAND:
                        return upper_ref[1, :, rows].T
                    return lower_ref[index - BAND, :, rows].astype(F32).T

                @pl.when(jnp.logical_and(core == mine, z == target))
                def _():
                    for place, index in enumerate(tiles):
                        own_ref[place] = value(index)
                    if len(tiles) < BAND:
                        own_ref[BAND - 1] = jnp.zeros((64, BW), F32)

                for step in range(1, 4):

                    @pl.when(jnp.logical_and(core == mine, (z + step) % 4 == target))
                    def _():
                        out_ref = sent_refs[step - 1]
                        rest = jnp.zeros((64, BW), BF16)
                        for place, index in enumerate(tiles):
                            whole = value(index)
                            high = whole.astype(BF16)
                            out_ref[place] = high
                            if index == 0:
                                rest = (whole - high.astype(F32)).astype(BF16)
                        if len(tiles) < BAND:
                            out_ref[BAND - 1] = jnp.zeros((64, BW), BF16)
                        out_ref[BAND] = rest


def pack(upper, lower):
    own = jax.ShapeDtypeStruct((BAND, 64, BW), F32)
    sent = jax.ShapeDtypeStruct((BAND + 1, 64, BW), BF16)
    return pl.pallas_call(
        pack_kernel,
        in_specs=[VMEM, VMEM],
        out_specs=[VMEM] * 4,
        out_shape=[own] + [sent] * 3,
        compiler_params=SMALL,
    )(upper, lower)


def split_kernel(own_ref, first_ref, second_ref, third_ref, kept_ref, sent_ref):
    z, core, _ = place_here()
    for ref, part in ((kept_ref, core), (sent_ref, 1 - core)):
        rows = pl.ds(pl.multiple_of(part * 32, 32), 32)
        for place in range(BAND):
            total = own_ref[place, rows]
            for source in (first_ref, second_ref, third_ref):
                total = total + source[place, rows].astype(F32)
                if place == 0:
                    total = total + source[BAND, rows].astype(F32)
            ref[place] = total


def split(own, arrived):
    shape = jax.ShapeDtypeStruct((BAND, 32, BW), F32)
    return pl.pallas_call(
        split_kernel,
        in_specs=[VMEM] * 4,
        out_specs=[VMEM] * 2,
        out_shape=[shape] * 2,
        compiler_params=SMALL,
    )(own, *arrived)


def final_kernel(size_ref, screen_ref, own_ref, other_ref, out_ref, *, factor):
    z, core, owner = place_here()
    for row in range(2):
        for mine in range(2):

            @pl.when(jnp.logical_and(core == mine, z // 2 == row))
            def _():
                block = owner * 2 + row
                start = (z % 2) * 64 + mine * 32
                rows = lax.broadcasted_iota(jnp.int32, (32, BW), 0) + start
                columns = lax.broadcasted_iota(jnp.int32, (32, BW), 1)
                row_mask = rows < size_ref[block]
                for half in range(2):
                    source = own_ref if half == mine else other_ref
                    for place, slot in enumerate(PANEL[(half, row)][1]):
                        offset = slot - (BAND - 1)
                        partner = jnp.clip(block + offset, 0, NB - 1)
                        inside = jnp.logical_and(block + offset >= 0, block + offset < NB)
                        kept = jnp.where(inside, screen_ref[abs(offset), jnp.minimum(block, partner)], 0)
                        limit = jnp.where(kept > 0, size_ref[partner], 0)
                        mask = jnp.logical_and(row_mask, columns < limit)
                        out_ref[:, slot * BW : (slot + 1) * BW] = jnp.where(mask, source[place] * factor, 0.0)


def final(block_size, screen, own, other):
    factor = 1.0 / math.sqrt(AUX * OCC)
    return pl.pallas_call(
        functools.partial(final_kernel, factor=factor),
        in_specs=[SCALARS, SCALARS, VMEM, VMEM],
        out_specs=VMEM,
        out_shape=jax.ShapeDtypeStruct((32, (2 * BAND - 1) * BW), F32),
        compiler_params=SMALL,
    )(block_size, screen.T, own, other)


def local(three_index, block_size, screen):
    flat = three_index.reshape(-1, three_index.shape[2])
    def exchanged(pieces):
        return jnp.concatenate([send(piece, core_pairs()) for piece in pieces])

    def passed(step, mine, other):
        outgoing = pair_sum(mine, other)
        return outgoing, send(outgoing, plane_pairs(step, True))

    mine, theirs, held = first_tiles(flat, STEPS[0])
    other = send(theirs, core_pairs())
    next_mine, *next_theirs = later_tiles(held, block_size, STEPS[1], 1)
    next_other = exchanged(next_theirs)
    sent1, arrived1 = passed(STEPS[0], mine, other)
    sent2, arrived2 = passed(STEPS[1], next_mine, next_other)
    mine, *theirs = later_tiles(held, sent2, STEPS[2], 2)
    other = exchanged(theirs)
    sent3, arrived3 = passed(STEPS[2], mine, other)
    mine, *theirs = later_tiles(held, arrived1, STEPS[3], 1)
    upper, *outgoing = first_total(mine, exchanged(theirs), [arrived1, arrived2, arrived3])
    arrived = [send(outgoing[step - 1], plane_pairs(step, False)) for step in (2, 1, 3)]
    for piece in arrived:
        upper = upper + piece.astype(F32)

    lower = send(upper[1:].astype(BF16), mirror_pairs())
    own, *outgoing = pack(upper, lower)
    arrived = [send(outgoing[step - 1], z_pairs(step)) for step in (2, 1, 3)]
    own, theirs = split(own, arrived)
    other = send(theirs, core_pairs())
    return final(block_size, screen, own, other)


def solution(mesh):
    in_specs = (P(("aux", "bas"), None, None), P(), P())
    out_specs = P(("bas", "aux"), None)
    return jax.shard_map(local, mesh=mesh, in_specs=in_specs, out_specs=out_specs, check_vma=False)
```

time: 1030 us -> 64.9 us (0.06); the launches traced: 1020 us -> 64.8 us
  waiting for transfers between devices: 273 us -> 18.6 us
  starting transfers between devices: 279 us -> 27.1 us
  local copies, waits for them, and re-layouts: 231 us -> 0.03 us
  blocking collectives: 147 us -> 0 us
  matrix products: 54.6 us -> 0 us
  between operations: 20.2 us -> 0.11 us
  Pallas kernels: 0 us -> 18.3 us
  other arithmetic: 11 us -> 0.65 us
    ppermute x4 -> x16, starting transfers between devices: 279 us -> 27.1 us  [send(): return lax.ppermute(value, AXES, pairs)]
    ppermute x4 -> x16, waiting for transfers between devices: 230 us -> 18.6 us  [send(): return lax.ppermute(value, AXES, pairs)]
    all_to_all x1 -> x0, blocking collectives: 147 us -> none  [local(): lax.all_to_all(three_index, 'bas', split_axis=2, concat_axis=0, tiled=True)]
    unnamed x18 -> x4, local copies, waits for them, and re-layouts: 141 us -> 0.01 us
    dot_general x8 -> x0, matrix products: 54.6 us -> none  [compute(): lax.dot_general(left_block, right_block, (((0, 1), (0, 1)), ((), ())), pr...]
    all_to_all x1 -> x0, local copies, waits for them, and re-layouts: 45.2 us -> none  [local(): lax.all_to_all(three_index, 'bas', split_axis=2, concat_axis=0, tiled=True)]
    reduce_scatter x1 -> x0, waiting for transfers between devices: 43.4 us -> none  [local(): return lax.psum_scatter(row_panel, 'aux', scatter_dimension=0, tiled=True)]
    slice x4 -> x1, local copies, waits for them, and re-layouts: 32.3 us -> 0.02 us  [local(): lower = send(upper[1:].astype(BF16), mirror_pairs())]
  transfers between devices with their start and end apart: 5 -> 16, of which waited for: 3 -> 9; matrix products, arithmetic and copies ran while one was open for 5% -> 1% of each run, Pallas kernels for 0% -> 15%
where the time goes in v2:
time: 64.9 us; the launch traced here: 64.8 us
  starting transfers between devices  27.1 us (42%)
  waiting for transfers between devices  18.6 us (29%)
  Pallas kernels  18.3 us (28%)
  other arithmetic  0.65 us (1%)
    ppermute x16, starting transfers between devices, send(): return lax.ppermute(value, AXES, pairs)  27.1 us
    ppermute x16, waiting for transfers between devices, send(): return lax.ppermute(value, AXES, pairs)  18.6 us
    pallas_call x3, Pallas kernels, later_tiles(): pl.pallas_call(functools.partial(later_kernel, step=step), in_specs=[VMEM...  9.74 us
    pallas_call x1, Pallas kernels, first_tiles(): pl.pallas_call(functools.partial(first_kernel, step=step), in_specs=[ANYW...  6.24 us
    pallas_call x1, Pallas kernels, final(): pl.pallas_call(functools.partial(final_kernel, factor=factor), in_specs=[...  1.36 us
  transfers between devices with their start and end apart: 16, of which 9 were waited for; matrix products, arithmetic and copies ran while one was open for 1% of the time, Pallas kernels for 15%

profile of v2, /device:TPU:1, one launch (start us, length us, event | category | flops | bytes accessed | tf_op | source)
XLA Modules:
  0.0 64.8 jit_solution(3149305658830740682)
XLA Ops:
  0.0 0.0 copy-start.1
  0.0 6.2 %shard_map.37 = (bf16[4,5,128,128]{3,2,1,0:T(8,128)(2,1)S(1)}, bf16[4,5,128,128]{3,2,1,0:T(8,128)(2,1)S(1)}, bf16[1536,4096]{1,0:T(8,128)(2,1)S(1)}) custom-call(bf16[1536,4096]{1,0:T(8,128)(2,1)} %bitcast.3), custom_call_target="tpu_custom_call" | custom-call | flops 2617245696 | bytes 12582912 | tf_op jit(solution)/shard_map/pallas_call | solution.py:164
  6.2 1.5 %collective-permute-start = (bf16[4,5,128,128]{3,2,1,0:T(8,128)(2,1)S(1)}, bf16[4,5,128,128]{3,2,1,0:T(8,128)(2,1)S(1)}, u32[]{:S(2)}, u32[]{:S(2)}) collective-permute-start(bf16[4,5,128,128]{3,2,1,0:T(8,128)(2,1)S(1)} %get-tuple-element.27), channel_id=1, source_target_pairs={{0,16},{1,17},{2,18},{3,19},{4,20},{5,21},{6,22},{7,23},{8,24},{9,... | collective-permute-start | bytes 1966088 | tf_op jit(solution)/shard_map/ppermute | solution.py:70
  7.7 0.0 copy-done.1
  7.8 3.3 %shard_map.39 = (bf16[4,5,128,128]{3,2,1,0:T(8,128)(2,1)S(1)}, bf16[4,5,128,128]{3,2,1,0:T(8,128)(2,1)S(1)}) custom-call(bf16[1536,4096]{1,0:T(8,128)(2,1)S(1)} %get-tuple-element.25.flat_ref, s32[32]{0:T(128)S(1)} %copy-done.1), custom_call_target="tpu_custom_call" | custom-call | flops 2617245696 | tf_op jit(solution)/shard_map/pallas_call | solution.py:180
  11.0 0.1 collective-permute-start.3
  11.1 0.0 collective-permute-done
  11.1 0.2 add_convert_fusion.2
  11.4 2.9 %collective-permute-start.1 = (bf16[4,5,128,128]{3,2,1,0:T(8,128)(2,1)S(1)}, bf16[4,5,128,128]{3,2,1,0:T(8,128)(2,1)S(1)}, u32[]{:S(2)}, u32[]{:S(2)}) collective-permute-start(bf16[4,5,128,128]{3,2,1,0:T(8,128)(2,1)S(1)} %add_convert_fusion.2), channel_id=1, source_target_pairs={{0,8},{1,9},{2,10},{3,11},{4,12},{5,13},{6,14},{7,15},{8,0},{9,1},... | collective-permute-start | bytes 1966088 | tf_op jit(solution)/shard_map/ppermute | solution.py:70
  14.3 0.0 collective-permute-done.3
  14.3 0.2 add_convert_fusion.1.after_ref
  14.5 3.3 %shard_map.40 = (bf16[4,5,128,128]{3,2,1,0:T(8,128)(2,1)S(1)}, bf16[2,5,128,128]{3,2,1,0:T(8,128)(2,1)S(1)}, bf16[2,5,128,128]{3,2,1,0:T(8,128)(2,1)S(1)}) custom-call(bf16[1536,4096]{1,0:T(8,128)(2,1)S(1)} %get-tuple-element.25.flat_ref, bf16[4,5,128,128]{3,2,1,0:T(8,128)(2,1)S(1)} %add_convert_fusion.1.after_ref), custom_call_target="tpu_custom_call" | custom-call | flops 2617245696 | tf_op jit(solution)/shard_map/pallas_call | solution.py:180
  17.7 1.0 %collective-permute-start.5 = (bf16[2,5,128,128]{3,2,1,0:T(8,128)(2,1)S(1)}, bf16[2,5,128,128]{3,2,1,0:T(8,128)(2,1)S(1)}, u32[]{:S(2)}, u32[]{:S(2)}) collective-permute-start(bf16[2,5,128,128]{3,2,1,0:T(8,128)(2,1)S(1)} %get-tuple-element.33), channel_id=1, source_target_pairs={{0,16},{1,17},{2,18},{3,19},{4,20},{5,21},{6,22},{7,23},{8,24},{9,... | collective-permute-start | bytes 983048 | tf_op jit(solution)/shard_map/ppermute | solution.py:70
  18.8 0.1 collective-permute-start.6
  18.9 1.2 %collective-permute-start.4 = (bf16[4,5,128,128]{3,2,1,0:T(8,128)(2,1)S(1)}, bf16[4,5,128,128]{3,2,1,0:T(8,128)(2,1)S(1)}, u32[]{:S(2)}, u32[]{:S(2)}) collective-permute-start(bf16[4,5,128,128]{3,2,1,0:T(8,128)(2,1)S(1)} %add_convert_fusion.1.after_ref), channel_id=1, source_target_pairs={{0,4},{1,5},{2,6},{3,7},{4,8},{5,9},{6,10},{7,11},{8,12},{9,13},{1... | collective-permute-start | bytes 1966088 | tf_op jit(solution)/shard_map/ppermute | solution.py:70
  20.0 0.0 collective-permute-done.5
  20.0 0.5 collective-permute-done.6
  20.5 0.2 add_convert_fusion
  20.7 2.5 %collective-permute-start.7 = (bf16[4,5,128,128]{3,2,1,0:T(8,128)(2,1)S(1)}, bf16[4,5,128,128]{3,2,1,0:T(8,128)(2,1)S(1)}, u32[]{:S(2)}, u32[]{:S(2)}) collective-permute-start(bf16[4,5,128,128]{3,2,1,0:T(8,128)(2,1)S(1)} %add_convert_fusion), channel_id=1, source_target_pairs={{0,12},{1,13},{2,14},{3,15},{4,0},{5,1},{6,2},{7,3},{8,4},{9,5},{1... | collective-permute-start | bytes 1966088 | tf_op jit(solution)/shard_map/ppermute | solution.py:70
  23.2 0.0 collective-permute-done.1.after_ref.refs_2_
  23.2 3.2 %shard_map.38 = (bf16[4,5,128,128]{3,2,1,0:T(8,128)(2,1)S(1)}, bf16[4,5,128,128]{3,2,1,0:T(8,128)(2,1)S(1)}) custom-call(bf16[1536,4096]{1,0:T(8,128)(2,1)S(1)} %get-tuple-element.25.flat_ref, bf16[4,5,128,128]{3,2,1,0:T(8,128)(2,1)S(1)} %collective-permute-done.1.after_ref.refs_2_), custom_call_target="tpu_custom_call" | custom-call | flops 2617245696 | tf_op jit(solution)/shard_map/pallas_call | solution.py:180
  26.4 0.9 %collective-permute-start.2 = (bf16[4,5,128,128]{3,2,1,0:T(8,128)(2,1)S(1)}, bf16[4,5,128,128]{3,2,1,0:T(8,128)(2,1)S(1)}, u32[]{:S(2)}, u32[]{:S(2)}) collective-permute-start(bf16[4,5,128,128]{3,2,1,0:T(8,128)(2,1)S(1)} %get-tuple-element.29), channel_id=1, source_target_pairs={{0,16},{1,17},{2,18},{3,19},{4,20},{5,21},{6,22},{7,23},{8,24},{9,... | collective-permute-start | bytes 1966088 | tf_op jit(solution)/shard_map/ppermute | solution.py:70
  27.3 2.5 %collective-permute-done.4.refs_3_ = bf16[4,5,128,128]{3,2,1,0:T(8,128)(2,1)S(1)} collective-permute-done((bf16[4,5,128,128]{3,2,1,0:T(8,128)(2,1)S(1)}, bf16[4,5,128,128]{3,2,1,0:T(8,128)(2,1)S(1)}, u32[]{:S(2)}, u32[]{:S(2)}) %collective-permute-start.4) | collective-permute-done | bytes 655392 | tf_op jit(solution)/shard_map/ppermute | solution.py:70
  29.8 0.9 %collective-permute-done.7.refs_4_ = bf16[4,5,128,128]{3,2,1,0:T(8,128)(2,1)S(1)} collective-permute-done((bf16[4,5,128,128]{3,2,1,0:T(8,128)(2,1)S(1)}, bf16[4,5,128,128]{3,2,1,0:T(8,128)(2,1)S(1)}, u32[]{:S(2)}, u32[]{:S(2)}) %collective-permute-start.7) | collective-permute-done | bytes 655392 | tf_op jit(solution)/shard_map/ppermute | solution.py:70
  30.7 0.0 collective-permute-done.2.refs_1_
  30.7 0.4 shard_map.41
  31.1 0.0 copy-start
  31.1 2.0 %collective-permute-start.10 = (bf16[5,128,128]{2,1,0:T(8,128)(2,1)S(1)}, bf16[5,128,128]{2,1,0:T(8,128)(2,1)S(1)}, u32[]{:S(2)}, u32[]{:S(2)}) collective-permute-start(bf16[5,128,128]{2,1,0:T(8,128)(2,1)S(1)} %get-tuple-element.38), channel_id=1, source_target_pairs={{0,3},{1,0},{2,1},{3,2},{4,7},{5,4},{6,5},{7,6},{8,11},{9,8},{10,9... | collective-permute-start | bytes 491528 | tf_op jit(solution)/shard_map/ppermute | solution.py:70
  33.1 0.4 collective-permute-start.8
  33.5 0.7 %collective-permute-start.9 = (bf16[5,128,128]{2,1,0:T(8,128)(2,1)S(1)}, bf16[5,128,128]{2,1,0:T(8,128)(2,1)S(1)}, u32[]{:S(2)}, u32[]{:S(2)}) collective-permute-start(bf16[5,128,128]{2,1,0:T(8,128)(2,1)S(1)} %get-tuple-element.37), channel_id=1, source_target_pairs={{0,1},{1,2},{2,3},{3,0},{4,5},{5,6},{6,7},{7,4},{8,9},{9,10},{10,1... | collective-permute-start | bytes 491528 | tf_op jit(solution)/shard_map/ppermute | solution.py:70
  34.2 3.0 %collective-permute-done.10 = bf16[5,128,128]{2,1,0:T(8,128)(2,1)S(1)} collective-permute-done((bf16[5,128,128]{2,1,0:T(8,128)(2,1)S(1)}, bf16[5,128,128]{2,1,0:T(8,128)(2,1)S(1)}, u32[]{:S(2)}, u32[]{:S(2)}) %collective-permute-start.10) | collective-permute-done | bytes 163872 | tf_op jit(solution)/shard_map/ppermute | solution.py:70
  37.1 1.8 %collective-permute-done.8 = bf16[5,128,128]{2,1,0:T(8,128)(2,1)S(1)} collective-permute-done((bf16[5,128,128]{2,1,0:T(8,128)(2,1)S(1)}, bf16[5,128,128]{2,1,0:T(8,128)(2,1)S(1)}, u32[]{:S(2)}, u32[]{:S(2)}) %collective-permute-start.8) | collective-permute-done | bytes 163872 | tf_op jit(solution)/shard_map/ppermute | solution.py:70
  38.9 1.9 %collective-permute-done.9 = bf16[5,128,128]{2,1,0:T(8,128)(2,1)S(1)} collective-permute-done((bf16[5,128,128]{2,1,0:T(8,128)(2,1)S(1)}, bf16[5,128,128]{2,1,0:T(8,128)(2,1)S(1)}, u32[]{:S(2)}, u32[]{:S(2)}) %collective-permute-start.9) | collective-permute-done | bytes 163872 | tf_op jit(solution)/shard_map/ppermute | solution.py:70
  40.9 0.1 convert_add_fusion.upper_ref
  41.0 2.4 %collective-permute-start.11 = (bf16[4,128,128]{2,1,0:T(8,128)(2,1)S(1)}, bf16[4,128,128]{2,1,0:T(8,128)(2,1)S(1)}, u32[]{:S(2)}, u32[]{:S(2)}) collective-permute-start(bf16[4,128,128]{2,1,0:T(8,128)(2,1)S(1)} %slice.7), channel_id=1, source_target_pairs={{0,1},{1,2},{2,3},{3,4},{4,5},{5,6},{6,7},{7,8},{8,9},{9,10},{10,1... | collective-permute-start | bytes 393224 | tf_op jit(solution)/shard_map/ppermute | solution.py:70
  43.4 5.1 %collective-permute-done.11.lower_ref = bf16[4,128,128]{2,1,0:T(8,128)(2,1)S(1)} collective-permute-done((bf16[4,128,128]{2,1,0:T(8,128)(2,1)S(1)}, bf16[4,128,128]{2,1,0:T(8,128)(2,1)S(1)}, u32[]{:S(2)}, u32[]{:S(2)}) %collective-permute-start.11) | collective-permute-done | bytes 131104 | tf_op jit(solution)/shard_map/ppermute | solution.py:70
  48.5 0.5 shard_map.42
  49.0 3.7 %collective-permute-start.12 = (bf16[6,64,128]{2,1,0:T(8,128)(2,1)S(1)}, bf16[6,64,128]{2,1,0:T(8,128)(2,1)S(1)}, u32[]{:S(2)}, u32[]{:S(2)}) collective-permute-start(bf16[6,64,128]{2,1,0:T(8,128)(2,1)S(1)} %get-tuple-element.40), channel_id=1, source_target_pairs={{0,64},{1,65},{2,66},{3,67},{4,68},{5,69},{6,70},{7,71},{8,72},{9,... | collective-permute-start | bytes 294920 | tf_op jit(solution)/shard_map/ppermute | solution.py:70
  52.7 0.7 %collective-permute-start.13 = (bf16[6,64,128]{2,1,0:T(8,128)(2,1)S(1)}, bf16[6,64,128]{2,1,0:T(8,128)(2,1)S(1)}, u32[]{:S(2)}, u32[]{:S(2)}) collective-permute-start(bf16[6,64,128]{2,1,0:T(8,128)(2,1)S(1)} %get-tuple-element.41), channel_id=1, source_target_pairs={{0,32},{1,33},{2,34},{3,35},{4,36},{5,37},{6,38},{7,39},{8,40},{9,... | collective-permute-start | bytes 294920 | tf_op jit(solution)/shard_map/ppermute | solution.py:70
  53.4 1.9 %collective-permute-start.14 = (bf16[6,64,128]{2,1,0:T(8,128)(2,1)S(1)}, bf16[6,64,128]{2,1,0:T(8,128)(2,1)S(1)}, u32[]{:S(2)}, u32[]{:S(2)}) collective-permute-start(bf16[6,64,128]{2,1,0:T(8,128)(2,1)S(1)} %get-tuple-element.42), channel_id=1, source_target_pairs={{0,96},{1,97},{2,98},{3,99},{4,100},{5,101},{6,102},{7,103},{8,104... | collective-permute-start | bytes 294920 | tf_op jit(solution)/shard_map/ppermute | solution.py:70
  55.3 0.0 collective-permute-done.12.first_ref
  55.3 2.0 %collective-permute-done.13.second_ref = bf16[6,64,128]{2,1,0:T(8,128)(2,1)S(1)} collective-permute-done((bf16[6,64,128]{2,1,0:T(8,128)(2,1)S(1)}, bf16[6,64,128]{2,1,0:T(8,128)(2,1)S(1)}, u32[]{:S(2)}, u32[]{:S(2)}) %collective-permute-start.13) | collective-permute-done | bytes 98336 | tf_op jit(solution)/shard_map/ppermute | solution.py:70
  57.3 0.0 collective-permute-done.14.third_ref
  57.4 5.1 %collective-permute-start.15 = (f32[5,32,128]{2,1,0:T(8,128)S(1)}, f32[5,32,128]{2,1,0:T(8,128)S(1)}, u32[]{:S(2)}, u32[]{:S(2)}) collective-permute-start(f32[5,32,128]{2,1,0:T(8,128)S(1)} %get-tuple-element.44), channel_id=1, source_target_pairs={{0,16},{1,17},{2,18},{3,19},{4,20},{5,21},{6,22},{7,23},{8,24},{9,... | collective-permute-start | bytes 245768 | tf_op jit(solution)/shard_map/ppermute | solution.py:70
  62.5 0.9 %collective-permute-done.15.other_ref = f32[5,32,128]{2,1,0:T(8,128)S(1)} collective-permute-done((f32[5,32,128]{2,1,0:T(8,128)S(1)}, f32[5,32,128]{2,1,0:T(8,128)S(1)}, u32[]{:S(2)}, u32[]{:S(2)}) %collective-permute-start.15) | collective-permute-done | bytes 81952 | tf_op jit(solution)/shard_map/ppermute | solution.py:70
  63.4 0.0 copy-done
  63.4 1.4 %shard_map.44 = f32[32,1152]{1,0:T(8,128)} custom-call(s32[32]{0:T(128)S(1)} %copy-done.1, s32[5,32]{1,0:T(8,128)S(1)} %bitcast.2, f32[5,32,128]{2,1,0:T(8,128)S(1)} %get-tuple-element.43.own_ref, f32[5,32,128]{2,1,0:T(8,128)S(1)} %collective-permute-done.15.other_ref), custom_call_target="tpu_custom_call" | custom-call | tf_op jit(solution)/shard_map/pallas_call | solution.py:316
  (2 shorter events, 0.1 us)
Async XLA Ops:
  0.0 7.8 %copy-start.1 = (s32[32]{0:T(128)S(1)}, s32[32]{0:T(128)}, u32[]{:S(2)}) copy-start(s32[32]{0:T(128)} %size_ref.1) | copy-start | bytes 388
  6.2 4.9 %collective-permute-start = (bf16[4,5,128,128]{3,2,1,0:T(8,128)(2,1)S(1)}, bf16[4,5,128,128]{3,2,1,0:T(8,128)(2,1)S(1)}, u32[]{:S(2)}, u32[]{:S(2)}) collective-permute-start(bf16[4,5,128,128]{3,2,1,0:T(8,128)(2,1)S(1)} %get-tuple-element.27), channel_id=1, source_target_pairs={{0,16},{1,17},{2,18},{3,19},{4,20},{5,21},{6,22},{7,23},{8,24},{9,... | collective-permute-start | bytes 1966088 | tf_op jit(solution)/shard_map/ppermute | solution.py:70
  11.0 3.2 %collective-permute-start.3 = (bf16[4,5,128,128]{3,2,1,0:T(8,128)(2,1)S(1)}, bf16[4,5,128,128]{3,2,1,0:T(8,128)(2,1)S(1)}, u32[]{:S(2)}, u32[]{:S(2)}) collective-permute-start(bf16[4,5,128,128]{3,2,1,0:T(8,128)(2,1)S(1)} %get-tuple-element.31), channel_id=1, source_target_pairs={{0,16},{1,17},{2,18},{3,19},{4,20},{5,21},{6,22},{7,23},{8,24},{9,... | collective-permute-start | bytes 1966088 | tf_op jit(solution)/shard_map/ppermute | solution.py:70
  11.4 11.8 %collective-permute-start.1 = (bf16[4,5,128,128]{3,2,1,0:T(8,128)(2,1)S(1)}, bf16[4,5,128,128]{3,2,1,0:T(8,128)(2,1)S(1)}, u32[]{:S(2)}, u32[]{:S(2)}) collective-permute-start(bf16[4,5,128,128]{3,2,1,0:T(8,128)(2,1)S(1)} %add_convert_fusion.2), channel_id=1, source_target_pairs={{0,8},{1,9},{2,10},{3,11},{4,12},{5,13},{6,14},{7,15},{8,0},{9,1},... | collective-permute-start | bytes 1966088 | tf_op jit(solution)/shard_map/ppermute | solution.py:70
  17.7 2.3 %collective-permute-start.5 = (bf16[2,5,128,128]{3,2,1,0:T(8,128)(2,1)S(1)}, bf16[2,5,128,128]{3,2,1,0:T(8,128)(2,1)S(1)}, u32[]{:S(2)}, u32[]{:S(2)}) collective-permute-start(bf16[2,5,128,128]{3,2,1,0:T(8,128)(2,1)S(1)} %get-tuple-element.33), channel_id=1, source_target_pairs={{0,16},{1,17},{2,18},{3,19},{4,20},{5,21},{6,22},{7,23},{8,24},{9,... | collective-permute-start | bytes 983048 | tf_op jit(solution)/shard_map/ppermute | solution.py:70
  18.8 1.7 %collective-permute-start.6 = (bf16[2,5,128,128]{3,2,1,0:T(8,128)(2,1)S(1)}, bf16[2,5,128,128]{3,2,1,0:T(8,128)(2,1)S(1)}, u32[]{:S(2)}, u32[]{:S(2)}) collective-permute-start(bf16[2,5,128,128]{3,2,1,0:T(8,128)(2,1)S(1)} %get-tuple-element.34), channel_id=1, source_target_pairs={{0,16},{1,17},{2,18},{3,19},{4,20},{5,21},{6,22},{7,23},{8,24},{9,... | collective-permute-start | bytes 983048 | tf_op jit(solution)/shard_map/ppermute | solution.py:70
  18.9 10.9 %collective-permute-start.4 = (bf16[4,5,128,128]{3,2,1,0:T(8,128)(2,1)S(1)}, bf16[4,5,128,128]{3,2,1,0:T(8,128)(2,1)S(1)}, u32[]{:S(2)}, u32[]{:S(2)}) collective-permute-start(bf16[4,5,128,128]{3,2,1,0:T(8,128)(2,1)S(1)} %add_convert_fusion.1.after_ref), channel_id=1, source_target_pairs={{0,4},{1,5},{2,6},{3,7},{4,8},{5,9},{6,10},{7,11},{8,12},{9,13},{1... | collective-permute-start | bytes 1966088 | tf_op jit(solution)/shard_map/ppermute | solution.py:70
  20.7 10.0 %collective-permute-start.7 = (bf16[4,5,128,128]{3,2,1,0:T(8,128)(2,1)S(1)}, bf16[4,5,128,128]{3,2,1,0:T(8,128)(2,1)S(1)}, u32[]{:S(2)}, u32[]{:S(2)}) collective-permute-start(bf16[4,5,128,128]{3,2,1,0:T(8,128)(2,1)S(1)} %add_convert_fusion), channel_id=1, source_target_pairs={{0,12},{1,13},{2,14},{3,15},{4,0},{5,1},{6,2},{7,3},{8,4},{9,5},{1... | collective-permute-start | bytes 1966088 | tf_op jit(solution)/shard_map/ppermute | solution.py:70
  26.4 4.3 %collective-permute-start.2 = (bf16[4,5,128,128]{3,2,1,0:T(8,128)(2,1)S(1)}, bf16[4,5,128,128]{3,2,1,0:T(8,128)(2,1)S(1)}, u32[]{:S(2)}, u32[]{:S(2)}) collective-permute-start(bf16[4,5,128,128]{3,2,1,0:T(8,128)(2,1)S(1)} %get-tuple-element.29), channel_id=1, source_target_pairs={{0,16},{1,17},{2,18},{3,19},{4,20},{5,21},{6,22},{7,23},{8,24},{9,... | collective-permute-start | bytes 1966088 | tf_op jit(solution)/shard_map/ppermute | solution.py:70
  31.1 32.3 %copy-start = (s32[32,5]{0,1:T(8,128)S(1)}, s32[32,5]{0,1:T(8,128)}, u32[]{:S(2)}) copy-start(s32[32,5]{0,1:T(8,128)} %param.5) | copy-start | bytes 1924
  31.1 6.0 %collective-permute-start.10 = (bf16[5,128,128]{2,1,0:T(8,128)(2,1)S(1)}, bf16[5,128,128]{2,1,0:T(8,128)(2,1)S(1)}, u32[]{:S(2)}, u32[]{:S(2)}) collective-permute-start(bf16[5,128,128]{2,1,0:T(8,128)(2,1)S(1)} %get-tuple-element.38), channel_id=1, source_target_pairs={{0,3},{1,0},{2,1},{3,2},{4,7},{5,4},{6,5},{7,6},{8,11},{9,8},{10,9... | collective-permute-start | bytes 491528 | tf_op jit(solution)/shard_map/ppermute | solution.py:70
  33.1 5.8 %collective-permute-start.8 = (bf16[5,128,128]{2,1,0:T(8,128)(2,1)S(1)}, bf16[5,128,128]{2,1,0:T(8,128)(2,1)S(1)}, u32[]{:S(2)}, u32[]{:S(2)}) collective-permute-start(bf16[5,128,128]{2,1,0:T(8,128)(2,1)S(1)} %get-tuple-element.36), channel_id=1, source_target_pairs={{0,2},{1,3},{2,0},{3,1},{4,6},{5,7},{6,4},{7,5},{8,10},{9,11},{10,... | collective-permute-start | bytes 491528 | tf_op jit(solution)/shard_map/ppermute | solution.py:70
  33.5 7.4 %collective-permute-start.9 = (bf16[5,128,128]{2,1,0:T(8,128)(2,1)S(1)}, bf16[5,128,128]{2,1,0:T(8,128)(2,1)S(1)}, u32[]{:S(2)}, u32[]{:S(2)}) collective-permute-start(bf16[5,128,128]{2,1,0:T(8,128)(2,1)S(1)} %get-tuple-element.37), channel_id=1, source_target_pairs={{0,1},{1,2},{2,3},{3,0},{4,5},{5,6},{6,7},{7,4},{8,9},{9,10},{10,1... | collective-permute-start | bytes 491528 | tf_op jit(solution)/shard_map/ppermute | solution.py:70
  41.0 7.5 %collective-permute-start.11 = (bf16[4,128,128]{2,1,0:T(8,128)(2,1)S(1)}, bf16[4,128,128]{2,1,0:T(8,128)(2,1)S(1)}, u32[]{:S(2)}, u32[]{:S(2)}) collective-permute-start(bf16[4,128,128]{2,1,0:T(8,128)(2,1)S(1)} %slice.7), channel_id=1, source_target_pairs={{0,1},{1,2},{2,3},{3,4},{4,5},{5,6},{6,7},{7,8},{8,9},{9,10},{10,1... | collective-permute-start | bytes 393224 | tf_op jit(solution)/shard_map/ppermute | solution.py:70
  49.0 6.4 %collective-permute-start.12 = (bf16[6,64,128]{2,1,0:T(8,128)(2,1)S(1)}, bf16[6,64,128]{2,1,0:T(8,128)(2,1)S(1)}, u32[]{:S(2)}, u32[]{:S(2)}) collective-permute-start(bf16[6,64,128]{2,1,0:T(8,128)(2,1)S(1)} %get-tuple-element.40), channel_id=1, source_target_pairs={{0,64},{1,65},{2,66},{3,67},{4,68},{5,69},{6,70},{7,71},{8,72},{9,... | collective-permute-start | bytes 294920 | tf_op jit(solution)/shard_map/ppermute | solution.py:70
  52.7 4.7 %collective-permute-start.13 = (bf16[6,64,128]{2,1,0:T(8,128)(2,1)S(1)}, bf16[6,64,128]{2,1,0:T(8,128)(2,1)S(1)}, u32[]{:S(2)}, u32[]{:S(2)}) collective-permute-start(bf16[6,64,128]{2,1,0:T(8,128)(2,1)S(1)} %get-tuple-element.41), channel_id=1, source_target_pairs={{0,32},{1,33},{2,34},{3,35},{4,36},{5,37},{6,38},{7,39},{8,40},{9,... | collective-permute-start | bytes 294920 | tf_op jit(solution)/shard_map/ppermute | solution.py:70
  53.4 3.9 %collective-permute-start.14 = (bf16[6,64,128]{2,1,0:T(8,128)(2,1)S(1)}, bf16[6,64,128]{2,1,0:T(8,128)(2,1)S(1)}, u32[]{:S(2)}, u32[]{:S(2)}) collective-permute-start(bf16[6,64,128]{2,1,0:T(8,128)(2,1)S(1)} %get-tuple-element.42), channel_id=1, source_target_pairs={{0,96},{1,97},{2,98},{3,99},{4,100},{5,101},{6,102},{7,103},{8,104... | collective-permute-start | bytes 294920 | tf_op jit(solution)/shard_map/ppermute | solution.py:70
  57.4 6.0 %collective-permute-start.15 = (f32[5,32,128]{2,1,0:T(8,128)S(1)}, f32[5,32,128]{2,1,0:T(8,128)S(1)}, u32[]{:S(2)}, u32[]{:S(2)}) collective-permute-start(f32[5,32,128]{2,1,0:T(8,128)S(1)} %get-tuple-element.44), channel_id=1, source_target_pairs={{0,16},{1,17},{2,18},{3,19},{4,20},{5,21},{6,22},{7,23},{8,24},{9,... | collective-permute-start | bytes 245768 | tf_op jit(solution)/shard_map/ppermute | solution.py:70

commit v3 on v2

--- a/solution.py
+++ b/solution.py
@@ -23,12 +23,11 @@
     ((0, 0), (0, 2), (0, 3), (1, 1), (1, 2)),
     ((1, 0), (0, 1), (0, 4), (1, 3), (1, 4)),
 )
-PANEL = {
-    (0, 0): ((0, 1, 2, 5, 7), (4, 6, 7, 2, 3)),
-    (1, 0): ((1, 2, 6, 7), (5, 8, 0, 1)),
-    (0, 1): ((3, 4, 6, 8), (5, 6, 1, 2)),
-    (1, 1): ((0, 3, 4, 5, 8), (4, 7, 8, 3, 0)),
-}
+MIRROR = BAND
+UPPER = {(0, 0): (0, 1, 2), (1, 0): (1, 2), (0, 1): (3, 4), (1, 1): (0, 3, 4, MIRROR)}
+LOWER = {(0, 0): (1, 3), (1, 0): (2, 3), (0, 1): (2, 4), (1, 1): (4,)}
+SLOTS = {(0, 0): (4, 6, 7, 2, 3), (1, 0): (5, 8, 0, 1), (0, 1): (5, 6, 1, 2), (1, 1): (4, 7, 8, 3, 0)}
+SLOT_COUNT = 2 * BAND - 1
 STEPS = (2, 1, 3, 0)
 
 
@@ -144,6 +143,23 @@
         put_tiles(parts, position, core, mine_ref, theirs_ref)
 
 
+def last_kernel(size_ref, screen_ref, flat_ref, after_ref, mine_ref, theirs_ref, mask_ref, *, step, factor):
+    later_kernel(flat_ref, after_ref, mine_ref, theirs_ref, step=step)
+    z, core, bas = place_here()
+    block = bas * 2 + z // 2
+    rows = lax.broadcasted_iota(jnp.int32, (32, BW), 0) + (z % 2) * 64 + core * 32
+    columns = lax.broadcasted_iota(jnp.int32, (32, BW), 1)
+    row_mask = rows < size_ref[block]
+    for slot in range(SLOT_COUNT):
+        offset = slot - (BAND - 1)
+        partner = jnp.clip(block + offset, 0, NB - 1)
+        inside = jnp.logical_and(block + offset >= 0, block + offset < NB)
+        kept = jnp.where(inside, screen_ref[abs(offset), jnp.minimum(block, partner)], 0)
+        limit = jnp.where(kept > 0, size_ref[partner], 0)
+        mask = jnp.logical_and(row_mask, columns < limit)
+        mask_ref[:, slot * BW : (slot + 1) * BW] = jnp.where(mask, factor, 0.0)
+
+
 VMEM = pl.BlockSpec(memory_space=pltpu.VMEM)
 ANYWHERE = pl.BlockSpec(memory_space=pl.ANY)
 SMALL = pltpu.CompilerParams(vmem_limit_bytes=4 << 20)
@@ -187,6 +203,18 @@
     )(flat, after)
 
 
+def last_tiles(block_size, screen, flat, after, step):
+    factor = 1.0 / math.sqrt(AUX * OCC)
+    return pl.pallas_call(
+        functools.partial(last_kernel, step=step, factor=factor),
+        in_specs=[SCALARS, SCALARS, VMEM, ANYWHERE],
+        out_specs=[VMEM] * 3,
+        out_shape=[SET, SET, jax.ShapeDtypeStruct((32, SLOT_COUNT * BW), F32)],
+        compiler_params=pltpu.CompilerParams(vmem_limit_bytes=16 << 20),
+        cost_estimate=cost(flat.shape[0]),
+    )(block_size, screen.T, flat, after)
+
+
 def total_kernel(*refs):
     mine_ref, other_ref, *arrived, own_ref, first_ref, second_ref, third_ref = refs
     for position, out_ref in enumerate((own_ref, first_ref, second_ref, third_ref)):
@@ -211,115 +239,143 @@
     return (mine.astype(F32) + other.astype(F32)).astype(BF16)
 
 
-def pack_kernel(upper_ref, lower_ref, own_ref, *sent_refs):
+def pack_kernel(own_ref, first_ref, second_ref, third_ref, kept_ref, turned_ref, *refs):
+    upper_refs, sums_ref, mirror_ref = refs[:3], refs[3], refs[4]
     z, core, _ = place_here()
+    for index in range(BAND):
+        total = own_ref[index]
+        for ref in (first_ref, second_ref, third_ref):
+            total = total + ref[index].astype(F32)
+        sums_ref[index] = total
+        if index > 0:
+            turned = total.T
+            turned_ref[index - 1] = turned.astype(BF16)
+            if index == 1:
+                mirror_ref[...] = turned
     for mine in range(2):
         for row in range(2):
-            tiles = PANEL[(mine, row)][0]
             for half in range(2):
                 target = row * 2 + half
                 rows = pl.ds(half * 64, 64)
+                upper = UPPER[(mine, row)]
 
                 def value(index):
-                    if index < BAND:
-                        return upper_ref[index, rows]
-                    if mine == 1 and index == BAND:
-                        return upper_ref[1, :, rows].T
-                    return lower_ref[index - BAND, :, rows].astype(F32).T
+                    return mirror_ref[rows] if index == MIRROR else sums_ref[index, rows]
 
                 @pl.when(jnp.logical_and(core == mine, z == target))
                 def _():
-                    for place, index in enumerate(tiles):
-                        own_ref[place] = value(index)
-                    if len(tiles) < BAND:
-                        own_ref[BAND - 1] = jnp.zeros((64, BW), F32)
+                    for place, index in enumerate(upper):
+                        kept_ref[place] = value(index)
 
                 for step in range(1, 4):
 
                     @pl.when(jnp.logical_and(core == mine, (z + step) % 4 == target))
                     def _():
-                        out_ref = sent_refs[step - 1]
-                        rest = jnp.zeros((64, BW), BF16)
-                        for place, index in enumerate(tiles):
+                        out_ref = upper_refs[step - 1]
+                        for place in range(BAND):
+                            out_ref[place] = jnp.zeros((64, BW), BF16)
+                        for place, index in enumerate(upper):
                             whole = value(index)
                             high = whole.astype(BF16)
                             out_ref[place] = high
                             if index == 0:
-                                rest = (whole - high.astype(F32)).astype(BF16)
-                        if len(tiles) < BAND:
-                            out_ref[BAND - 1] = jnp.zeros((64, BW), BF16)
-                        out_ref[BAND] = rest
-
-
-def pack(upper, lower):
-    own = jax.ShapeDtypeStruct((BAND, 64, BW), F32)
-    sent = jax.ShapeDtypeStruct((BAND + 1, 64, BW), BF16)
+                                out_ref[BAND - 1] = (whole - high.astype(F32)).astype(BF16)
+
+
+def pack(own, arrived):
+    kept = jax.ShapeDtypeStruct((BAND - 1, 64, BW), F32)
+    turned = jax.ShapeDtypeStruct((BAND - 1, BW, BW), BF16)
+    upper = jax.ShapeDtypeStruct((BAND, 64, BW), BF16)
     return pl.pallas_call(
         pack_kernel,
-        in_specs=[VMEM, VMEM],
-        out_specs=[VMEM] * 4,
-        out_shape=[own] + [sent] * 3,
+        in_specs=[VMEM] * 4,
+        out_specs=[VMEM] * 5,
+        out_shape=[kept, turned] + [upper] * 3,
+        scratch_shapes=[pltpu.VMEM((BAND, BW, BW), F32), pltpu.VMEM((BW, BW), F32)],
         compiler_params=SMALL,
-    )(upper, lower)
-
-
-def split_kernel(own_ref, first_ref, second_ref, third_ref, kept_ref, sent_ref):
+    )(own, *arrived)
+
+
+def lower_kernel(turned_ref, *out_refs):
+    z, core, _ = place_here()
+    for mine in range(2):
+        for row in range(2):
+            for half in range(2):
+                for step in range(4):
+
+                    @pl.when(jnp.logical_and(core == mine, (z + step) % 4 == row * 2 + half))
+                    def _():
+                        lower = LOWER[(mine, row)]
+                        for place in range(2):
+                            index = lower[min(place, len(lower) - 1)] - 1
+                            out_refs[step][place] = turned_ref[index, half * 64 : half * 64 + 64]
+
+
+def pack_lower(turned):
+    lower = jax.ShapeDtypeStruct((2, 64, BW), BF16)
+    return pl.pallas_call(
+        lower_kernel, in_specs=[VMEM], out_specs=[VMEM] * 4, out_shape=[lower] * 4, compiler_params=SMALL
+    )(turned)
+
+
+def split_kernel(own_ref, *refs):
+    upper_refs, lower_refs, kept_ref, sent_ref = refs[:3], refs[3:7], refs[7], refs[8]
     z, core, _ = place_here()
     for ref, part in ((kept_ref, core), (sent_ref, 1 - core)):
         rows = pl.ds(pl.multiple_of(part * 32, 32), 32)
-        for place in range(BAND):
-            total = own_ref[place, rows]
-            for source in (first_ref, second_ref, third_ref):
-                total = total + source[place, rows].astype(F32)
-                if place == 0:
-                    total = total + source[BAND, rows].astype(F32)
-            ref[place] = total
-
-
-def split(own, arrived):
+        for mine in range(2):
+            for row in range(2):
+
+                @pl.when(jnp.logical_and(core == mine, z // 2 == row))
+                def _():
+                    count = len(UPPER[(mine, row)])
+                    for place in range(count):
+                        total = own_ref[place, rows]
+                        for source in upper_refs:
+                            total = total + source[place, rows].astype(F32)
+                            if UPPER[(mine, row)][place] == 0:
+                                total = total + source[BAND - 1, rows].astype(F32)
+                        ref[place] = total
+                    for place in range(len(LOWER[(mine, row)])):
+                        first, second, third, fourth = (source[place, rows].astype(F32) for source in lower_refs)
+                        ref[count + place] = (first + second) + (third + fourth)
+                    for place in range(len(SLOTS[(mine, row)]), BAND):
+                        ref[place] = jnp.zeros((32, BW), F32)
+
+
+def split(own, upper, lower):
     shape = jax.ShapeDtypeStruct((BAND, 32, BW), F32)
     return pl.pallas_call(
         split_kernel,
-        in_specs=[VMEM] * 4,
+        in_specs=[VMEM] * 8,
         out_specs=[VMEM] * 2,
         out_shape=[shape] * 2,
         compiler_params=SMALL,
-    )(own, *arrived)
-
-
-def final_kernel(size_ref, screen_ref, own_ref, other_ref, out_ref, *, factor):
-    z, core, owner = place_here()
+    )(own, *upper, *lower)
+
+
+def final_kernel(mask_ref, own_ref, other_ref, out_ref):
+    z, core, _ = place_here()
     for row in range(2):
         for mine in range(2):
 
             @pl.when(jnp.logical_and(core == mine, z // 2 == row))
             def _():
-                block = owner * 2 + row
-                start = (z % 2) * 64 + mine * 32
-                rows = lax.broadcasted_iota(jnp.int32, (32, BW), 0) + start
-                columns = lax.broadcasted_iota(jnp.int32, (32, BW), 1)
-                row_mask = rows < size_ref[block]
                 for half in range(2):
                     source = own_ref if half == mine else other_ref
-                    for place, slot in enumerate(PANEL[(half, row)][1]):
-                        offset = slot - (BAND - 1)
-                        partner = jnp.clip(block + offset, 0, NB - 1)
-                        inside = jnp.logical_and(block + offset >= 0, block + offset < NB)
-                        kept = jnp.where(inside, screen_ref[abs(offset), jnp.minimum(block, partner)], 0)
-                        limit = jnp.where(kept > 0, size_ref[partner], 0)
-                        mask = jnp.logical_and(row_mask, columns < limit)
-                        out_ref[:, slot * BW : (slot + 1) * BW] = jnp.where(mask, source[place] * factor, 0.0)
-
-
-def final(block_size, screen, own, other):
-    factor = 1.0 / math.sqrt(AUX * OCC)
-    return pl.pallas_call(
-        functools.partial(final_kernel, factor=factor),
-        in_specs=[SCALARS, SCALARS, VMEM, VMEM],
+                    for place, slot in enumerate(SLOTS[(half, row)]):
+                        columns = slice(slot * BW, (slot + 1) * BW)
+                        out_ref[:, columns] = source[place] * mask_ref[:, columns]
+
+
+def final(mask, own, other):
+    return pl.pallas_call(
+        final_kernel,
+        in_specs=[VMEM] * 3,
         out_specs=VMEM,
-        out_shape=jax.ShapeDtypeStruct((32, (2 * BAND - 1) * BW), F32),
+        out_shape=jax.ShapeDtypeStruct(mask.shape, F32),
         compiler_params=SMALL,
-    )(block_size, screen.T, own, other)
+    )(mask, own, other)
 
 
 def local(three_index, block_size, screen):
@@ -340,18 +396,16 @@
     mine, *theirs = later_tiles(held, sent2, STEPS[2], 2)
     other = exchanged(theirs)
     sent3, arrived3 = passed(STEPS[2], mine, other)
-    mine, *theirs = later_tiles(held, arrived1, STEPS[3], 1)
-    upper, *outgoing = first_total(mine, exchanged(theirs), [arrived1, arrived2, arrived3])
-    arrived = [send(outgoing[step - 1], plane_pairs(step, False)) for step in (2, 1, 3)]
-    for piece in arrived:
-        upper = upper + piece.astype(F32)
-
-    lower = send(upper[1:].astype(BF16), mirror_pairs())
-    own, *outgoing = pack(upper, lower)
-    arrived = [send(outgoing[step - 1], z_pairs(step)) for step in (2, 1, 3)]
-    own, theirs = split(own, arrived)
-    other = send(theirs, core_pairs())
-    return final(block_size, screen, own, other)
+    mine, theirs, mask = last_tiles(block_size, screen, held, arrived1, STEPS[3])
+    own, *outgoing = first_total(mine, send(theirs, core_pairs()), [arrived1, arrived2, arrived3])
+    arrived = [send(outgoing[step - 1], plane_pairs(step, False)) for step in (1, 3, 2)]
+    own, turned, *outgoing = pack(own, arrived)
+    turned = send(turned, mirror_pairs())
+    upper = [send(outgoing[step - 1], z_pairs(step)) for step in (1, 3, 2)]
+    kept, *outgoing = pack_lower(turned)
+    lower = [kept] + [send(outgoing[step - 1], z_pairs(step)) for step in (1, 3, 2)]
+    own, theirs = split(own, upper, lower)
+    return final(mask, own, send(theirs, core_pairs()))
 
 
 def solution(mesh):

time: 64.9 us -> 62.2 us (0.958)
  waiting for transfers between devices: 18.6 us -> 9.92 us
  starting transfers between devices: 27.1 us -> 33.4 us
    ppermute x16 -> x19, waiting for transfers between devices: 18.6 us -> 9.92 us  [send(): return lax.ppermute(value, AXES, pairs)]
    ppermute x16 -> x19, starting transfers between devices: 27.1 us -> 33.4 us  [send(): return lax.ppermute(value, AXES, pairs)]
    pallas_call x3 -> x2, Pallas kernels: 9.74 us -> 6.52 us  [later_tiles(): pl.pallas_call(functools.partial(later_kernel, step=step), in_specs=[VMEM...]
    pallas_call x3 -> x5, Pallas kernels: 1.94 us -> 4.94 us  [the longest x1 3.81 us: last_tiles(): pl.pallas_call(functools.partial(last_kernel, step=step, factor=factor),...]
  transfers between devices with their start and end apart: 16 -> 19, of which waited for: 9 -> 8; matrix products, arithmetic and copies ran while one was open for 1% -> 1% of each run, Pallas kernels for 15% -> 17%
where the time goes in v3:
time: 62.2 us; the launch traced here: 62.1 us
  starting transfers between devices  33.4 us (54%)
  Pallas kernels  18.1 us (29%)
  waiting for transfers between devices  9.92 us (16%)
    ppermute x19, starting transfers between devices, send(): return lax.ppermute(value, AXES, pairs)  33.4 us
    ppermute x19, waiting for transfers between devices, send(): return lax.ppermute(value, AXES, pairs)  9.92 us
    pallas_call x2, Pallas kernels, later_tiles(): pl.pallas_call(functools.partial(later_kernel, step=step), in_specs=[VMEM...  6.52 us
    pallas_call x1, Pallas kernels, first_tiles(): pl.pallas_call(functools.partial(first_kernel, step=step), in_specs=[ANYW...  6.24 us
    pallas_call x1, Pallas kernels, last_tiles(): pl.pallas_call(functools.partial(last_kernel, step=step, factor=factor),...  3.81 us
  transfers between devices with their start and end apart: 19, of which 8 were waited for; matrix products, arithmetic and copies ran while one was open for 1% of the time, Pallas kernels for 17%

profile of v3, /device:TPU:1, one launch (start us, length us, event | category | flops | bytes accessed | tf_op | source)
XLA Modules:
  0.0 62.1 jit_solution(7548973526879916365)
XLA Ops:
  0.0 6.2 %shard_map.37 = (bf16[4,5,128,128]{3,2,1,0:T(8,128)(2,1)S(1)}, bf16[4,5,128,128]{3,2,1,0:T(8,128)(2,1)S(1)}, bf16[1536,4096]{1,0:T(8,128)(2,1)S(1)}) custom-call(bf16[1536,4096]{1,0:T(8,128)(2,1)} %bitcast.3), custom_call_target="tpu_custom_call" | custom-call | flops 2617245696 | bytes 12582912 | tf_op jit(solution)/shard_map/pallas_call | solution.py:180
  6.2 1.5 %collective-permute-start = (bf16[4,5,128,128]{3,2,1,0:T(8,128)(2,1)S(1)}, bf16[4,5,128,128]{3,2,1,0:T(8,128)(2,1)S(1)}, u32[]{:S(2)}, u32[]{:S(2)}) collective-permute-start(bf16[4,5,128,128]{3,2,1,0:T(8,128)(2,1)S(1)} %get-tuple-element.33), channel_id=1, source_target_pairs={{0,16},{1,17},{2,18},{3,19},{4,20},{5,21},{6,22},{7,23},{8,24},{9,... | collective-permute-start | bytes 1966088 | tf_op jit(solution)/shard_map/ppermute | solution.py:69
  7.8 3.2 %shard_map.39 = (bf16[4,5,128,128]{3,2,1,0:T(8,128)(2,1)S(1)}, bf16[4,5,128,128]{3,2,1,0:T(8,128)(2,1)S(1)}) custom-call(bf16[1536,4096]{1,0:T(8,128)(2,1)S(1)} %get-tuple-element.31.flat_ref, s32[32]{0:T(128)S(1)} %copy-done.1), custom_call_target="tpu_custom_call" | custom-call | flops 2617245696 | tf_op jit(solution)/shard_map/pallas_call | solution.py:196
  11.0 0.1 collective-permute-start.3
  11.1 0.0 collective-permute-done
  11.1 0.2 add_convert_fusion.2
  11.3 2.9 %collective-permute-start.1 = (bf16[4,5,128,128]{3,2,1,0:T(8,128)(2,1)S(1)}, bf16[4,5,128,128]{3,2,1,0:T(8,128)(2,1)S(1)}, u32[]{:S(2)}, u32[]{:S(2)}) collective-permute-start(bf16[4,5,128,128]{3,2,1,0:T(8,128)(2,1)S(1)} %add_convert_fusion.2), channel_id=1, source_target_pairs={{0,8},{1,9},{2,10},{3,11},{4,12},{5,13},{6,14},{7,15},{8,0},{9,1},... | collective-permute-start | bytes 1966088 | tf_op jit(solution)/shard_map/ppermute | solution.py:69
  14.2 0.0 collective-permute-done.3
  14.2 0.2 add_convert_fusion.1.after_ref
  14.4 3.3 %shard_map.40 = (bf16[4,5,128,128]{3,2,1,0:T(8,128)(2,1)S(1)}, bf16[2,5,128,128]{3,2,1,0:T(8,128)(2,1)S(1)}, bf16[2,5,128,128]{3,2,1,0:T(8,128)(2,1)S(1)}) custom-call(bf16[1536,4096]{1,0:T(8,128)(2,1)S(1)} %get-tuple-element.31.flat_ref, bf16[4,5,128,128]{3,2,1,0:T(8,128)(2,1)S(1)} %add_convert_fusion.1.after_ref), custom_call_target="tpu_custom_call" | custom-call | flops 2617245696 | tf_op jit(solution)/shard_map/pallas_call | solution.py:196
  17.7 0.0 copy-start
  17.7 1.0 %collective-permute-start.5 = (bf16[2,5,128,128]{3,2,1,0:T(8,128)(2,1)S(1)}, bf16[2,5,128,128]{3,2,1,0:T(8,128)(2,1)S(1)}, u32[]{:S(2)}, u32[]{:S(2)}) collective-permute-start(bf16[2,5,128,128]{3,2,1,0:T(8,128)(2,1)S(1)} %get-tuple-element.40), channel_id=1, source_target_pairs={{0,16},{1,17},{2,18},{3,19},{4,20},{5,21},{6,22},{7,23},{8,24},{9,... | collective-permute-start | bytes 983048 | tf_op jit(solution)/shard_map/ppermute | solution.py:69
  18.7 0.1 collective-permute-start.6
  18.8 1.2 %collective-permute-start.4 = (bf16[4,5,128,128]{3,2,1,0:T(8,128)(2,1)S(1)}, bf16[4,5,128,128]{3,2,1,0:T(8,128)(2,1)S(1)}, u32[]{:S(2)}, u32[]{:S(2)}) collective-permute-start(bf16[4,5,128,128]{3,2,1,0:T(8,128)(2,1)S(1)} %add_convert_fusion.1.after_ref), channel_id=1, source_target_pairs={{0,4},{1,5},{2,6},{3,7},{4,8},{5,9},{6,10},{7,11},{8,12},{9,13},{1... | collective-permute-start | bytes 1966088 | tf_op jit(solution)/shard_map/ppermute | solution.py:69
  20.0 0.0 collective-permute-done.5
  20.0 0.5 collective-permute-done.6
  20.4 0.2 add_convert_fusion
  20.6 2.5 %collective-permute-start.7 = (bf16[4,5,128,128]{3,2,1,0:T(8,128)(2,1)S(1)}, bf16[4,5,128,128]{3,2,1,0:T(8,128)(2,1)S(1)}, u32[]{:S(2)}, u32[]{:S(2)}) collective-permute-start(bf16[4,5,128,128]{3,2,1,0:T(8,128)(2,1)S(1)} %add_convert_fusion), channel_id=1, source_target_pairs={{0,12},{1,13},{2,14},{3,15},{4,0},{5,1},{6,2},{7,3},{8,4},{9,5},{1... | collective-permute-start | bytes 1966088 | tf_op jit(solution)/shard_map/ppermute | solution.py:69
  23.1 0.0 collective-permute-done.1.after_ref.refs_2_
  23.1 3.8 %shard_map.38 = (bf16[4,5,128,128]{3,2,1,0:T(8,128)(2,1)S(1)}, bf16[4,5,128,128]{3,2,1,0:T(8,128)(2,1)S(1)}, f32[32,1152]{1,0:T(8,128)S(1)}) custom-call(s32[32]{0:T(128)S(1)} %copy-done.1, s32[5,32]{1,0:T(8,128)S(1)} %bitcast.2, bf16[1536,4096]{1,0:T(8,128)(2,1)S(1)} %get-tuple-element.31.flat_ref, ...), custom_call_target="tpu_custom_call" | custom-call | flops 2617245696 | tf_op jit(solution)/shard_map/pallas_call | solution.py:208
  26.9 0.9 %collective-permute-start.2 = (bf16[4,5,128,128]{3,2,1,0:T(8,128)(2,1)S(1)}, bf16[4,5,128,128]{3,2,1,0:T(8,128)(2,1)S(1)}, u32[]{:S(2)}, u32[]{:S(2)}) collective-permute-start(bf16[4,5,128,128]{3,2,1,0:T(8,128)(2,1)S(1)} %get-tuple-element.36), channel_id=1, source_target_pairs={{0,16},{1,17},{2,18},{3,19},{4,20},{5,21},{6,22},{7,23},{8,24},{9,... | collective-permute-start | bytes 1966088 | tf_op jit(solution)/shard_map/ppermute | solution.py:69
  27.9 1.9 %collective-permute-done.4.refs_3_ = bf16[4,5,128,128]{3,2,1,0:T(8,128)(2,1)S(1)} collective-permute-done((bf16[4,5,128,128]{3,2,1,0:T(8,128)(2,1)S(1)}, bf16[4,5,128,128]{3,2,1,0:T(8,128)(2,1)S(1)}, u32[]{:S(2)}, u32[]{:S(2)}) %collective-permute-start.4) | collective-permute-done | bytes 655392 | tf_op jit(solution)/shard_map/ppermute | solution.py:69
  29.7 0.9 %collective-permute-done.7.refs_4_ = bf16[4,5,128,128]{3,2,1,0:T(8,128)(2,1)S(1)} collective-permute-done((bf16[4,5,128,128]{3,2,1,0:T(8,128)(2,1)S(1)}, bf16[4,5,128,128]{3,2,1,0:T(8,128)(2,1)S(1)}, u32[]{:S(2)}, u32[]{:S(2)}) %collective-permute-start.7) | collective-permute-done | bytes 655392 | tf_op jit(solution)/shard_map/ppermute | solution.py:69
  30.7 0.0 collective-permute-done.2.refs_1_
  30.7 0.4 shard_map.41
  31.1 2.2 %collective-permute-start.10 = (bf16[5,128,128]{2,1,0:T(8,128)(2,1)S(1)}, bf16[5,128,128]{2,1,0:T(8,128)(2,1)S(1)}, u32[]{:S(2)}, u32[]{:S(2)}) collective-permute-start(bf16[5,128,128]{2,1,0:T(8,128)(2,1)S(1)} %get-tuple-element.45), channel_id=1, source_target_pairs={{0,2},{1,3},{2,0},{3,1},{4,6},{5,7},{6,4},{7,5},{8,10},{9,11},{10,... | collective-permute-start | bytes 491528 | tf_op jit(solution)/shard_map/ppermute | solution.py:69
  33.3 0.4 collective-permute-start.8
  33.7 2.3 %collective-permute-start.9 = (bf16[5,128,128]{2,1,0:T(8,128)(2,1)S(1)}, bf16[5,128,128]{2,1,0:T(8,128)(2,1)S(1)}, u32[]{:S(2)}, u32[]{:S(2)}) collective-permute-start(bf16[5,128,128]{2,1,0:T(8,128)(2,1)S(1)} %get-tuple-element.44), channel_id=1, source_target_pairs={{0,3},{1,0},{2,1},{3,2},{4,7},{5,4},{6,5},{7,6},{8,11},{9,8},{10,9... | collective-permute-start | bytes 491528 | tf_op jit(solution)/shard_map/ppermute | solution.py:69
  36.0 1.2 %collective-permute-done.10.third_ref = bf16[5,128,128]{2,1,0:T(8,128)(2,1)S(1)} collective-permute-done((bf16[5,128,128]{2,1,0:T(8,128)(2,1)S(1)}, bf16[5,128,128]{2,1,0:T(8,128)(2,1)S(1)}, u32[]{:S(2)}, u32[]{:S(2)}) %collective-permute-start.10) | collective-permute-done | bytes 163872 | tf_op jit(solution)/shard_map/ppermute | solution.py:69
  37.1 1.5 %collective-permute-done.8.first_ref = bf16[5,128,128]{2,1,0:T(8,128)(2,1)S(1)} collective-permute-done((bf16[5,128,128]{2,1,0:T(8,128)(2,1)S(1)}, bf16[5,128,128]{2,1,0:T(8,128)(2,1)S(1)}, u32[]{:S(2)}, u32[]{:S(2)}) %collective-permute-start.8) | collective-permute-done | bytes 163872 | tf_op jit(solution)/shard_map/ppermute | solution.py:69
  38.7 0.0 collective-permute-done.9.second_ref
  38.7 0.3 shard_map.42
  39.0 2.8 %collective-permute-start.14 = (bf16[4,128,128]{2,1,0:T(8,128)(2,1)S(1)}, bf16[4,128,128]{2,1,0:T(8,128)(2,1)S(1)}, u32[]{:S(2)}, u32[]{:S(2)}) collective-permute-start(bf16[4,128,128]{2,1,0:T(8,128)(2,1)S(1)} %get-tuple-element.50), channel_id=1, source_target_pairs={{0,1},{1,2},{2,3},{3,4},{4,5},{5,6},{6,7},{7,8},{8,9},{9,10},{10,1... | collective-permute-start | bytes 393224 | tf_op jit(solution)/shard_map/ppermute | solution.py:69
  41.8 1.6 %collective-permute-start.11 = (bf16[5,64,128]{2,1,0:T(8,128)(2,1)S(1)}, bf16[5,64,128]{2,1,0:T(8,128)(2,1)S(1)}, u32[]{:S(2)}, u32[]{:S(2)}) collective-permute-start(bf16[5,64,128]{2,1,0:T(8,128)(2,1)S(1)} %get-tuple-element.47), channel_id=1, source_target_pairs={{0,32},{1,33},{2,34},{3,35},{4,36},{5,37},{6,38},{7,39},{8,40},{9,... | collective-permute-start | bytes 245768 | tf_op jit(solution)/shard_map/ppermute | solution.py:69
  43.4 2.1 %collective-permute-start.12 = (bf16[5,64,128]{2,1,0:T(8,128)(2,1)S(1)}, bf16[5,64,128]{2,1,0:T(8,128)(2,1)S(1)}, u32[]{:S(2)}, u32[]{:S(2)}) collective-permute-start(bf16[5,64,128]{2,1,0:T(8,128)(2,1)S(1)} %get-tuple-element.48), channel_id=1, source_target_pairs={{0,96},{1,97},{2,98},{3,99},{4,100},{5,101},{6,102},{7,103},{8,104... | collective-permute-start | bytes 245768 | tf_op jit(solution)/shard_map/ppermute | solution.py:69
  45.5 1.3 %collective-permute-start.13 = (bf16[5,64,128]{2,1,0:T(8,128)(2,1)S(1)}, bf16[5,64,128]{2,1,0:T(8,128)(2,1)S(1)}, u32[]{:S(2)}, u32[]{:S(2)}) collective-permute-start(bf16[5,64,128]{2,1,0:T(8,128)(2,1)S(1)} %get-tuple-element.49), channel_id=1, source_target_pairs={{0,64},{1,65},{2,66},{3,67},{4,68},{5,69},{6,70},{7,71},{8,72},{9,... | collective-permute-start | bytes 245768 | tf_op jit(solution)/shard_map/ppermute | solution.py:69
  46.8 0.0 collective-permute-done.14.turned_ref
  46.8 0.1 shard_map.43
  46.9 1.4 %collective-permute-start.15 = (bf16[2,64,128]{2,1,0:T(8,128)(2,1)S(1)}, bf16[2,64,128]{2,1,0:T(8,128)(2,1)S(1)}, u32[]{:S(2)}, u32[]{:S(2)}) collective-permute-start(bf16[2,64,128]{2,1,0:T(8,128)(2,1)S(1)} %get-tuple-element.52), channel_id=1, source_target_pairs={{0,32},{1,33},{2,34},{3,35},{4,36},{5,37},{6,38},{7,39},{8,40},{9,... | collective-permute-start | bytes 98312 | tf_op jit(solution)/shard_map/ppermute | solution.py:69
  48.3 2.2 %collective-permute-start.16 = (bf16[2,64,128]{2,1,0:T(8,128)(2,1)S(1)}, bf16[2,64,128]{2,1,0:T(8,128)(2,1)S(1)}, u32[]{:S(2)}, u32[]{:S(2)}) collective-permute-start(bf16[2,64,128]{2,1,0:T(8,128)(2,1)S(1)} %get-tuple-element.53), channel_id=1, source_target_pairs={{0,96},{1,97},{2,98},{3,99},{4,100},{5,101},{6,102},{7,103},{8,104... | collective-permute-start | bytes 98312 | tf_op jit(solution)/shard_map/ppermute | solution.py:69
  50.5 0.0 collective-permute-done.11.refs_0_
  50.5 1.2 %collective-permute-start.17 = (bf16[2,64,128]{2,1,0:T(8,128)(2,1)S(1)}, bf16[2,64,128]{2,1,0:T(8,128)(2,1)S(1)}, u32[]{:S(2)}, u32[]{:S(2)}) collective-permute-start(bf16[2,64,128]{2,1,0:T(8,128)(2,1)S(1)} %get-tuple-element.54), channel_id=1, source_target_pairs={{0,64},{1,65},{2,66},{3,67},{4,68},{5,69},{6,70},{7,71},{8,72},{9,... | collective-permute-start | bytes 98312 | tf_op jit(solution)/shard_map/ppermute | solution.py:69
  51.7 0.6 %collective-permute-done.15.refs_4_ = bf16[2,64,128]{2,1,0:T(8,128)(2,1)S(1)} collective-permute-done((bf16[2,64,128]{2,1,0:T(8,128)(2,1)S(1)}, bf16[2,64,128]{2,1,0:T(8,128)(2,1)S(1)}, u32[]{:S(2)}, u32[]{:S(2)}) %collective-permute-start.15) | collective-permute-done | bytes 32800 | tf_op jit(solution)/shard_map/ppermute | solution.py:69
  52.3 0.0 collective-permute-done.16.refs_5_
  52.3 2.4 %collective-permute-done.17.refs_6_ = bf16[2,64,128]{2,1,0:T(8,128)(2,1)S(1)} collective-permute-done((bf16[2,64,128]{2,1,0:T(8,128)(2,1)S(1)}, bf16[2,64,128]{2,1,0:T(8,128)(2,1)S(1)}, u32[]{:S(2)}, u32[]{:S(2)}) %collective-permute-start.17) | collective-permute-done | bytes 32800 | tf_op jit(solution)/shard_map/ppermute | solution.py:69
  54.8 5.7 %collective-permute-start.18 = (f32[5,32,128]{2,1,0:T(8,128)S(1)}, f32[5,32,128]{2,1,0:T(8,128)S(1)}, u32[]{:S(2)}, u32[]{:S(2)}) collective-permute-start(f32[5,32,128]{2,1,0:T(8,128)S(1)} %get-tuple-element.56), channel_id=1, source_target_pairs={{0,16},{1,17},{2,18},{3,19},{4,20},{5,21},{6,22},{7,23},{8,24},{9,... | collective-permute-start | bytes 245768 | tf_op jit(solution)/shard_map/ppermute | solution.py:69
  60.5 0.9 %collective-permute-done.18.other_ref = f32[5,32,128]{2,1,0:T(8,128)S(1)} collective-permute-done((f32[5,32,128]{2,1,0:T(8,128)S(1)}, f32[5,32,128]{2,1,0:T(8,128)S(1)}, u32[]{:S(2)}, u32[]{:S(2)}) %collective-permute-start.18) | collective-permute-done | bytes 81952 | tf_op jit(solution)/shard_map/ppermute | solution.py:69
  61.4 0.7 %shard_map.45 = f32[32,1152]{1,0:T(8,128)} custom-call(f32[32,1152]{1,0:T(8,128)S(1)} %get-tuple-element.34.mask_ref, f32[5,32,128]{2,1,0:T(8,128)S(1)} %get-tuple-element.55.own_ref, f32[5,32,128]{2,1,0:T(8,128)S(1)} %collective-permute-done.18.other_ref), custom_call_target="tpu_custom_call" | custom-call | tf_op jit(solution)/shard_map/pallas_call | solution.py:372
  (6 shorter events, 0.1 us)
Async XLA Ops:
  0.0 7.8 %copy-start.1 = (s32[32]{0:T(128)S(1)}, s32[32]{0:T(128)}, u32[]{:S(2)}) copy-start(s32[32]{0:T(128)} %after_ref.1) | copy-start | bytes 388
  6.2 4.9 %collective-permute-start = (bf16[4,5,128,128]{3,2,1,0:T(8,128)(2,1)S(1)}, bf16[4,5,128,128]{3,2,1,0:T(8,128)(2,1)S(1)}, u32[]{:S(2)}, u32[]{:S(2)}) collective-permute-start(bf16[4,5,128,128]{3,2,1,0:T(8,128)(2,1)S(1)} %get-tuple-element.33), channel_id=1, source_target_pairs={{0,16},{1,17},{2,18},{3,19},{4,20},{5,21},{6,22},{7,23},{8,24},{9,... | collective-permute-start | bytes 1966088 | tf_op jit(solution)/shard_map/ppermute | solution.py:69
  11.0 3.2 %collective-permute-start.3 = (bf16[4,5,128,128]{3,2,1,0:T(8,128)(2,1)S(1)}, bf16[4,5,128,128]{3,2,1,0:T(8,128)(2,1)S(1)}, u32[]{:S(2)}, u32[]{:S(2)}) collective-permute-start(bf16[4,5,128,128]{3,2,1,0:T(8,128)(2,1)S(1)} %get-tuple-element.38), channel_id=1, source_target_pairs={{0,16},{1,17},{2,18},{3,19},{4,20},{5,21},{6,22},{7,23},{8,24},{9,... | collective-permute-start | bytes 1966088 | tf_op jit(solution)/shard_map/ppermute | solution.py:69
  11.3 11.8 %collective-permute-start.1 = (bf16[4,5,128,128]{3,2,1,0:T(8,128)(2,1)S(1)}, bf16[4,5,128,128]{3,2,1,0:T(8,128)(2,1)S(1)}, u32[]{:S(2)}, u32[]{:S(2)}) collective-permute-start(bf16[4,5,128,128]{3,2,1,0:T(8,128)(2,1)S(1)} %add_convert_fusion.2), channel_id=1, source_target_pairs={{0,8},{1,9},{2,10},{3,11},{4,12},{5,13},{6,14},{7,15},{8,0},{9,1},... | collective-permute-start | bytes 1966088 | tf_op jit(solution)/shard_map/ppermute | solution.py:69
  17.7 5.4 %copy-start = (s32[32,5]{0,1:T(8,128)S(1)}, s32[32,5]{0,1:T(8,128)}, u32[]{:S(2)}) copy-start(s32[32,5]{0,1:T(8,128)} %param.5) | copy-start | bytes 1924
  17.7 2.3 %collective-permute-start.5 = (bf16[2,5,128,128]{3,2,1,0:T(8,128)(2,1)S(1)}, bf16[2,5,128,128]{3,2,1,0:T(8,128)(2,1)S(1)}, u32[]{:S(2)}, u32[]{:S(2)}) collective-permute-start(bf16[2,5,128,128]{3,2,1,0:T(8,128)(2,1)S(1)} %get-tuple-element.40), channel_id=1, source_target_pairs={{0,16},{1,17},{2,18},{3,19},{4,20},{5,21},{6,22},{7,23},{8,24},{9,... | collective-permute-start | bytes 983048 | tf_op jit(solution)/shard_map/ppermute | solution.py:69
  18.7 1.7 %collective-permute-start.6 = (bf16[2,5,128,128]{3,2,1,0:T(8,128)(2,1)S(1)}, bf16[2,5,128,128]{3,2,1,0:T(8,128)(2,1)S(1)}, u32[]{:S(2)}, u32[]{:S(2)}) collective-permute-start(bf16[2,5,128,128]{3,2,1,0:T(8,128)(2,1)S(1)} %get-tuple-element.41), channel_id=1, source_target_pairs={{0,16},{1,17},{2,18},{3,19},{4,20},{5,21},{6,22},{7,23},{8,24},{9,... | collective-permute-start | bytes 983048 | tf_op jit(solution)/shard_map/ppermute | solution.py:69
  18.8 10.9 %collective-permute-start.4 = (bf16[4,5,128,128]{3,2,1,0:T(8,128)(2,1)S(1)}, bf16[4,5,128,128]{3,2,1,0:T(8,128)(2,1)S(1)}, u32[]{:S(2)}, u32[]{:S(2)}) collective-permute-start(bf16[4,5,128,128]{3,2,1,0:T(8,128)(2,1)S(1)} %add_convert_fusion.1.after_ref), channel_id=1, source_target_pairs={{0,4},{1,5},{2,6},{3,7},{4,8},{5,9},{6,10},{7,11},{8,12},{9,13},{1... | collective-permute-start | bytes 1966088 | tf_op jit(solution)/shard_map/ppermute | solution.py:69
  20.6 10.0 %collective-permute-start.7 = (bf16[4,5,128,128]{3,2,1,0:T(8,128)(2,1)S(1)}, bf16[4,5,128,128]{3,2,1,0:T(8,128)(2,1)S(1)}, u32[]{:S(2)}, u32[]{:S(2)}) collective-permute-start(bf16[4,5,128,128]{3,2,1,0:T(8,128)(2,1)S(1)} %add_convert_fusion), channel_id=1, source_target_pairs={{0,12},{1,13},{2,14},{3,15},{4,0},{5,1},{6,2},{7,3},{8,4},{9,5},{1... | collective-permute-start | bytes 1966088 | tf_op jit(solution)/shard_map/ppermute | solution.py:69
  26.9 3.7 %collective-permute-start.2 = (bf16[4,5,128,128]{3,2,1,0:T(8,128)(2,1)S(1)}, bf16[4,5,128,128]{3,2,1,0:T(8,128)(2,1)S(1)}, u32[]{:S(2)}, u32[]{:S(2)}) collective-permute-start(bf16[4,5,128,128]{3,2,1,0:T(8,128)(2,1)S(1)} %get-tuple-element.36), channel_id=1, source_target_pairs={{0,16},{1,17},{2,18},{3,19},{4,20},{5,21},{6,22},{7,23},{8,24},{9,... | collective-permute-start | bytes 1966088 | tf_op jit(solution)/shard_map/ppermute | solution.py:69
  31.1 6.0 %collective-permute-start.10 = (bf16[5,128,128]{2,1,0:T(8,128)(2,1)S(1)}, bf16[5,128,128]{2,1,0:T(8,128)(2,1)S(1)}, u32[]{:S(2)}, u32[]{:S(2)}) collective-permute-start(bf16[5,128,128]{2,1,0:T(8,128)(2,1)S(1)} %get-tuple-element.45), channel_id=1, source_target_pairs={{0,2},{1,3},{2,0},{3,1},{4,6},{5,7},{6,4},{7,5},{8,10},{9,11},{10,... | collective-permute-start | bytes 491528 | tf_op jit(solution)/shard_map/ppermute | solution.py:69
  33.3 5.4 %collective-permute-start.8 = (bf16[5,128,128]{2,1,0:T(8,128)(2,1)S(1)}, bf16[5,128,128]{2,1,0:T(8,128)(2,1)S(1)}, u32[]{:S(2)}, u32[]{:S(2)}) collective-permute-start(bf16[5,128,128]{2,1,0:T(8,128)(2,1)S(1)} %get-tuple-element.43), channel_id=1, source_target_pairs={{0,1},{1,2},{2,3},{3,0},{4,5},{5,6},{6,7},{7,4},{8,9},{9,10},{10,1... | collective-permute-start | bytes 491528 | tf_op jit(solution)/shard_map/ppermute | solution.py:69
  33.7 5.0 %collective-permute-start.9 = (bf16[5,128,128]{2,1,0:T(8,128)(2,1)S(1)}, bf16[5,128,128]{2,1,0:T(8,128)(2,1)S(1)}, u32[]{:S(2)}, u32[]{:S(2)}) collective-permute-start(bf16[5,128,128]{2,1,0:T(8,128)(2,1)S(1)} %get-tuple-element.44), channel_id=1, source_target_pairs={{0,3},{1,0},{2,1},{3,2},{4,7},{5,4},{6,5},{7,6},{8,11},{9,8},{10,9... | collective-permute-start | bytes 491528 | tf_op jit(solution)/shard_map/ppermute | solution.py:69
  39.0 7.8 %collective-permute-start.14 = (bf16[4,128,128]{2,1,0:T(8,128)(2,1)S(1)}, bf16[4,128,128]{2,1,0:T(8,128)(2,1)S(1)}, u32[]{:S(2)}, u32[]{:S(2)}) collective-permute-start(bf16[4,128,128]{2,1,0:T(8,128)(2,1)S(1)} %get-tuple-element.50), channel_id=1, source_target_pairs={{0,1},{1,2},{2,3},{3,4},{4,5},{5,6},{6,7},{7,8},{8,9},{9,10},{10,1... | collective-permute-start | bytes 393224 | tf_op jit(solution)/shard_map/ppermute | solution.py:69
  41.8 8.7 %collective-permute-start.11 = (bf16[5,64,128]{2,1,0:T(8,128)(2,1)S(1)}, bf16[5,64,128]{2,1,0:T(8,128)(2,1)S(1)}, u32[]{:S(2)}, u32[]{:S(2)}) collective-permute-start(bf16[5,64,128]{2,1,0:T(8,128)(2,1)S(1)} %get-tuple-element.47), channel_id=1, source_target_pairs={{0,32},{1,33},{2,34},{3,35},{4,36},{5,37},{6,38},{7,39},{8,40},{9,... | collective-permute-start | bytes 245768 | tf_op jit(solution)/shard_map/ppermute | solution.py:69
  43.4 8.3 %collective-permute-start.12 = (bf16[5,64,128]{2,1,0:T(8,128)(2,1)S(1)}, bf16[5,64,128]{2,1,0:T(8,128)(2,1)S(1)}, u32[]{:S(2)}, u32[]{:S(2)}) collective-permute-start(bf16[5,64,128]{2,1,0:T(8,128)(2,1)S(1)} %get-tuple-element.48), channel_id=1, source_target_pairs={{0,96},{1,97},{2,98},{3,99},{4,100},{5,101},{6,102},{7,103},{8,104... | collective-permute-start | bytes 245768 | tf_op jit(solution)/shard_map/ppermute | solution.py:69
  45.5 6.2 %collective-permute-start.13 = (bf16[5,64,128]{2,1,0:T(8,128)(2,1)S(1)}, bf16[5,64,128]{2,1,0:T(8,128)(2,1)S(1)}, u32[]{:S(2)}, u32[]{:S(2)}) collective-permute-start(bf16[5,64,128]{2,1,0:T(8,128)(2,1)S(1)} %get-tuple-element.49), channel_id=1, source_target_pairs={{0,64},{1,65},{2,66},{3,67},{4,68},{5,69},{6,70},{7,71},{8,72},{9,... | collective-permute-start | bytes 245768 | tf_op jit(solution)/shard_map/ppermute | solution.py:69
  46.9 5.4 %collective-permute-start.15 = (bf16[2,64,128]{2,1,0:T(8,128)(2,1)S(1)}, bf16[2,64,128]{2,1,0:T(8,128)(2,1)S(1)}, u32[]{:S(2)}, u32[]{:S(2)}) collective-permute-start(bf16[2,64,128]{2,1,0:T(8,128)(2,1)S(1)} %get-tuple-element.52), channel_id=1, source_target_pairs={{0,32},{1,33},{2,34},{3,35},{4,36},{5,37},{6,38},{7,39},{8,40},{9,... | collective-permute-start | bytes 98312 | tf_op jit(solution)/shard_map/ppermute | solution.py:69
  48.3 4.1 %collective-permute-start.16 = (bf16[2,64,128]{2,1,0:T(8,128)(2,1)S(1)}, bf16[2,64,128]{2,1,0:T(8,128)(2,1)S(1)}, u32[]{:S(2)}, u32[]{:S(2)}) collective-permute-start(bf16[2,64,128]{2,1,0:T(8,128)(2,1)S(1)} %get-tuple-element.53), channel_id=1, source_target_pairs={{0,96},{1,97},{2,98},{3,99},{4,100},{5,101},{6,102},{7,103},{8,104... | collective-permute-start | bytes 98312 | tf_op jit(solution)/shard_map/ppermute | solution.py:69
  50.5 4.3 %collective-permute-start.17 = (bf16[2,64,128]{2,1,0:T(8,128)(2,1)S(1)}, bf16[2,64,128]{2,1,0:T(8,128)(2,1)S(1)}, u32[]{:S(2)}, u32[]{:S(2)}) collective-permute-start(bf16[2,64,128]{2,1,0:T(8,128)(2,1)S(1)} %get-tuple-element.54), channel_id=1, source_target_pairs={{0,64},{1,65},{2,66},{3,67},{4,68},{5,69},{6,70},{7,71},{8,72},{9,... | collective-permute-start | bytes 98312 | tf_op jit(solution)/shard_map/ppermute | solution.py:69
  54.8 6.6 %collective-permute-start.18 = (f32[5,32,128]{2,1,0:T(8,128)S(1)}, f32[5,32,128]{2,1,0:T(8,128)S(1)}, u32[]{:S(2)}, u32[]{:S(2)}) collective-permute-start(f32[5,32,128]{2,1,0:T(8,128)S(1)} %get-tuple-element.56), channel_id=1, source_target_pairs={{0,16},{1,17},{2,18},{3,19},{4,20},{5,21},{6,22},{7,23},{8,24},{9,... | collective-permute-start | bytes 245768 | tf_op jit(solution)/shard_map/ppermute | solution.py:69

commit v4 on v3

--- a/solution.py
+++ b/solution.py
@@ -239,8 +239,8 @@
     return (mine.astype(F32) + other.astype(F32)).astype(BF16)
 
 
-def pack_kernel(own_ref, first_ref, second_ref, third_ref, kept_ref, turned_ref, *refs):
-    upper_refs, sums_ref, mirror_ref = refs[:3], refs[3], refs[4]
+def pack_kernel(own_ref, first_ref, second_ref, third_ref, upper_ref, lower_ref, *refs):
+    out_refs, sums_ref, turned_ref = refs[:3], refs[3], refs[4]
     z, core, _ = place_here()
     for index in range(BAND):
         total = own_ref[index]
@@ -248,30 +248,29 @@
             total = total + ref[index].astype(F32)
         sums_ref[index] = total
         if index > 0:
-            turned = total.T
-            turned_ref[index - 1] = turned.astype(BF16)
-            if index == 1:
-                mirror_ref[...] = turned
+            turned_ref[index] = total.T
     for mine in range(2):
         for row in range(2):
             for half in range(2):
                 target = row * 2 + half
                 rows = pl.ds(half * 64, 64)
-                upper = UPPER[(mine, row)]
+                upper, lower = UPPER[(mine, row)], LOWER[(mine, row)]
 
                 def value(index):
-                    return mirror_ref[rows] if index == MIRROR else sums_ref[index, rows]
+                    return turned_ref[1, rows] if index == MIRROR else sums_ref[index, rows]
 
                 @pl.when(jnp.logical_and(core == mine, z == target))
                 def _():
                     for place, index in enumerate(upper):
-                        kept_ref[place] = value(index)
+                        upper_ref[place] = value(index)
+                    for place in range(2):
+                        lower_ref[place] = turned_ref[lower[min(place, len(lower) - 1)], rows]
 
                 for step in range(1, 4):
 
                     @pl.when(jnp.logical_and(core == mine, (z + step) % 4 == target))
                     def _():
-                        out_ref = upper_refs[step - 1]
+                        out_ref = out_refs[step - 1]
                         for place in range(BAND):
                             out_ref[place] = jnp.zeros((64, BW), BF16)
                         for place, index in enumerate(upper):
@@ -280,81 +279,56 @@
                             out_ref[place] = high
                             if index == 0:
                                 out_ref[BAND - 1] = (whole - high.astype(F32)).astype(BF16)
+                        for place in range(2):
+                            turned = turned_ref[lower[min(place, len(lower) - 1)], rows]
+                            out_ref[BAND + place] = turned.astype(BF16)
 
 
 def pack(own, arrived):
-    kept = jax.ShapeDtypeStruct((BAND - 1, 64, BW), F32)
-    turned = jax.ShapeDtypeStruct((BAND - 1, BW, BW), BF16)
-    upper = jax.ShapeDtypeStruct((BAND, 64, BW), BF16)
+    upper = jax.ShapeDtypeStruct((BAND - 1, 64, BW), F32)
+    lower = jax.ShapeDtypeStruct((2, 64, BW), F32)
+    sent = jax.ShapeDtypeStruct((BAND + 2, 64, BW), BF16)
     return pl.pallas_call(
         pack_kernel,
         in_specs=[VMEM] * 4,
         out_specs=[VMEM] * 5,
-        out_shape=[kept, turned] + [upper] * 3,
-        scratch_shapes=[pltpu.VMEM((BAND, BW, BW), F32), pltpu.VMEM((BW, BW), F32)],
+        out_shape=[upper, lower] + [sent] * 3,
+        scratch_shapes=[pltpu.VMEM((BAND, BW, BW), F32), pltpu.VMEM((BAND, BW, BW), F32)],
         compiler_params=SMALL,
     )(own, *arrived)
 
 
-def lower_kernel(turned_ref, *out_refs):
+def split_kernel(upper_ref, lower_ref, *refs):
+    arrived, turned_ref, kept_ref, sent_ref = refs[:3], refs[3], refs[4], refs[5]
     z, core, _ = place_here()
-    for mine in range(2):
-        for row in range(2):
-            for half in range(2):
-                for step in range(4):
-
-                    @pl.when(jnp.logical_and(core == mine, (z + step) % 4 == row * 2 + half))
-                    def _():
-                        lower = LOWER[(mine, row)]
-                        for place in range(2):
-                            index = lower[min(place, len(lower) - 1)] - 1
-                            out_refs[step][place] = turned_ref[index, half * 64 : half * 64 + 64]
-
-
-def pack_lower(turned):
-    lower = jax.ShapeDtypeStruct((2, 64, BW), BF16)
-    return pl.pallas_call(
-        lower_kernel, in_specs=[VMEM], out_specs=[VMEM] * 4, out_shape=[lower] * 4, compiler_params=SMALL
-    )(turned)
-
-
-def split_kernel(own_ref, *refs):
-    upper_refs, lower_refs, kept_ref, sent_ref = refs[:3], refs[3:7], refs[7], refs[8]
-    z, core, _ = place_here()
+    for place in range(2):
+        total = lower_ref[place]
+        for source in arrived:
+            total = total + source[BAND + place].astype(F32)
+        turned_ref[place] = total
     for ref, part in ((kept_ref, core), (sent_ref, 1 - core)):
         rows = pl.ds(pl.multiple_of(part * 32, 32), 32)
-        for mine in range(2):
-            for row in range(2):
-
-                @pl.when(jnp.logical_and(core == mine, z // 2 == row))
-                def _():
-                    count = len(UPPER[(mine, row)])
-                    for place in range(count):
-                        total = own_ref[place, rows]
-                        for source in upper_refs:
-                            total = total + source[place, rows].astype(F32)
-                            if UPPER[(mine, row)][place] == 0:
-                                total = total + source[BAND - 1, rows].astype(F32)
-                        ref[place] = total
-                    for place in range(len(LOWER[(mine, row)])):
-                        first, second, third, fourth = (source[place, rows].astype(F32) for source in lower_refs)
-                        ref[count + place] = (first + second) + (third + fourth)
-                    for place in range(len(SLOTS[(mine, row)]), BAND):
-                        ref[place] = jnp.zeros((32, BW), F32)
-
-
-def split(own, upper, lower):
-    shape = jax.ShapeDtypeStruct((BAND, 32, BW), F32)
+        for place in range(BAND - 1):
+            total = upper_ref[place, rows]
+            for source in arrived:
+                total = total + source[place, rows].astype(F32)
+                if place == 0:
+                    total = total + source[BAND - 1, rows].astype(F32)
+            ref[place] = total
+
+
+def split(upper, lower, arrived):
+    half = jax.ShapeDtypeStruct((BAND - 1, 32, BW), F32)
     return pl.pallas_call(
         split_kernel,
-        in_specs=[VMEM] * 8,
-        out_specs=[VMEM] * 2,
-        out_shape=[shape] * 2,
+        in_specs=[VMEM] * 5,
+        out_specs=[VMEM] * 3,
+        out_shape=[jax.ShapeDtypeStruct(lower.shape, F32), half, half],
         compiler_params=SMALL,
-    )(own, *upper, *lower)
-
-
-def final_kernel(mask_ref, own_ref, other_ref, out_ref):
+    )(upper, lower, *arrived)
+
+
+def final_kernel(mask_ref, own_upper_ref, other_upper_ref, own_lower_ref, other_lower_ref, out_ref):
     z, core, _ = place_here()
     for row in range(2):
         for mine in range(2):
@@ -362,20 +336,26 @@
             @pl.when(jnp.logical_and(core == mine, z // 2 == row))
             def _():
                 for half in range(2):
-                    source = own_ref if half == mine else other_ref
+                    upper_ref = own_upper_ref if half == mine else other_upper_ref
+                    lower_ref = own_lower_ref if half == mine else other_lower_ref
+                    count = len(UPPER[(half, row)])
                     for place, slot in enumerate(SLOTS[(half, row)]):
+                        if place < count:
+                            value = upper_ref[place]
+                        else:
+                            value = lower_ref[place - count, mine * 32 : mine * 32 + 32]
                         columns = slice(slot * BW, (slot + 1) * BW)
-                        out_ref[:, columns] = source[place] * mask_ref[:, columns]
-
-
-def final(mask, own, other):
+                        out_ref[:, columns] = value * mask_ref[:, columns]
+
+
+def final(mask, *pieces):
     return pl.pallas_call(
         final_kernel,
-        in_specs=[VMEM] * 3,
+        in_specs=[VMEM] * 5,
         out_specs=VMEM,
         out_shape=jax.ShapeDtypeStruct(mask.shape, F32),
         compiler_params=SMALL,
-    )(mask, own, other)
+    )(mask, *pieces)
 
 
 def local(three_index, block_size, screen):
@@ -398,14 +378,12 @@
     sent3, arrived3 = passed(STEPS[2], mine, other)
     mine, theirs, mask = last_tiles(block_size, screen, held, arrived1, STEPS[3])
     own, *outgoing = first_total(mine, send(theirs, core_pairs()), [arrived1, arrived2, arrived3])
-    arrived = [send(outgoing[step - 1], plane_pairs(step, False)) for step in (1, 3, 2)]
-    own, turned, *outgoing = pack(own, arrived)
-    turned = send(turned, mirror_pairs())
-    upper = [send(outgoing[step - 1], z_pairs(step)) for step in (1, 3, 2)]
-    kept, *outgoing = pack_lower(turned)
-    lower = [kept] + [send(outgoing[step - 1], z_pairs(step)) for step in (1, 3, 2)]
-    own, theirs = split(own, upper, lower)
-    return final(mask, own, send(theirs, core_pairs()))
+    arrived = [send(outgoing[step - 1], plane_pairs(step, False)) for step in (2, 3, 1)]
+    upper, lower, *outgoing = pack(own, arrived)
+    arrived = [send(outgoing[step - 1], z_pairs(step)) for step in (2, 3, 1)]
+    lower, upper, theirs = split(upper, lower, arrived)
+    lower = send(lower, mirror_pairs())
+    return final(mask, upper, send(theirs, core_pairs()), lower, send(lower, core_pairs()))
 
 
 def solution(mesh):

time: 62.2 us -> 62.1 us (level)
  starting transfers between devices: 33.4 us -> 29 us
  waiting for transfers between devices: 9.92 us -> 14.3 us
    ppermute x19 -> x17, starting transfers between devices: 33.4 us -> 29 us  [send(): return lax.ppermute(value, AXES, pairs)]
    ppermute x19 -> x17, waiting for transfers between devices: 9.92 us -> 14.3 us  [send(): return lax.ppermute(value, AXES, pairs)]
  transfers between devices with their start and end apart: 19 -> 17, of which waited for: 8 -> 11; matrix products, arithmetic and copies ran while one was open for 1% -> 1% of each run, Pallas kernels for 17% -> 17%
where the time goes in v4:
time: 62.1 us; the launch traced here: 62 us
  starting transfers between devices  29 us (47%)
  Pallas kernels  18.1 us (29%)
  waiting for transfers between devices  14.3 us (23%)
    ppermute x17, starting transfers between devices, send(): return lax.ppermute(value, AXES, pairs)  29 us
    ppermute x17, waiting for transfers between devices, send(): return lax.ppermute(value, AXES, pairs)  14.3 us
    pallas_call x2, Pallas kernels, later_tiles(): pl.pallas_call(functools.partial(later_kernel, step=step), in_specs=[VMEM...  6.52 us
    pallas_call x1, Pallas kernels, first_tiles(): pl.pallas_call(functools.partial(first_kernel, step=step), in_specs=[ANYW...  6.24 us
    pallas_call x1, Pallas kernels, last_tiles(): pl.pallas_call(functools.partial(last_kernel, step=step, factor=factor),...  3.81 us
  transfers between devices with their start and end apart: 17, of which 11 were waited for; matrix products, arithmetic and copies ran while one was open for 1% of the time, Pallas kernels for 17%

profile of v4, /device:TPU:1, one launch (start us, length us, event | category | flops | bytes accessed | tf_op | source)
XLA Modules:
  0.0 62.0 jit_solution(13504198699764666442)
XLA Ops:
  0.0 6.2 %shard_map.37 = (bf16[4,5,128,128]{3,2,1,0:T(8,128)(2,1)S(1)}, bf16[4,5,128,128]{3,2,1,0:T(8,128)(2,1)S(1)}, bf16[1536,4096]{1,0:T(8,128)(2,1)S(1)}) custom-call(bf16[1536,4096]{1,0:T(8,128)(2,1)} %bitcast.3), custom_call_target="tpu_custom_call" | custom-call | flops 2617245696 | bytes 12582912 | tf_op jit(solution)/shard_map/pallas_call | solution.py:180
  6.2 1.5 %collective-permute-start = (bf16[4,5,128,128]{3,2,1,0:T(8,128)(2,1)S(1)}, bf16[4,5,128,128]{3,2,1,0:T(8,128)(2,1)S(1)}, u32[]{:S(2)}, u32[]{:S(2)}) collective-permute-start(bf16[4,5,128,128]{3,2,1,0:T(8,128)(2,1)S(1)} %get-tuple-element.30), channel_id=1, source_target_pairs={{0,16},{1,17},{2,18},{3,19},{4,20},{5,21},{6,22},{7,23},{8,24},{9,... | collective-permute-start | bytes 1966088 | tf_op jit(solution)/shard_map/ppermute | solution.py:69
  7.8 0.0 copy-done.1
  7.8 3.2 %shard_map.39 = (bf16[4,5,128,128]{3,2,1,0:T(8,128)(2,1)S(1)}, bf16[4,5,128,128]{3,2,1,0:T(8,128)(2,1)S(1)}) custom-call(bf16[1536,4096]{1,0:T(8,128)(2,1)S(1)} %get-tuple-element.28.flat_ref, s32[32]{0:T(128)S(1)} %copy-done.1), custom_call_target="tpu_custom_call" | custom-call | flops 2617245696 | tf_op jit(solution)/shard_map/pallas_call | solution.py:196
  11.0 0.1 collective-permute-start.3
  11.1 0.0 collective-permute-done
  11.1 0.2 add_convert_fusion.2
  11.3 2.9 %collective-permute-start.1 = (bf16[4,5,128,128]{3,2,1,0:T(8,128)(2,1)S(1)}, bf16[4,5,128,128]{3,2,1,0:T(8,128)(2,1)S(1)}, u32[]{:S(2)}, u32[]{:S(2)}) collective-permute-start(bf16[4,5,128,128]{3,2,1,0:T(8,128)(2,1)S(1)} %add_convert_fusion.2), channel_id=1, source_target_pairs={{0,8},{1,9},{2,10},{3,11},{4,12},{5,13},{6,14},{7,15},{8,0},{9,1},... | collective-permute-start | bytes 1966088 | tf_op jit(solution)/shard_map/ppermute | solution.py:69
  14.2 0.0 collective-permute-done.3
  14.2 0.2 add_convert_fusion.1.after_ref
  14.4 3.3 %shard_map.40 = (bf16[4,5,128,128]{3,2,1,0:T(8,128)(2,1)S(1)}, bf16[2,5,128,128]{3,2,1,0:T(8,128)(2,1)S(1)}, bf16[2,5,128,128]{3,2,1,0:T(8,128)(2,1)S(1)}) custom-call(bf16[1536,4096]{1,0:T(8,128)(2,1)S(1)} %get-tuple-element.28.flat_ref, bf16[4,5,128,128]{3,2,1,0:T(8,128)(2,1)S(1)} %add_convert_fusion.1.after_ref), custom_call_target="tpu_custom_call" | custom-call | flops 2617245696 | tf_op jit(solution)/shard_map/pallas_call | solution.py:196
  17.7 0.0 copy-start
  17.7 1.0 %collective-permute-start.5 = (bf16[2,5,128,128]{3,2,1,0:T(8,128)(2,1)S(1)}, bf16[2,5,128,128]{3,2,1,0:T(8,128)(2,1)S(1)}, u32[]{:S(2)}, u32[]{:S(2)}) collective-permute-start(bf16[2,5,128,128]{3,2,1,0:T(8,128)(2,1)S(1)} %get-tuple-element.37), channel_id=1, source_target_pairs={{0,16},{1,17},{2,18},{3,19},{4,20},{5,21},{6,22},{7,23},{8,24},{9,... | collective-permute-start | bytes 983048 | tf_op jit(solution)/shard_map/ppermute | solution.py:69
  18.7 0.1 collective-permute-start.6
  18.8 1.2 %collective-permute-start.4 = (bf16[4,5,128,128]{3,2,1,0:T(8,128)(2,1)S(1)}, bf16[4,5,128,128]{3,2,1,0:T(8,128)(2,1)S(1)}, u32[]{:S(2)}, u32[]{:S(2)}) collective-permute-start(bf16[4,5,128,128]{3,2,1,0:T(8,128)(2,1)S(1)} %add_convert_fusion.1.after_ref), channel_id=1, source_target_pairs={{0,4},{1,5},{2,6},{3,7},{4,8},{5,9},{6,10},{7,11},{8,12},{9,13},{1... | collective-permute-start | bytes 1966088 | tf_op jit(solution)/shard_map/ppermute | solution.py:69
  20.0 0.0 collective-permute-done.5
  20.0 0.5 collective-permute-done.6
  20.4 0.2 add_convert_fusion
  20.6 2.5 %collective-permute-start.7 = (bf16[4,5,128,128]{3,2,1,0:T(8,128)(2,1)S(1)}, bf16[4,5,128,128]{3,2,1,0:T(8,128)(2,1)S(1)}, u32[]{:S(2)}, u32[]{:S(2)}) collective-permute-start(bf16[4,5,128,128]{3,2,1,0:T(8,128)(2,1)S(1)} %add_convert_fusion), channel_id=1, source_target_pairs={{0,12},{1,13},{2,14},{3,15},{4,0},{5,1},{6,2},{7,3},{8,4},{9,5},{1... | collective-permute-start | bytes 1966088 | tf_op jit(solution)/shard_map/ppermute | solution.py:69
  23.1 0.0 collective-permute-done.1.after_ref.refs_2_
  23.1 0.0 copy-done
  23.1 3.8 %shard_map.38 = (bf16[4,5,128,128]{3,2,1,0:T(8,128)(2,1)S(1)}, bf16[4,5,128,128]{3,2,1,0:T(8,128)(2,1)S(1)}, f32[32,1152]{1,0:T(8,128)S(1)}) custom-call(s32[32]{0:T(128)S(1)} %copy-done.1, s32[5,32]{1,0:T(8,128)S(1)} %bitcast.2, bf16[1536,4096]{1,0:T(8,128)(2,1)S(1)} %get-tuple-element.28.flat_ref, ...), custom_call_target="tpu_custom_call" | custom-call | flops 2617245696 | tf_op jit(solution)/shard_map/pallas_call | solution.py:208
  26.9 0.9 %collective-permute-start.2 = (bf16[4,5,128,128]{3,2,1,0:T(8,128)(2,1)S(1)}, bf16[4,5,128,128]{3,2,1,0:T(8,128)(2,1)S(1)}, u32[]{:S(2)}, u32[]{:S(2)}) collective-permute-start(bf16[4,5,128,128]{3,2,1,0:T(8,128)(2,1)S(1)} %get-tuple-element.33), channel_id=1, source_target_pairs={{0,16},{1,17},{2,18},{3,19},{4,20},{5,21},{6,22},{7,23},{8,24},{9,... | collective-permute-start | bytes 1966088 | tf_op jit(solution)/shard_map/ppermute | solution.py:69
  27.9 1.9 %collective-permute-done.4.refs_3_ = bf16[4,5,128,128]{3,2,1,0:T(8,128)(2,1)S(1)} collective-permute-done((bf16[4,5,128,128]{3,2,1,0:T(8,128)(2,1)S(1)}, bf16[4,5,128,128]{3,2,1,0:T(8,128)(2,1)S(1)}, u32[]{:S(2)}, u32[]{:S(2)}) %collective-permute-start.4) | collective-permute-done | bytes 655392 | tf_op jit(solution)/shard_map/ppermute | solution.py:69
  29.7 0.9 %collective-permute-done.7.refs_4_ = bf16[4,5,128,128]{3,2,1,0:T(8,128)(2,1)S(1)} collective-permute-done((bf16[4,5,128,128]{3,2,1,0:T(8,128)(2,1)S(1)}, bf16[4,5,128,128]{3,2,1,0:T(8,128)(2,1)S(1)}, u32[]{:S(2)}, u32[]{:S(2)}) %collective-permute-start.7) | collective-permute-done | bytes 655392 | tf_op jit(solution)/shard_map/ppermute | solution.py:69
  30.7 0.0 collective-permute-done.2.refs_1_
  30.7 0.4 shard_map.41
  31.1 0.6 collective-permute-start.10
  31.6 2.6 %collective-permute-start.8 = (bf16[5,128,128]{2,1,0:T(8,128)(2,1)S(1)}, bf16[5,128,128]{2,1,0:T(8,128)(2,1)S(1)}, u32[]{:S(2)}, u32[]{:S(2)}) collective-permute-start(bf16[5,128,128]{2,1,0:T(8,128)(2,1)S(1)} %get-tuple-element.40), channel_id=1, source_target_pairs={{0,2},{1,3},{2,0},{3,1},{4,6},{5,7},{6,4},{7,5},{8,10},{9,11},{10,... | collective-permute-start | bytes 491528 | tf_op jit(solution)/shard_map/ppermute | solution.py:69
  34.3 1.1 %collective-permute-start.9 = (bf16[5,128,128]{2,1,0:T(8,128)(2,1)S(1)}, bf16[5,128,128]{2,1,0:T(8,128)(2,1)S(1)}, u32[]{:S(2)}, u32[]{:S(2)}) collective-permute-start(bf16[5,128,128]{2,1,0:T(8,128)(2,1)S(1)} %get-tuple-element.41), channel_id=1, source_target_pairs={{0,3},{1,0},{2,1},{3,2},{4,7},{5,4},{6,5},{7,6},{8,11},{9,8},{10,9... | collective-permute-start | bytes 491528 | tf_op jit(solution)/shard_map/ppermute | solution.py:69
  35.3 1.5 %collective-permute-done.10.third_ref = bf16[5,128,128]{2,1,0:T(8,128)(2,1)S(1)} collective-permute-done((bf16[5,128,128]{2,1,0:T(8,128)(2,1)S(1)}, bf16[5,128,128]{2,1,0:T(8,128)(2,1)S(1)}, u32[]{:S(2)}, u32[]{:S(2)}) %collective-permute-start.10) | collective-permute-done | bytes 163872 | tf_op jit(solution)/shard_map/ppermute | solution.py:69
  36.8 1.9 %collective-permute-done.8.first_ref = bf16[5,128,128]{2,1,0:T(8,128)(2,1)S(1)} collective-permute-done((bf16[5,128,128]{2,1,0:T(8,128)(2,1)S(1)}, bf16[5,128,128]{2,1,0:T(8,128)(2,1)S(1)}, u32[]{:S(2)}, u32[]{:S(2)}) %collective-permute-start.8) | collective-permute-done | bytes 163872 | tf_op jit(solution)/shard_map/ppermute | solution.py:69
  38.7 0.1 collective-permute-done.9.second_ref
  38.8 0.4 shard_map.42
  39.2 3.7 %collective-permute-start.11 = (bf16[7,64,128]{2,1,0:T(8,128)(2,1)S(1)}, bf16[7,64,128]{2,1,0:T(8,128)(2,1)S(1)}, u32[]{:S(2)}, u32[]{:S(2)}) collective-permute-start(bf16[7,64,128]{2,1,0:T(8,128)(2,1)S(1)} %get-tuple-element.45), channel_id=1, source_target_pairs={{0,64},{1,65},{2,66},{3,67},{4,68},{5,69},{6,70},{7,71},{8,72},{9,... | collective-permute-start | bytes 344072 | tf_op jit(solution)/shard_map/ppermute | solution.py:69
  42.9 0.4 collective-permute-start.12
  43.3 1.0 %collective-permute-start.13 = (bf16[7,64,128]{2,1,0:T(8,128)(2,1)S(1)}, bf16[7,64,128]{2,1,0:T(8,128)(2,1)S(1)}, u32[]{:S(2)}, u32[]{:S(2)}) collective-permute-start(bf16[7,64,128]{2,1,0:T(8,128)(2,1)S(1)} %get-tuple-element.47), channel_id=1, source_target_pairs={{0,32},{1,33},{2,34},{3,35},{4,36},{5,37},{6,38},{7,39},{8,40},{9,... | collective-permute-start | bytes 344072 | tf_op jit(solution)/shard_map/ppermute | solution.py:69
  44.3 0.7 %collective-permute-done.11.refs_0_ = bf16[7,64,128]{2,1,0:T(8,128)(2,1)S(1)} collective-permute-done((bf16[7,64,128]{2,1,0:T(8,128)(2,1)S(1)}, bf16[7,64,128]{2,1,0:T(8,128)(2,1)S(1)}, u32[]{:S(2)}, u32[]{:S(2)}) %collective-permute-start.11) | collective-permute-done | bytes 114720 | tf_op jit(solution)/shard_map/ppermute | solution.py:69
  45.1 2.3 %collective-permute-done.12.refs_1_ = bf16[7,64,128]{2,1,0:T(8,128)(2,1)S(1)} collective-permute-done((bf16[7,64,128]{2,1,0:T(8,128)(2,1)S(1)}, bf16[7,64,128]{2,1,0:T(8,128)(2,1)S(1)}, u32[]{:S(2)}, u32[]{:S(2)}) %collective-permute-start.12) | collective-permute-done | bytes 114720 | tf_op jit(solution)/shard_map/ppermute | solution.py:69
  47.4 1.9 %collective-permute-done.13.refs_2_ = bf16[7,64,128]{2,1,0:T(8,128)(2,1)S(1)} collective-permute-done((bf16[7,64,128]{2,1,0:T(8,128)(2,1)S(1)}, bf16[7,64,128]{2,1,0:T(8,128)(2,1)S(1)}, u32[]{:S(2)}, u32[]{:S(2)}) %collective-permute-start.13) | collective-permute-done | bytes 114720 | tf_op jit(solution)/shard_map/ppermute | solution.py:69
  49.3 0.1 shard_map.43
  49.3 2.7 %collective-permute-start.15 = (f32[2,64,128]{2,1,0:T(8,128)S(1)}, f32[2,64,128]{2,1,0:T(8,128)S(1)}, u32[]{:S(2)}, u32[]{:S(2)}) collective-permute-start(f32[2,64,128]{2,1,0:T(8,128)S(1)} %get-tuple-element.50), channel_id=1, source_target_pairs={{0,1},{1,2},{2,3},{3,4},{4,5},{5,6},{6,7},{7,8},{8,9},{9,10},{10,1... | collective-permute-start | bytes 196616 | tf_op jit(solution)/shard_map/ppermute | solution.py:69
  52.1 2.4 %collective-permute-start.14 = (f32[4,32,128]{2,1,0:T(8,128)S(1)}, f32[4,32,128]{2,1,0:T(8,128)S(1)}, u32[]{:S(2)}, u32[]{:S(2)}) collective-permute-start(f32[4,32,128]{2,1,0:T(8,128)S(1)} %get-tuple-element.49), channel_id=1, source_target_pairs={{0,16},{1,17},{2,18},{3,19},{4,20},{5,21},{6,22},{7,23},{8,24},{9,... | collective-permute-start | bytes 196616 | tf_op jit(solution)/shard_map/ppermute | solution.py:69
  54.4 1.7 %collective-permute-done.15.own_lower_ref = f32[2,64,128]{2,1,0:T(8,128)S(1)} collective-permute-done((f32[2,64,128]{2,1,0:T(8,128)S(1)}, f32[2,64,128]{2,1,0:T(8,128)S(1)}, u32[]{:S(2)}, u32[]{:S(2)}) %collective-permute-start.15) | collective-permute-done | bytes 65568 | tf_op jit(solution)/shard_map/ppermute | solution.py:69
  56.1 4.2 %collective-permute-start.16 = (f32[2,64,128]{2,1,0:T(8,128)S(1)}, f32[2,64,128]{2,1,0:T(8,128)S(1)}, u32[]{:S(2)}, u32[]{:S(2)}) collective-permute-start(f32[2,64,128]{2,1,0:T(8,128)S(1)} %collective-permute-done.15.own_lower_ref), channel_id=1, source_target_pairs={{0,16},{1,17},{2,18},{3,19},{4,20},{5,21},{6,22},{7,23},{8,24},{9,... | collective-permute-start | bytes 196616 | tf_op jit(solution)/shard_map/ppermute | solution.py:69
  60.4 0.0 collective-permute-done.14.other_upper_ref
  60.4 0.9 %collective-permute-done.16.other_lower_ref = f32[2,64,128]{2,1,0:T(8,128)S(1)} collective-permute-done((f32[2,64,128]{2,1,0:T(8,128)S(1)}, f32[2,64,128]{2,1,0:T(8,128)S(1)}, u32[]{:S(2)}, u32[]{:S(2)}) %collective-permute-start.16) | collective-permute-done | bytes 65568 | tf_op jit(solution)/shard_map/ppermute | solution.py:69
  61.3 0.7 %shard_map.44 = f32[32,1152]{1,0:T(8,128)} custom-call(f32[32,1152]{1,0:T(8,128)S(1)} %get-tuple-element.31.mask_ref, f32[4,32,128]{2,1,0:T(8,128)S(1)} %get-tuple-element.48.own_upper_ref, f32[4,32,128]{2,1,0:T(8,128)S(1)} %collective-permute-done.14.other_upper_ref, f32[2,64,128]{2,1,0:T(8,128)S(1)} %collective-permute-done.15.own_lower_ref, ...), custom_call_target="tpu_custom_call" | custom-call | tf_op jit(solution)/shard_map/pallas_call | solution.py:352
  (1 shorter events, 0.0 us)
Async XLA Ops:
  0.0 7.8 %copy-start.1 = (s32[32]{0:T(128)S(1)}, s32[32]{0:T(128)}, u32[]{:S(2)}) copy-start(s32[32]{0:T(128)} %after_ref.1) | copy-start | bytes 388
  6.2 4.9 %collective-permute-start = (bf16[4,5,128,128]{3,2,1,0:T(8,128)(2,1)S(1)}, bf16[4,5,128,128]{3,2,1,0:T(8,128)(2,1)S(1)}, u32[]{:S(2)}, u32[]{:S(2)}) collective-permute-start(bf16[4,5,128,128]{3,2,1,0:T(8,128)(2,1)S(1)} %get-tuple-element.30), channel_id=1, source_target_pairs={{0,16},{1,17},{2,18},{3,19},{4,20},{5,21},{6,22},{7,23},{8,24},{9,... | collective-permute-start | bytes 1966088 | tf_op jit(solution)/shard_map/ppermute | solution.py:69
  11.0 3.2 %collective-permute-start.3 = (bf16[4,5,128,128]{3,2,1,0:T(8,128)(2,1)S(1)}, bf16[4,5,128,128]{3,2,1,0:T(8,128)(2,1)S(1)}, u32[]{:S(2)}, u32[]{:S(2)}) collective-permute-start(bf16[4,5,128,128]{3,2,1,0:T(8,128)(2,1)S(1)} %get-tuple-element.35), channel_id=1, source_target_pairs={{0,16},{1,17},{2,18},{3,19},{4,20},{5,21},{6,22},{7,23},{8,24},{9,... | collective-permute-start | bytes 1966088 | tf_op jit(solution)/shard_map/ppermute | solution.py:69
  11.3 11.8 %collective-permute-start.1 = (bf16[4,5,128,128]{3,2,1,0:T(8,128)(2,1)S(1)}, bf16[4,5,128,128]{3,2,1,0:T(8,128)(2,1)S(1)}, u32[]{:S(2)}, u32[]{:S(2)}) collective-permute-start(bf16[4,5,128,128]{3,2,1,0:T(8,128)(2,1)S(1)} %add_convert_fusion.2), channel_id=1, source_target_pairs={{0,8},{1,9},{2,10},{3,11},{4,12},{5,13},{6,14},{7,15},{8,0},{9,1},... | collective-permute-start | bytes 1966088 | tf_op jit(solution)/shard_map/ppermute | solution.py:69
  17.7 5.4 %copy-start = (s32[32,5]{0,1:T(8,128)S(1)}, s32[32,5]{0,1:T(8,128)}, u32[]{:S(2)}) copy-start(s32[32,5]{0,1:T(8,128)} %param.5) | copy-start | bytes 1924
  17.7 2.3 %collective-permute-start.5 = (bf16[2,5,128,128]{3,2,1,0:T(8,128)(2,1)S(1)}, bf16[2,5,128,128]{3,2,1,0:T(8,128)(2,1)S(1)}, u32[]{:S(2)}, u32[]{:S(2)}) collective-permute-start(bf16[2,5,128,128]{3,2,1,0:T(8,128)(2,1)S(1)} %get-tuple-element.37), channel_id=1, source_target_pairs={{0,16},{1,17},{2,18},{3,19},{4,20},{5,21},{6,22},{7,23},{8,24},{9,... | collective-permute-start | bytes 983048 | tf_op jit(solution)/shard_map/ppermute | solution.py:69
  18.7 1.7 %collective-permute-start.6 = (bf16[2,5,128,128]{3,2,1,0:T(8,128)(2,1)S(1)}, bf16[2,5,128,128]{3,2,1,0:T(8,128)(2,1)S(1)}, u32[]{:S(2)}, u32[]{:S(2)}) collective-permute-start(bf16[2,5,128,128]{3,2,1,0:T(8,128)(2,1)S(1)} %get-tuple-element.38), channel_id=1, source_target_pairs={{0,16},{1,17},{2,18},{3,19},{4,20},{5,21},{6,22},{7,23},{8,24},{9,... | collective-permute-start | bytes 983048 | tf_op jit(solution)/shard_map/ppermute | solution.py:69
  18.8 10.9 %collective-permute-start.4 = (bf16[4,5,128,128]{3,2,1,0:T(8,128)(2,1)S(1)}, bf16[4,5,128,128]{3,2,1,0:T(8,128)(2,1)S(1)}, u32[]{:S(2)}, u32[]{:S(2)}) collective-permute-start(bf16[4,5,128,128]{3,2,1,0:T(8,128)(2,1)S(1)} %add_convert_fusion.1.after_ref), channel_id=1, source_target_pairs={{0,4},{1,5},{2,6},{3,7},{4,8},{5,9},{6,10},{7,11},{8,12},{9,13},{1... | collective-permute-start | bytes 1966088 | tf_op jit(solution)/shard_map/ppermute | solution.py:69
  20.6 10.0 %collective-permute-start.7 = (bf16[4,5,128,128]{3,2,1,0:T(8,128)(2,1)S(1)}, bf16[4,5,128,128]{3,2,1,0:T(8,128)(2,1)S(1)}, u32[]{:S(2)}, u32[]{:S(2)}) collective-permute-start(bf16[4,5,128,128]{3,2,1,0:T(8,128)(2,1)S(1)} %add_convert_fusion), channel_id=1, source_target_pairs={{0,12},{1,13},{2,14},{3,15},{4,0},{5,1},{6,2},{7,3},{8,4},{9,5},{1... | collective-permute-start | bytes 1966088 | tf_op jit(solution)/shard_map/ppermute | solution.py:69
  26.9 3.7 %collective-permute-start.2 = (bf16[4,5,128,128]{3,2,1,0:T(8,128)(2,1)S(1)}, bf16[4,5,128,128]{3,2,1,0:T(8,128)(2,1)S(1)}, u32[]{:S(2)}, u32[]{:S(2)}) collective-permute-start(bf16[4,5,128,128]{3,2,1,0:T(8,128)(2,1)S(1)} %get-tuple-element.33), channel_id=1, source_target_pairs={{0,16},{1,17},{2,18},{3,19},{4,20},{5,21},{6,22},{7,23},{8,24},{9,... | collective-permute-start | bytes 1966088 | tf_op jit(solution)/shard_map/ppermute | solution.py:69
  31.1 5.7 %collective-permute-start.10 = (bf16[5,128,128]{2,1,0:T(8,128)(2,1)S(1)}, bf16[5,128,128]{2,1,0:T(8,128)(2,1)S(1)}, u32[]{:S(2)}, u32[]{:S(2)}) collective-permute-start(bf16[5,128,128]{2,1,0:T(8,128)(2,1)S(1)} %get-tuple-element.42), channel_id=1, source_target_pairs={{0,1},{1,2},{2,3},{3,0},{4,5},{5,6},{6,7},{7,4},{8,9},{9,10},{10,1... | collective-permute-start | bytes 491528 | tf_op jit(solution)/shard_map/ppermute | solution.py:69
  31.6 7.1 %collective-permute-start.8 = (bf16[5,128,128]{2,1,0:T(8,128)(2,1)S(1)}, bf16[5,128,128]{2,1,0:T(8,128)(2,1)S(1)}, u32[]{:S(2)}, u32[]{:S(2)}) collective-permute-start(bf16[5,128,128]{2,1,0:T(8,128)(2,1)S(1)} %get-tuple-element.40), channel_id=1, source_target_pairs={{0,2},{1,3},{2,0},{3,1},{4,6},{5,7},{6,4},{7,5},{8,10},{9,11},{10,... | collective-permute-start | bytes 491528 | tf_op jit(solution)/shard_map/ppermute | solution.py:69
  34.3 4.6 %collective-permute-start.9 = (bf16[5,128,128]{2,1,0:T(8,128)(2,1)S(1)}, bf16[5,128,128]{2,1,0:T(8,128)(2,1)S(1)}, u32[]{:S(2)}, u32[]{:S(2)}) collective-permute-start(bf16[5,128,128]{2,1,0:T(8,128)(2,1)S(1)} %get-tuple-element.41), channel_id=1, source_target_pairs={{0,3},{1,0},{2,1},{3,2},{4,7},{5,4},{6,5},{7,6},{8,11},{9,8},{10,9... | collective-permute-start | bytes 491528 | tf_op jit(solution)/shard_map/ppermute | solution.py:69
  39.2 5.9 %collective-permute-start.11 = (bf16[7,64,128]{2,1,0:T(8,128)(2,1)S(1)}, bf16[7,64,128]{2,1,0:T(8,128)(2,1)S(1)}, u32[]{:S(2)}, u32[]{:S(2)}) collective-permute-start(bf16[7,64,128]{2,1,0:T(8,128)(2,1)S(1)} %get-tuple-element.45), channel_id=1, source_target_pairs={{0,64},{1,65},{2,66},{3,67},{4,68},{5,69},{6,70},{7,71},{8,72},{9,... | collective-permute-start | bytes 344072 | tf_op jit(solution)/shard_map/ppermute | solution.py:69
  42.9 4.5 %collective-permute-start.12 = (bf16[7,64,128]{2,1,0:T(8,128)(2,1)S(1)}, bf16[7,64,128]{2,1,0:T(8,128)(2,1)S(1)}, u32[]{:S(2)}, u32[]{:S(2)}) collective-permute-start(bf16[7,64,128]{2,1,0:T(8,128)(2,1)S(1)} %get-tuple-element.46), channel_id=1, source_target_pairs={{0,96},{1,97},{2,98},{3,99},{4,100},{5,101},{6,102},{7,103},{8,104... | collective-permute-start | bytes 344072 | tf_op jit(solution)/shard_map/ppermute | solution.py:69
  43.3 6.0 %collective-permute-start.13 = (bf16[7,64,128]{2,1,0:T(8,128)(2,1)S(1)}, bf16[7,64,128]{2,1,0:T(8,128)(2,1)S(1)}, u32[]{:S(2)}, u32[]{:S(2)}) collective-permute-start(bf16[7,64,128]{2,1,0:T(8,128)(2,1)S(1)} %get-tuple-element.47), channel_id=1, source_target_pairs={{0,32},{1,33},{2,34},{3,35},{4,36},{5,37},{6,38},{7,39},{8,40},{9,... | collective-permute-start | bytes 344072 | tf_op jit(solution)/shard_map/ppermute | solution.py:69
  49.3 6.8 %collective-permute-start.15 = (f32[2,64,128]{2,1,0:T(8,128)S(1)}, f32[2,64,128]{2,1,0:T(8,128)S(1)}, u32[]{:S(2)}, u32[]{:S(2)}) collective-permute-start(f32[2,64,128]{2,1,0:T(8,128)S(1)} %get-tuple-element.50), channel_id=1, source_target_pairs={{0,1},{1,2},{2,3},{3,4},{4,5},{5,6},{6,7},{7,8},{8,9},{9,10},{10,1... | collective-permute-start | bytes 196616 | tf_op jit(solution)/shard_map/ppermute | solution.py:69
  52.1 8.3 %collective-permute-start.14 = (f32[4,32,128]{2,1,0:T(8,128)S(1)}, f32[4,32,128]{2,1,0:T(8,128)S(1)}, u32[]{:S(2)}, u32[]{:S(2)}) collective-permute-start(f32[4,32,128]{2,1,0:T(8,128)S(1)} %get-tuple-element.49), channel_id=1, source_target_pairs={{0,16},{1,17},{2,18},{3,19},{4,20},{5,21},{6,22},{7,23},{8,24},{9,... | collective-permute-start | bytes 196616 | tf_op jit(solution)/shard_map/ppermute | solution.py:69
  56.1 5.1 %collective-permute-start.16 = (f32[2,64,128]{2,1,0:T(8,128)S(1)}, f32[2,64,128]{2,1,0:T(8,128)S(1)}, u32[]{:S(2)}, u32[]{:S(2)}) collective-permute-start(f32[2,64,128]{2,1,0:T(8,128)S(1)} %collective-permute-done.15.own_lower_ref), channel_id=1, source_target_pairs={{0,16},{1,17},{2,18},{3,19},{4,20},{5,21},{6,22},{7,23},{8,24},{9,... | collective-permute-start | bytes 196616 | tf_op jit(solution)/shard_map/ppermute | solution.py:69

commit v5 on v4

--- a/solution.py
+++ b/solution.py
@@ -28,6 +28,7 @@
 LOWER = {(0, 0): (1, 3), (1, 0): (2, 3), (0, 1): (2, 4), (1, 1): (4,)}
 SLOTS = {(0, 0): (4, 6, 7, 2, 3), (1, 0): (5, 8, 0, 1), (0, 1): (5, 6, 1, 2), (1, 1): (4, 7, 8, 3, 0)}
 SLOT_COUNT = 2 * BAND - 1
+LOWER_PLACES = (BAND, BAND - 2)
 STEPS = (2, 1, 3, 0)
 
 
@@ -261,8 +262,8 @@
 
                 @pl.when(jnp.logical_and(core == mine, z == target))
                 def _():
-                    for place, index in enumerate(upper):
-                        upper_ref[place] = value(index)
+                    for place in range(BAND - 1):
+                        upper_ref[place] = value(upper[place]) if place < len(upper) else jnp.zeros((64, BW), F32)
                     for place in range(2):
                         lower_ref[place] = turned_ref[lower[min(place, len(lower) - 1)], rows]
 
@@ -271,7 +272,7 @@
                     @pl.when(jnp.logical_and(core == mine, (z + step) % 4 == target))
                     def _():
                         out_ref = out_refs[step - 1]
-                        for place in range(BAND):
+                        for place in range(BAND + 1):
                             out_ref[place] = jnp.zeros((64, BW), BF16)
                         for place, index in enumerate(upper):
                             whole = value(index)
@@ -279,15 +280,14 @@
                             out_ref[place] = high
                             if index == 0:
                                 out_ref[BAND - 1] = (whole - high.astype(F32)).astype(BF16)
-                        for place in range(2):
-                            turned = turned_ref[lower[min(place, len(lower) - 1)], rows]
-                            out_ref[BAND + place] = turned.astype(BF16)
+                        for place, index in zip(LOWER_PLACES, lower):
+                            out_ref[place] = turned_ref[index, rows].astype(BF16)
 
 
 def pack(own, arrived):
     upper = jax.ShapeDtypeStruct((BAND - 1, 64, BW), F32)
     lower = jax.ShapeDtypeStruct((2, 64, BW), F32)
-    sent = jax.ShapeDtypeStruct((BAND + 2, 64, BW), BF16)
+    sent = jax.ShapeDtypeStruct((BAND + 1, 64, BW), BF16)
     return pl.pallas_call(
         pack_kernel,
         in_specs=[VMEM] * 4,
@@ -304,7 +304,7 @@
     for place in range(2):
         total = lower_ref[place]
         for source in arrived:
-            total = total + source[BAND + place].astype(F32)
+            total = total + source[LOWER_PLACES[place]].astype(F32)
         turned_ref[place] = total
     for ref, part in ((kept_ref, core), (sent_ref, 1 - core)):
         rows = pl.ds(pl.multiple_of(part * 32, 32), 32)
@@ -380,7 +380,7 @@
     own, *outgoing = first_total(mine, send(theirs, core_pairs()), [arrived1, arrived2, arrived3])
     arrived = [send(outgoing[step - 1], plane_pairs(step, False)) for step in (2, 3, 1)]
     upper, lower, *outgoing = pack(own, arrived)
-    arrived = [send(outgoing[step - 1], z_pairs(step)) for step in (2, 3, 1)]
+    arrived = [send(outgoing[step - 1], z_pairs(step)) for step in (1, 3, 2)]
     lower, upper, theirs = split(upper, lower, arrived)
     lower = send(lower, mirror_pairs())
     return final(mask, upper, send(theirs, core_pairs()), lower, send(lower, core_pairs()))

time: 62.1 us -> 61.7 us (level)
  waiting for transfers between devices: 14.3 us -> 12.5 us
  starting transfers between devices: 29 us -> 30.4 us
    ppermute x17, waiting for transfers between devices: 14.3 us -> 12.5 us  [send(): return lax.ppermute(value, AXES, pairs)]
    ppermute x17, starting transfers between devices: 29 us -> 30.4 us  [send(): return lax.ppermute(value, AXES, pairs)]
  transfers between devices with their start and end apart: 17 -> 17, of which waited for: 11 -> 10; matrix products, arithmetic and copies ran while one was open for 1% -> 1% of each run, Pallas kernels for 17% -> 17%
where the time goes in v5:
time: 61.7 us; the launch traced here: 61.6 us
  starting transfers between devices  30.4 us (49%)
  Pallas kernels  18.1 us (29%)
  waiting for transfers between devices  12.5 us (20%)
    ppermute x17, starting transfers between devices, send(): return lax.ppermute(value, AXES, pairs)  30.4 us
    ppermute x17, waiting for transfers between devices, send(): return lax.ppermute(value, AXES, pairs)  12.5 us
    pallas_call x2, Pallas kernels, later_tiles(): pl.pallas_call(functools.partial(later_kernel, step=step), in_specs=[VMEM...  6.52 us
    pallas_call x1, Pallas kernels, first_tiles(): pl.pallas_call(functools.partial(first_kernel, step=step), in_specs=[ANYW...  6.24 us
    pallas_call x1, Pallas kernels, last_tiles(): pl.pallas_call(functools.partial(last_kernel, step=step, factor=factor),...  3.81 us
  transfers between devices with their start and end apart: 17, of which 10 were waited for; matrix products, arithmetic and copies ran while one was open for 1% of the time, Pallas kernels for 17%

profile of v5, /device:TPU:1, one launch (start us, length us, event | category | flops | bytes accessed | tf_op | source)
XLA Modules:
  0.0 61.6 jit_solution(5376715056705734056)
XLA Ops:
  0.0 6.2 %shard_map.37 = (bf16[4,5,128,128]{3,2,1,0:T(8,128)(2,1)S(1)}, bf16[4,5,128,128]{3,2,1,0:T(8,128)(2,1)S(1)}, bf16[1536,4096]{1,0:T(8,128)(2,1)S(1)}) custom-call(bf16[1536,4096]{1,0:T(8,128)(2,1)} %bitcast.3), custom_call_target="tpu_custom_call" | custom-call | flops 2617245696 | bytes 12582912 | tf_op jit(solution)/shard_map/pallas_call | solution.py:181
  6.2 1.5 %collective-permute-start = (bf16[4,5,128,128]{3,2,1,0:T(8,128)(2,1)S(1)}, bf16[4,5,128,128]{3,2,1,0:T(8,128)(2,1)S(1)}, u32[]{:S(2)}, u32[]{:S(2)}) collective-permute-start(bf16[4,5,128,128]{3,2,1,0:T(8,128)(2,1)S(1)} %get-tuple-element.30), channel_id=1, source_target_pairs={{0,16},{1,17},{2,18},{3,19},{4,20},{5,21},{6,22},{7,23},{8,24},{9,... | collective-permute-start | bytes 1966088 | tf_op jit(solution)/shard_map/ppermute | solution.py:70
  7.8 0.0 copy-done.1
  7.8 3.2 %shard_map.39 = (bf16[4,5,128,128]{3,2,1,0:T(8,128)(2,1)S(1)}, bf16[4,5,128,128]{3,2,1,0:T(8,128)(2,1)S(1)}) custom-call(bf16[1536,4096]{1,0:T(8,128)(2,1)S(1)} %get-tuple-element.28.flat_ref, s32[32]{0:T(128)S(1)} %copy-done.1), custom_call_target="tpu_custom_call" | custom-call | flops 2617245696 | tf_op jit(solution)/shard_map/pallas_call | solution.py:197
  11.0 0.1 collective-permute-start.3
  11.1 0.0 collective-permute-done
  11.1 0.2 add_convert_fusion.2
  11.3 2.9 %collective-permute-start.1 = (bf16[4,5,128,128]{3,2,1,0:T(8,128)(2,1)S(1)}, bf16[4,5,128,128]{3,2,1,0:T(8,128)(2,1)S(1)}, u32[]{:S(2)}, u32[]{:S(2)}) collective-permute-start(bf16[4,5,128,128]{3,2,1,0:T(8,128)(2,1)S(1)} %add_convert_fusion.2), channel_id=1, source_target_pairs={{0,8},{1,9},{2,10},{3,11},{4,12},{5,13},{6,14},{7,15},{8,0},{9,1},... | collective-permute-start | bytes 1966088 | tf_op jit(solution)/shard_map/ppermute | solution.py:70
  14.2 0.0 collective-permute-done.3
  14.2 0.2 add_convert_fusion.1.after_ref
  14.4 3.3 %shard_map.40 = (bf16[4,5,128,128]{3,2,1,0:T(8,128)(2,1)S(1)}, bf16[2,5,128,128]{3,2,1,0:T(8,128)(2,1)S(1)}, bf16[2,5,128,128]{3,2,1,0:T(8,128)(2,1)S(1)}) custom-call(bf16[1536,4096]{1,0:T(8,128)(2,1)S(1)} %get-tuple-element.28.flat_ref, bf16[4,5,128,128]{3,2,1,0:T(8,128)(2,1)S(1)} %add_convert_fusion.1.after_ref), custom_call_target="tpu_custom_call" | custom-call | flops 2617245696 | tf_op jit(solution)/shard_map/pallas_call | solution.py:197
  17.7 0.0 copy-start
  17.7 1.0 %collective-permute-start.5 = (bf16[2,5,128,128]{3,2,1,0:T(8,128)(2,1)S(1)}, bf16[2,5,128,128]{3,2,1,0:T(8,128)(2,1)S(1)}, u32[]{:S(2)}, u32[]{:S(2)}) collective-permute-start(bf16[2,5,128,128]{3,2,1,0:T(8,128)(2,1)S(1)} %get-tuple-element.37), channel_id=1, source_target_pairs={{0,16},{1,17},{2,18},{3,19},{4,20},{5,21},{6,22},{7,23},{8,24},{9,... | collective-permute-start | bytes 983048 | tf_op jit(solution)/shard_map/ppermute | solution.py:70
  18.7 0.1 collective-permute-start.6
  18.8 1.2 %collective-permute-start.4 = (bf16[4,5,128,128]{3,2,1,0:T(8,128)(2,1)S(1)}, bf16[4,5,128,128]{3,2,1,0:T(8,128)(2,1)S(1)}, u32[]{:S(2)}, u32[]{:S(2)}) collective-permute-start(bf16[4,5,128,128]{3,2,1,0:T(8,128)(2,1)S(1)} %add_convert_fusion.1.after_ref), channel_id=1, source_target_pairs={{0,4},{1,5},{2,6},{3,7},{4,8},{5,9},{6,10},{7,11},{8,12},{9,13},{1... | collective-permute-start | bytes 1966088 | tf_op jit(solution)/shard_map/ppermute | solution.py:70
  20.0 0.0 collective-permute-done.5
  20.0 0.5 collective-permute-done.6
  20.4 0.2 add_convert_fusion
  20.6 2.5 %collective-permute-start.7 = (bf16[4,5,128,128]{3,2,1,0:T(8,128)(2,1)S(1)}, bf16[4,5,128,128]{3,2,1,0:T(8,128)(2,1)S(1)}, u32[]{:S(2)}, u32[]{:S(2)}) collective-permute-start(bf16[4,5,128,128]{3,2,1,0:T(8,128)(2,1)S(1)} %add_convert_fusion), channel_id=1, source_target_pairs={{0,12},{1,13},{2,14},{3,15},{4,0},{5,1},{6,2},{7,3},{8,4},{9,5},{1... | collective-permute-start | bytes 1966088 | tf_op jit(solution)/shard_map/ppermute | solution.py:70
  23.1 0.0 collective-permute-done.1.after_ref.refs_2_
  23.1 0.0 copy-done
  23.1 3.8 %shard_map.38 = (bf16[4,5,128,128]{3,2,1,0:T(8,128)(2,1)S(1)}, bf16[4,5,128,128]{3,2,1,0:T(8,128)(2,1)S(1)}, f32[32,1152]{1,0:T(8,128)S(1)}) custom-call(s32[32]{0:T(128)S(1)} %copy-done.1, s32[5,32]{1,0:T(8,128)S(1)} %bitcast.2, bf16[1536,4096]{1,0:T(8,128)(2,1)S(1)} %get-tuple-element.28.flat_ref, ...), custom_call_target="tpu_custom_call" | custom-call | flops 2617245696 | tf_op jit(solution)/shard_map/pallas_call | solution.py:209
  26.9 0.9 %collective-permute-start.2 = (bf16[4,5,128,128]{3,2,1,0:T(8,128)(2,1)S(1)}, bf16[4,5,128,128]{3,2,1,0:T(8,128)(2,1)S(1)}, u32[]{:S(2)}, u32[]{:S(2)}) collective-permute-start(bf16[4,5,128,128]{3,2,1,0:T(8,128)(2,1)S(1)} %get-tuple-element.33), channel_id=1, source_target_pairs={{0,16},{1,17},{2,18},{3,19},{4,20},{5,21},{6,22},{7,23},{8,24},{9,... | collective-permute-start | bytes 1966088 | tf_op jit(solution)/shard_map/ppermute | solution.py:70
  27.9 1.9 %collective-permute-done.4.refs_3_ = bf16[4,5,128,128]{3,2,1,0:T(8,128)(2,1)S(1)} collective-permute-done((bf16[4,5,128,128]{3,2,1,0:T(8,128)(2,1)S(1)}, bf16[4,5,128,128]{3,2,1,0:T(8,128)(2,1)S(1)}, u32[]{:S(2)}, u32[]{:S(2)}) %collective-permute-start.4) | collective-permute-done | bytes 655392 | tf_op jit(solution)/shard_map/ppermute | solution.py:70
  29.7 0.9 %collective-permute-done.7.refs_4_ = bf16[4,5,128,128]{3,2,1,0:T(8,128)(2,1)S(1)} collective-permute-done((bf16[4,5,128,128]{3,2,1,0:T(8,128)(2,1)S(1)}, bf16[4,5,128,128]{3,2,1,0:T(8,128)(2,1)S(1)}, u32[]{:S(2)}, u32[]{:S(2)}) %collective-permute-start.7) | collective-permute-done | bytes 655392 | tf_op jit(solution)/shard_map/ppermute | solution.py:70
  30.7 0.0 collective-permute-done.2.refs_1_
  30.7 0.4 shard_map.41
  31.1 0.6 collective-permute-start.10
  31.6 2.6 %collective-permute-start.8 = (bf16[5,128,128]{2,1,0:T(8,128)(2,1)S(1)}, bf16[5,128,128]{2,1,0:T(8,128)(2,1)S(1)}, u32[]{:S(2)}, u32[]{:S(2)}) collective-permute-start(bf16[5,128,128]{2,1,0:T(8,128)(2,1)S(1)} %get-tuple-element.40), channel_id=1, source_target_pairs={{0,2},{1,3},{2,0},{3,1},{4,6},{5,7},{6,4},{7,5},{8,10},{9,11},{10,... | collective-permute-start | bytes 491528 | tf_op jit(solution)/shard_map/ppermute | solution.py:70
  34.3 1.1 %collective-permute-start.9 = (bf16[5,128,128]{2,1,0:T(8,128)(2,1)S(1)}, bf16[5,128,128]{2,1,0:T(8,128)(2,1)S(1)}, u32[]{:S(2)}, u32[]{:S(2)}) collective-permute-start(bf16[5,128,128]{2,1,0:T(8,128)(2,1)S(1)} %get-tuple-element.41), channel_id=1, source_target_pairs={{0,3},{1,0},{2,1},{3,2},{4,7},{5,4},{6,5},{7,6},{8,11},{9,8},{10,9... | collective-permute-start | bytes 491528 | tf_op jit(solution)/shard_map/ppermute | solution.py:70
  35.3 1.5 %collective-permute-done.10.third_ref = bf16[5,128,128]{2,1,0:T(8,128)(2,1)S(1)} collective-permute-done((bf16[5,128,128]{2,1,0:T(8,128)(2,1)S(1)}, bf16[5,128,128]{2,1,0:T(8,128)(2,1)S(1)}, u32[]{:S(2)}, u32[]{:S(2)}) %collective-permute-start.10) | collective-permute-done | bytes 163872 | tf_op jit(solution)/shard_map/ppermute | solution.py:70
  36.8 1.9 %collective-permute-done.8.first_ref = bf16[5,128,128]{2,1,0:T(8,128)(2,1)S(1)} collective-permute-done((bf16[5,128,128]{2,1,0:T(8,128)(2,1)S(1)}, bf16[5,128,128]{2,1,0:T(8,128)(2,1)S(1)}, u32[]{:S(2)}, u32[]{:S(2)}) %collective-permute-start.8) | collective-permute-done | bytes 163872 | tf_op jit(solution)/shard_map/ppermute | solution.py:70
  38.7 0.1 collective-permute-done.9.second_ref
  38.8 0.4 shard_map.42
  39.2 1.7 %collective-permute-start.11 = (bf16[6,64,128]{2,1,0:T(8,128)(2,1)S(1)}, bf16[6,64,128]{2,1,0:T(8,128)(2,1)S(1)}, u32[]{:S(2)}, u32[]{:S(2)}) collective-permute-start(bf16[6,64,128]{2,1,0:T(8,128)(2,1)S(1)} %get-tuple-element.45), channel_id=1, source_target_pairs={{0,32},{1,33},{2,34},{3,35},{4,36},{5,37},{6,38},{7,39},{8,40},{9,... | collective-permute-start | bytes 294920 | tf_op jit(solution)/shard_map/ppermute | solution.py:70
  40.9 2.2 %collective-permute-start.12 = (bf16[6,64,128]{2,1,0:T(8,128)(2,1)S(1)}, bf16[6,64,128]{2,1,0:T(8,128)(2,1)S(1)}, u32[]{:S(2)}, u32[]{:S(2)}) collective-permute-start(bf16[6,64,128]{2,1,0:T(8,128)(2,1)S(1)} %get-tuple-element.46), channel_id=1, source_target_pairs={{0,96},{1,97},{2,98},{3,99},{4,100},{5,101},{6,102},{7,103},{8,104... | collective-permute-start | bytes 294920 | tf_op jit(solution)/shard_map/ppermute | solution.py:70
  43.1 1.2 %collective-permute-start.13 = (bf16[6,64,128]{2,1,0:T(8,128)(2,1)S(1)}, bf16[6,64,128]{2,1,0:T(8,128)(2,1)S(1)}, u32[]{:S(2)}, u32[]{:S(2)}) collective-permute-start(bf16[6,64,128]{2,1,0:T(8,128)(2,1)S(1)} %get-tuple-element.47), channel_id=1, source_target_pairs={{0,64},{1,65},{2,66},{3,67},{4,68},{5,69},{6,70},{7,71},{8,72},{9,... | collective-permute-start | bytes 294920 | tf_op jit(solution)/shard_map/ppermute | solution.py:70
  44.3 0.7 %collective-permute-done.11.refs_0_ = bf16[6,64,128]{2,1,0:T(8,128)(2,1)S(1)} collective-permute-done((bf16[6,64,128]{2,1,0:T(8,128)(2,1)S(1)}, bf16[6,64,128]{2,1,0:T(8,128)(2,1)S(1)}, u32[]{:S(2)}, u32[]{:S(2)}) %collective-permute-start.11) | collective-permute-done | bytes 98336 | tf_op jit(solution)/shard_map/ppermute | solution.py:70
  45.0 0.0 collective-permute-done.12.refs_1_
  45.0 3.1 %collective-permute-done.13.refs_2_ = bf16[6,64,128]{2,1,0:T(8,128)(2,1)S(1)} collective-permute-done((bf16[6,64,128]{2,1,0:T(8,128)(2,1)S(1)}, bf16[6,64,128]{2,1,0:T(8,128)(2,1)S(1)}, u32[]{:S(2)}, u32[]{:S(2)}) %collective-permute-start.13) | collective-permute-done | bytes 98336 | tf_op jit(solution)/shard_map/ppermute | solution.py:70
  48.2 0.1 shard_map.43
  48.2 2.9 %collective-permute-start.15 = (f32[2,64,128]{2,1,0:T(8,128)S(1)}, f32[2,64,128]{2,1,0:T(8,128)S(1)}, u32[]{:S(2)}, u32[]{:S(2)}) collective-permute-start(f32[2,64,128]{2,1,0:T(8,128)S(1)} %get-tuple-element.50), channel_id=1, source_target_pairs={{0,1},{1,2},{2,3},{3,4},{4,5},{5,6},{6,7},{7,8},{8,9},{9,10},{10,1... | collective-permute-start | bytes 196616 | tf_op jit(solution)/shard_map/ppermute | solution.py:70
  51.1 2.9 %collective-permute-start.14 = (f32[4,32,128]{2,1,0:T(8,128)S(1)}, f32[4,32,128]{2,1,0:T(8,128)S(1)}, u32[]{:S(2)}, u32[]{:S(2)}) collective-permute-start(f32[4,32,128]{2,1,0:T(8,128)S(1)} %get-tuple-element.49), channel_id=1, source_target_pairs={{0,16},{1,17},{2,18},{3,19},{4,20},{5,21},{6,22},{7,23},{8,24},{9,... | collective-permute-start | bytes 196616 | tf_op jit(solution)/shard_map/ppermute | solution.py:70
  54.1 1.0 %collective-permute-done.15.own_lower_ref = f32[2,64,128]{2,1,0:T(8,128)S(1)} collective-permute-done((f32[2,64,128]{2,1,0:T(8,128)S(1)}, f32[2,64,128]{2,1,0:T(8,128)S(1)}, u32[]{:S(2)}, u32[]{:S(2)}) %collective-permute-start.15) | collective-permute-done | bytes 65568 | tf_op jit(solution)/shard_map/ppermute | solution.py:70
  55.0 5.0 %collective-permute-start.16 = (f32[2,64,128]{2,1,0:T(8,128)S(1)}, f32[2,64,128]{2,1,0:T(8,128)S(1)}, u32[]{:S(2)}, u32[]{:S(2)}) collective-permute-start(f32[2,64,128]{2,1,0:T(8,128)S(1)} %collective-permute-done.15.own_lower_ref), channel_id=1, source_target_pairs={{0,16},{1,17},{2,18},{3,19},{4,20},{5,21},{6,22},{7,23},{8,24},{9,... | collective-permute-start | bytes 196616 | tf_op jit(solution)/shard_map/ppermute | solution.py:70
  60.0 0.0 collective-permute-done.14.other_upper_ref
  60.0 0.9 %collective-permute-done.16.other_lower_ref = f32[2,64,128]{2,1,0:T(8,128)S(1)} collective-permute-done((f32[2,64,128]{2,1,0:T(8,128)S(1)}, f32[2,64,128]{2,1,0:T(8,128)S(1)}, u32[]{:S(2)}, u32[]{:S(2)}) %collective-permute-start.16) | collective-permute-done | bytes 65568 | tf_op jit(solution)/shard_map/ppermute | solution.py:70
  60.9 0.7 %shard_map.44 = f32[32,1152]{1,0:T(8,128)} custom-call(f32[32,1152]{1,0:T(8,128)S(1)} %get-tuple-element.31.mask_ref, f32[4,32,128]{2,1,0:T(8,128)S(1)} %get-tuple-element.48.own_upper_ref, f32[4,32,128]{2,1,0:T(8,128)S(1)} %collective-permute-done.14.other_upper_ref, f32[2,64,128]{2,1,0:T(8,128)S(1)} %collective-permute-done.15.own_lower_ref, ...), custom_call_target="tpu_custom_call" | custom-call | tf_op jit(solution)/shard_map/pallas_call | solution.py:352
  (1 shorter events, 0.0 us)
Async XLA Ops:
  0.0 7.8 %copy-start.1 = (s32[32]{0:T(128)S(1)}, s32[32]{0:T(128)}, u32[]{:S(2)}) copy-start(s32[32]{0:T(128)} %after_ref.1) | copy-start | bytes 388
  6.2 4.9 %collective-permute-start = (bf16[4,5,128,128]{3,2,1,0:T(8,128)(2,1)S(1)}, bf16[4,5,128,128]{3,2,1,0:T(8,128)(2,1)S(1)}, u32[]{:S(2)}, u32[]{:S(2)}) collective-permute-start(bf16[4,5,128,128]{3,2,1,0:T(8,128)(2,1)S(1)} %get-tuple-element.30), channel_id=1, source_target_pairs={{0,16},{1,17},{2,18},{3,19},{4,20},{5,21},{6,22},{7,23},{8,24},{9,... | collective-permute-start | bytes 1966088 | tf_op jit(solution)/shard_map/ppermute | solution.py:70
  11.0 3.2 %collective-permute-start.3 = (bf16[4,5,128,128]{3,2,1,0:T(8,128)(2,1)S(1)}, bf16[4,5,128,128]{3,2,1,0:T(8,128)(2,1)S(1)}, u32[]{:S(2)}, u32[]{:S(2)}) collective-permute-start(bf16[4,5,128,128]{3,2,1,0:T(8,128)(2,1)S(1)} %get-tuple-element.35), channel_id=1, source_target_pairs={{0,16},{1,17},{2,18},{3,19},{4,20},{5,21},{6,22},{7,23},{8,24},{9,... | collective-permute-start | bytes 1966088 | tf_op jit(solution)/shard_map/ppermute | solution.py:70
  11.3 11.8 %collective-permute-start.1 = (bf16[4,5,128,128]{3,2,1,0:T(8,128)(2,1)S(1)}, bf16[4,5,128,128]{3,2,1,0:T(8,128)(2,1)S(1)}, u32[]{:S(2)}, u32[]{:S(2)}) collective-permute-start(bf16[4,5,128,128]{3,2,1,0:T(8,128)(2,1)S(1)} %add_convert_fusion.2), channel_id=1, source_target_pairs={{0,8},{1,9},{2,10},{3,11},{4,12},{5,13},{6,14},{7,15},{8,0},{9,1},... | collective-permute-start | bytes 1966088 | tf_op jit(solution)/shard_map/ppermute | solution.py:70
  17.7 5.4 %copy-start = (s32[32,5]{0,1:T(8,128)S(1)}, s32[32,5]{0,1:T(8,128)}, u32[]{:S(2)}) copy-start(s32[32,5]{0,1:T(8,128)} %param.5) | copy-start | bytes 1924
  17.7 2.3 %collective-permute-start.5 = (bf16[2,5,128,128]{3,2,1,0:T(8,128)(2,1)S(1)}, bf16[2,5,128,128]{3,2,1,0:T(8,128)(2,1)S(1)}, u32[]{:S(2)}, u32[]{:S(2)}) collective-permute-start(bf16[2,5,128,128]{3,2,1,0:T(8,128)(2,1)S(1)} %get-tuple-element.37), channel_id=1, source_target_pairs={{0,16},{1,17},{2,18},{3,19},{4,20},{5,21},{6,22},{7,23},{8,24},{9,... | collective-permute-start | bytes 983048 | tf_op jit(solution)/shard_map/ppermute | solution.py:70
  18.7 1.7 %collective-permute-start.6 = (bf16[2,5,128,128]{3,2,1,0:T(8,128)(2,1)S(1)}, bf16[2,5,128,128]{3,2,1,0:T(8,128)(2,1)S(1)}, u32[]{:S(2)}, u32[]{:S(2)}) collective-permute-start(bf16[2,5,128,128]{3,2,1,0:T(8,128)(2,1)S(1)} %get-tuple-element.38), channel_id=1, source_target_pairs={{0,16},{1,17},{2,18},{3,19},{4,20},{5,21},{6,22},{7,23},{8,24},{9,... | collective-permute-start | bytes 983048 | tf_op jit(solution)/shard_map/ppermute | solution.py:70
  18.8 10.9 %collective-permute-start.4 = (bf16[4,5,128,128]{3,2,1,0:T(8,128)(2,1)S(1)}, bf16[4,5,128,128]{3,2,1,0:T(8,128)(2,1)S(1)}, u32[]{:S(2)}, u32[]{:S(2)}) collective-permute-start(bf16[4,5,128,128]{3,2,1,0:T(8,128)(2,1)S(1)} %add_convert_fusion.1.after_ref), channel_id=1, source_target_pairs={{0,4},{1,5},{2,6},{3,7},{4,8},{5,9},{6,10},{7,11},{8,12},{9,13},{1... | collective-permute-start | bytes 1966088 | tf_op jit(solution)/shard_map/ppermute | solution.py:70
  20.6 10.0 %collective-permute-start.7 = (bf16[4,5,128,128]{3,2,1,0:T(8,128)(2,1)S(1)}, bf16[4,5,128,128]{3,2,1,0:T(8,128)(2,1)S(1)}, u32[]{:S(2)}, u32[]{:S(2)}) collective-permute-start(bf16[4,5,128,128]{3,2,1,0:T(8,128)(2,1)S(1)} %add_convert_fusion), channel_id=1, source_target_pairs={{0,12},{1,13},{2,14},{3,15},{4,0},{5,1},{6,2},{7,3},{8,4},{9,5},{1... | collective-permute-start | bytes 1966088 | tf_op jit(solution)/shard_map/ppermute | solution.py:70
  26.9 3.7 %collective-permute-start.2 = (bf16[4,5,128,128]{3,2,1,0:T(8,128)(2,1)S(1)}, bf16[4,5,128,128]{3,2,1,0:T(8,128)(2,1)S(1)}, u32[]{:S(2)}, u32[]{:S(2)}) collective-permute-start(bf16[4,5,128,128]{3,2,1,0:T(8,128)(2,1)S(1)} %get-tuple-element.33), channel_id=1, source_target_pairs={{0,16},{1,17},{2,18},{3,19},{4,20},{5,21},{6,22},{7,23},{8,24},{9,... | collective-permute-start | bytes 1966088 | tf_op jit(solution)/shard_map/ppermute | solution.py:70
  31.1 5.7 %collective-permute-start.10 = (bf16[5,128,128]{2,1,0:T(8,128)(2,1)S(1)}, bf16[5,128,128]{2,1,0:T(8,128)(2,1)S(1)}, u32[]{:S(2)}, u32[]{:S(2)}) collective-permute-start(bf16[5,128,128]{2,1,0:T(8,128)(2,1)S(1)} %get-tuple-element.42), channel_id=1, source_target_pairs={{0,1},{1,2},{2,3},{3,0},{4,5},{5,6},{6,7},{7,4},{8,9},{9,10},{10,1... | collective-permute-start | bytes 491528 | tf_op jit(solution)/shard_map/ppermute | solution.py:70
  31.6 7.1 %collective-permute-start.8 = (bf16[5,128,128]{2,1,0:T(8,128)(2,1)S(1)}, bf16[5,128,128]{2,1,0:T(8,128)(2,1)S(1)}, u32[]{:S(2)}, u32[]{:S(2)}) collective-permute-start(bf16[5,128,128]{2,1,0:T(8,128)(2,1)S(1)} %get-tuple-element.40), channel_id=1, source_target_pairs={{0,2},{1,3},{2,0},{3,1},{4,6},{5,7},{6,4},{7,5},{8,10},{9,11},{10,... | collective-permute-start | bytes 491528 | tf_op jit(solution)/shard_map/ppermute | solution.py:70
  34.3 4.6 %collective-permute-start.9 = (bf16[5,128,128]{2,1,0:T(8,128)(2,1)S(1)}, bf16[5,128,128]{2,1,0:T(8,128)(2,1)S(1)}, u32[]{:S(2)}, u32[]{:S(2)}) collective-permute-start(bf16[5,128,128]{2,1,0:T(8,128)(2,1)S(1)} %get-tuple-element.41), channel_id=1, source_target_pairs={{0,3},{1,0},{2,1},{3,2},{4,7},{5,4},{6,5},{7,6},{8,11},{9,8},{10,9... | collective-permute-start | bytes 491528 | tf_op jit(solution)/shard_map/ppermute | solution.py:70
  39.2 5.8 %collective-permute-start.11 = (bf16[6,64,128]{2,1,0:T(8,128)(2,1)S(1)}, bf16[6,64,128]{2,1,0:T(8,128)(2,1)S(1)}, u32[]{:S(2)}, u32[]{:S(2)}) collective-permute-start(bf16[6,64,128]{2,1,0:T(8,128)(2,1)S(1)} %get-tuple-element.45), channel_id=1, source_target_pairs={{0,32},{1,33},{2,34},{3,35},{4,36},{5,37},{6,38},{7,39},{8,40},{9,... | collective-permute-start | bytes 294920 | tf_op jit(solution)/shard_map/ppermute | solution.py:70
  40.9 4.1 %collective-permute-start.12 = (bf16[6,64,128]{2,1,0:T(8,128)(2,1)S(1)}, bf16[6,64,128]{2,1,0:T(8,128)(2,1)S(1)}, u32[]{:S(2)}, u32[]{:S(2)}) collective-permute-start(bf16[6,64,128]{2,1,0:T(8,128)(2,1)S(1)} %get-tuple-element.46), channel_id=1, source_target_pairs={{0,96},{1,97},{2,98},{3,99},{4,100},{5,101},{6,102},{7,103},{8,104... | collective-permute-start | bytes 294920 | tf_op jit(solution)/shard_map/ppermute | solution.py:70
  43.1 5.1 %collective-permute-start.13 = (bf16[6,64,128]{2,1,0:T(8,128)(2,1)S(1)}, bf16[6,64,128]{2,1,0:T(8,128)(2,1)S(1)}, u32[]{:S(2)}, u32[]{:S(2)}) collective-permute-start(bf16[6,64,128]{2,1,0:T(8,128)(2,1)S(1)} %get-tuple-element.47), channel_id=1, source_target_pairs={{0,64},{1,65},{2,66},{3,67},{4,68},{5,69},{6,70},{7,71},{8,72},{9,... | collective-permute-start | bytes 294920 | tf_op jit(solution)/shard_map/ppermute | solution.py:70
  48.2 6.8 %collective-permute-start.15 = (f32[2,64,128]{2,1,0:T(8,128)S(1)}, f32[2,64,128]{2,1,0:T(8,128)S(1)}, u32[]{:S(2)}, u32[]{:S(2)}) collective-permute-start(f32[2,64,128]{2,1,0:T(8,128)S(1)} %get-tuple-element.50), channel_id=1, source_target_pairs={{0,1},{1,2},{2,3},{3,4},{4,5},{5,6},{6,7},{7,8},{8,9},{9,10},{10,1... | collective-permute-start | bytes 196616 | tf_op jit(solution)/shard_map/ppermute | solution.py:70
  51.1 8.9 %collective-permute-start.14 = (f32[4,32,128]{2,1,0:T(8,128)S(1)}, f32[4,32,128]{2,1,0:T(8,128)S(1)}, u32[]{:S(2)}, u32[]{:S(2)}) collective-permute-start(f32[4,32,128]{2,1,0:T(8,128)S(1)} %get-tuple-element.49), channel_id=1, source_target_pairs={{0,16},{1,17},{2,18},{3,19},{4,20},{5,21},{6,22},{7,23},{8,24},{9,... | collective-permute-start | bytes 196616 | tf_op jit(solution)/shard_map/ppermute | solution.py:70
  55.0 5.9 %collective-permute-start.16 = (f32[2,64,128]{2,1,0:T(8,128)S(1)}, f32[2,64,128]{2,1,0:T(8,128)S(1)}, u32[]{:S(2)}, u32[]{:S(2)}) collective-permute-start(f32[2,64,128]{2,1,0:T(8,128)S(1)} %collective-permute-done.15.own_lower_ref), channel_id=1, source_target_pairs={{0,16},{1,17},{2,18},{3,19},{4,20},{5,21},{6,22},{7,23},{8,24},{9,... | collective-permute-start | bytes 196616 | tf_op jit(solution)/shard_map/ppermute | solution.py:70

commit v6 on v5

--- a/solution.py
+++ b/solution.py
@@ -109,7 +109,7 @@
 
 
 def depth_parts(depth):
-    sizes = (depth // 3, depth // 3, depth // 6, depth // 6)
+    sizes = (depth // 2, depth // 3, depth // 6)
     return [pl.ds(sum(sizes[:index]), size) for index, size in enumerate(sizes)]
 
 
@@ -186,7 +186,7 @@
         scratch_shapes=[
             pltpu.VMEM((4, BW, BW), F32),
             pltpu.VMEM((4, 3, PAIR, PAIR), F32),
-            pltpu.SemaphoreType.DMA((4,)),
+            pltpu.SemaphoreType.DMA((3,)),
         ],
         compiler_params=pltpu.CompilerParams(vmem_limit_bytes=20 << 20),
         cost_estimate=cost(depth, flat.size * 2),

time: 61.7 us -> 62.2 us (level)
  no operation moved by 1% of the time
where the time goes in v6:
time: 62.2 us; the launch traced here: 62.1 us
  starting transfers between devices  30.4 us (49%)
  Pallas kernels  18.4 us (30%)
  waiting for transfers between devices  12.6 us (20%)
    ppermute x17, starting transfers between devices, send(): return lax.ppermute(value, AXES, pairs)  30.4 us
    ppermute x17, waiting for transfers between devices, send(): return lax.ppermute(value, AXES, pairs)  12.6 us
    pallas_call x1, Pallas kernels, first_tiles(): pl.pallas_call(functools.partial(first_kernel, step=step), in_specs=[ANYW...  6.57 us
    pallas_call x2, Pallas kernels, later_tiles(): pl.pallas_call(functools.partial(later_kernel, step=step), in_specs=[VMEM...  6.51 us
    pallas_call x1, Pallas kernels, last_tiles(): pl.pallas_call(functools.partial(last_kernel, step=step, factor=factor),...  3.82 us
  transfers between devices with their start and end apart: 17, of which 10 were waited for; matrix products, arithmetic and copies ran while one was open for 1% of the time, Pallas kernels for 17%

profile of v6, /device:TPU:1, one launch (start us, length us, event | category | flops | bytes accessed | tf_op | source)
XLA Modules:
  0.0 62.1 jit_solution(12316616253643526091)
XLA Ops:
  0.0 6.6 %shard_map.37 = (bf16[4,5,128,128]{3,2,1,0:T(8,128)(2,1)S(1)}, bf16[4,5,128,128]{3,2,1,0:T(8,128)(2,1)S(1)}, bf16[1536,4096]{1,0:T(8,128)(2,1)S(1)}) custom-call(bf16[1536,4096]{1,0:T(8,128)(2,1)} %bitcast.3), custom_call_target="tpu_custom_call" | custom-call | flops 2617245696 | bytes 12582912 | tf_op jit(solution)/shard_map/pallas_call | solution.py:181
  6.6 1.5 %collective-permute-start = (bf16[4,5,128,128]{3,2,1,0:T(8,128)(2,1)S(1)}, bf16[4,5,128,128]{3,2,1,0:T(8,128)(2,1)S(1)}, u32[]{:S(2)}, u32[]{:S(2)}) collective-permute-start(bf16[4,5,128,128]{3,2,1,0:T(8,128)(2,1)S(1)} %get-tuple-element.30), channel_id=1, source_target_pairs={{0,16},{1,17},{2,18},{3,19},{4,20},{5,21},{6,22},{7,23},{8,24},{9,... | collective-permute-start | bytes 1966088 | tf_op jit(solution)/shard_map/ppermute | solution.py:70
  8.1 0.0 copy-done.1
  8.1 3.2 %shard_map.39 = (bf16[4,5,128,128]{3,2,1,0:T(8,128)(2,1)S(1)}, bf16[4,5,128,128]{3,2,1,0:T(8,128)(2,1)S(1)}) custom-call(bf16[1536,4096]{1,0:T(8,128)(2,1)S(1)} %get-tuple-element.28.flat_ref, s32[32]{0:T(128)S(1)} %copy-done.1), custom_call_target="tpu_custom_call" | custom-call | flops 2617245696 | tf_op jit(solution)/shard_map/pallas_call | solution.py:197
  11.3 0.1 collective-permute-start.3
  11.5 0.0 collective-permute-done
  11.5 0.2 add_convert_fusion.2
  11.7 2.9 %collective-permute-start.1 = (bf16[4,5,128,128]{3,2,1,0:T(8,128)(2,1)S(1)}, bf16[4,5,128,128]{3,2,1,0:T(8,128)(2,1)S(1)}, u32[]{:S(2)}, u32[]{:S(2)}) collective-permute-start(bf16[4,5,128,128]{3,2,1,0:T(8,128)(2,1)S(1)} %add_convert_fusion.2), channel_id=1, source_target_pairs={{0,8},{1,9},{2,10},{3,11},{4,12},{5,13},{6,14},{7,15},{8,0},{9,1},... | collective-permute-start | bytes 1966088 | tf_op jit(solution)/shard_map/ppermute | solution.py:70
  14.6 0.0 collective-permute-done.3
  14.6 0.2 add_convert_fusion.1.after_ref
  14.8 3.3 %shard_map.40 = (bf16[4,5,128,128]{3,2,1,0:T(8,128)(2,1)S(1)}, bf16[2,5,128,128]{3,2,1,0:T(8,128)(2,1)S(1)}, bf16[2,5,128,128]{3,2,1,0:T(8,128)(2,1)S(1)}) custom-call(bf16[1536,4096]{1,0:T(8,128)(2,1)S(1)} %get-tuple-element.28.flat_ref, bf16[4,5,128,128]{3,2,1,0:T(8,128)(2,1)S(1)} %add_convert_fusion.1.after_ref), custom_call_target="tpu_custom_call" | custom-call | flops 2617245696 | tf_op jit(solution)/shard_map/pallas_call | solution.py:197
  18.0 0.0 copy-start
  18.0 1.0 %collective-permute-start.5 = (bf16[2,5,128,128]{3,2,1,0:T(8,128)(2,1)S(1)}, bf16[2,5,128,128]{3,2,1,0:T(8,128)(2,1)S(1)}, u32[]{:S(2)}, u32[]{:S(2)}) collective-permute-start(bf16[2,5,128,128]{3,2,1,0:T(8,128)(2,1)S(1)} %get-tuple-element.37), channel_id=1, source_target_pairs={{0,16},{1,17},{2,18},{3,19},{4,20},{5,21},{6,22},{7,23},{8,24},{9,... | collective-permute-start | bytes 983048 | tf_op jit(solution)/shard_map/ppermute | solution.py:70
  19.0 0.1 collective-permute-start.6
  19.1 1.2 %collective-permute-start.4 = (bf16[4,5,128,128]{3,2,1,0:T(8,128)(2,1)S(1)}, bf16[4,5,128,128]{3,2,1,0:T(8,128)(2,1)S(1)}, u32[]{:S(2)}, u32[]{:S(2)}) collective-permute-start(bf16[4,5,128,128]{3,2,1,0:T(8,128)(2,1)S(1)} %add_convert_fusion.1.after_ref), channel_id=1, source_target_pairs={{0,4},{1,5},{2,6},{3,7},{4,8},{5,9},{6,10},{7,11},{8,12},{9,13},{1... | collective-permute-start | bytes 1966088 | tf_op jit(solution)/shard_map/ppermute | solution.py:70
  20.3 0.0 collective-permute-done.5
  20.3 0.4 collective-permute-done.6
  20.8 0.2 add_convert_fusion
  20.9 2.7 %collective-permute-start.7 = (bf16[4,5,128,128]{3,2,1,0:T(8,128)(2,1)S(1)}, bf16[4,5,128,128]{3,2,1,0:T(8,128)(2,1)S(1)}, u32[]{:S(2)}, u32[]{:S(2)}) collective-permute-start(bf16[4,5,128,128]{3,2,1,0:T(8,128)(2,1)S(1)} %add_convert_fusion), channel_id=1, source_target_pairs={{0,12},{1,13},{2,14},{3,15},{4,0},{5,1},{6,2},{7,3},{8,4},{9,5},{1... | collective-permute-start | bytes 1966088 | tf_op jit(solution)/shard_map/ppermute | solution.py:70
  23.6 0.0 collective-permute-done.1.after_ref.refs_2_
  23.6 0.0 copy-done
  23.6 3.8 %shard_map.38 = (bf16[4,5,128,128]{3,2,1,0:T(8,128)(2,1)S(1)}, bf16[4,5,128,128]{3,2,1,0:T(8,128)(2,1)S(1)}, f32[32,1152]{1,0:T(8,128)S(1)}) custom-call(s32[32]{0:T(128)S(1)} %copy-done.1, s32[5,32]{1,0:T(8,128)S(1)} %bitcast.2, bf16[1536,4096]{1,0:T(8,128)(2,1)S(1)} %get-tuple-element.28.flat_ref, ...), custom_call_target="tpu_custom_call" | custom-call | flops 2617245696 | tf_op jit(solution)/shard_map/pallas_call | solution.py:209
  27.5 0.7 %collective-permute-start.2 = (bf16[4,5,128,128]{3,2,1,0:T(8,128)(2,1)S(1)}, bf16[4,5,128,128]{3,2,1,0:T(8,128)(2,1)S(1)}, u32[]{:S(2)}, u32[]{:S(2)}) collective-permute-start(bf16[4,5,128,128]{3,2,1,0:T(8,128)(2,1)S(1)} %get-tuple-element.33), channel_id=1, source_target_pairs={{0,16},{1,17},{2,18},{3,19},{4,20},{5,21},{6,22},{7,23},{8,24},{9,... | collective-permute-start | bytes 1966088 | tf_op jit(solution)/shard_map/ppermute | solution.py:70
  28.2 1.9 %collective-permute-done.4.refs_3_ = bf16[4,5,128,128]{3,2,1,0:T(8,128)(2,1)S(1)} collective-permute-done((bf16[4,5,128,128]{3,2,1,0:T(8,128)(2,1)S(1)}, bf16[4,5,128,128]{3,2,1,0:T(8,128)(2,1)S(1)}, u32[]{:S(2)}, u32[]{:S(2)}) %collective-permute-start.4) | collective-permute-done | bytes 655392 | tf_op jit(solution)/shard_map/ppermute | solution.py:70
  30.1 1.1 %collective-permute-done.7.refs_4_ = bf16[4,5,128,128]{3,2,1,0:T(8,128)(2,1)S(1)} collective-permute-done((bf16[4,5,128,128]{3,2,1,0:T(8,128)(2,1)S(1)}, bf16[4,5,128,128]{3,2,1,0:T(8,128)(2,1)S(1)}, u32[]{:S(2)}, u32[]{:S(2)}) %collective-permute-start.7) | collective-permute-done | bytes 655392 | tf_op jit(solution)/shard_map/ppermute | solution.py:70
  31.2 0.0 collective-permute-done.2.refs_1_
  31.2 0.4 shard_map.41
  31.6 0.6 collective-permute-start.10
  32.1 2.6 %collective-permute-start.8 = (bf16[5,128,128]{2,1,0:T(8,128)(2,1)S(1)}, bf16[5,128,128]{2,1,0:T(8,128)(2,1)S(1)}, u32[]{:S(2)}, u32[]{:S(2)}) collective-permute-start(bf16[5,128,128]{2,1,0:T(8,128)(2,1)S(1)} %get-tuple-element.40), channel_id=1, source_target_pairs={{0,2},{1,3},{2,0},{3,1},{4,6},{5,7},{6,4},{7,5},{8,10},{9,11},{10,... | collective-permute-start | bytes 491528 | tf_op jit(solution)/shard_map/ppermute | solution.py:70
  34.8 1.1 %collective-permute-start.9 = (bf16[5,128,128]{2,1,0:T(8,128)(2,1)S(1)}, bf16[5,128,128]{2,1,0:T(8,128)(2,1)S(1)}, u32[]{:S(2)}, u32[]{:S(2)}) collective-permute-start(bf16[5,128,128]{2,1,0:T(8,128)(2,1)S(1)} %get-tuple-element.41), channel_id=1, source_target_pairs={{0,3},{1,0},{2,1},{3,2},{4,7},{5,4},{6,5},{7,6},{8,11},{9,8},{10,9... | collective-permute-start | bytes 491528 | tf_op jit(solution)/shard_map/ppermute | solution.py:70
  35.8 1.5 %collective-permute-done.10.third_ref = bf16[5,128,128]{2,1,0:T(8,128)(2,1)S(1)} collective-permute-done((bf16[5,128,128]{2,1,0:T(8,128)(2,1)S(1)}, bf16[5,128,128]{2,1,0:T(8,128)(2,1)S(1)}, u32[]{:S(2)}, u32[]{:S(2)}) %collective-permute-start.10) | collective-permute-done | bytes 163872 | tf_op jit(solution)/shard_map/ppermute | solution.py:70
  37.3 1.9 %collective-permute-done.8.first_ref = bf16[5,128,128]{2,1,0:T(8,128)(2,1)S(1)} collective-permute-done((bf16[5,128,128]{2,1,0:T(8,128)(2,1)S(1)}, bf16[5,128,128]{2,1,0:T(8,128)(2,1)S(1)}, u32[]{:S(2)}, u32[]{:S(2)}) %collective-permute-start.8) | collective-permute-done | bytes 163872 | tf_op jit(solution)/shard_map/ppermute | solution.py:70
  39.2 0.1 collective-permute-done.9.second_ref
  39.4 0.4 shard_map.42
  39.7 1.7 %collective-permute-start.11 = (bf16[6,64,128]{2,1,0:T(8,128)(2,1)S(1)}, bf16[6,64,128]{2,1,0:T(8,128)(2,1)S(1)}, u32[]{:S(2)}, u32[]{:S(2)}) collective-permute-start(bf16[6,64,128]{2,1,0:T(8,128)(2,1)S(1)} %get-tuple-element.45), channel_id=1, source_target_pairs={{0,32},{1,33},{2,34},{3,35},{4,36},{5,37},{6,38},{7,39},{8,40},{9,... | collective-permute-start | bytes 294920 | tf_op jit(solution)/shard_map/ppermute | solution.py:70
  41.4 2.2 %collective-permute-start.12 = (bf16[6,64,128]{2,1,0:T(8,128)(2,1)S(1)}, bf16[6,64,128]{2,1,0:T(8,128)(2,1)S(1)}, u32[]{:S(2)}, u32[]{:S(2)}) collective-permute-start(bf16[6,64,128]{2,1,0:T(8,128)(2,1)S(1)} %get-tuple-element.46), channel_id=1, source_target_pairs={{0,96},{1,97},{2,98},{3,99},{4,100},{5,101},{6,102},{7,103},{8,104... | collective-permute-start | bytes 294920 | tf_op jit(solution)/shard_map/ppermute | solution.py:70
  43.6 1.2 %collective-permute-start.13 = (bf16[6,64,128]{2,1,0:T(8,128)(2,1)S(1)}, bf16[6,64,128]{2,1,0:T(8,128)(2,1)S(1)}, u32[]{:S(2)}, u32[]{:S(2)}) collective-permute-start(bf16[6,64,128]{2,1,0:T(8,128)(2,1)S(1)} %get-tuple-element.47), channel_id=1, source_target_pairs={{0,64},{1,65},{2,66},{3,67},{4,68},{5,69},{6,70},{7,71},{8,72},{9,... | collective-permute-start | bytes 294920 | tf_op jit(solution)/shard_map/ppermute | solution.py:70
  44.9 0.7 %collective-permute-done.11.refs_0_ = bf16[6,64,128]{2,1,0:T(8,128)(2,1)S(1)} collective-permute-done((bf16[6,64,128]{2,1,0:T(8,128)(2,1)S(1)}, bf16[6,64,128]{2,1,0:T(8,128)(2,1)S(1)}, u32[]{:S(2)}, u32[]{:S(2)}) %collective-permute-start.11) | collective-permute-done | bytes 98336 | tf_op jit(solution)/shard_map/ppermute | solution.py:70
  45.6 0.0 collective-permute-done.12.refs_1_
  45.6 3.1 %collective-permute-done.13.refs_2_ = bf16[6,64,128]{2,1,0:T(8,128)(2,1)S(1)} collective-permute-done((bf16[6,64,128]{2,1,0:T(8,128)(2,1)S(1)}, bf16[6,64,128]{2,1,0:T(8,128)(2,1)S(1)}, u32[]{:S(2)}, u32[]{:S(2)}) %collective-permute-start.13) | collective-permute-done | bytes 98336 | tf_op jit(solution)/shard_map/ppermute | solution.py:70
  48.7 0.1 shard_map.43
  48.8 2.9 %collective-permute-start.15 = (f32[2,64,128]{2,1,0:T(8,128)S(1)}, f32[2,64,128]{2,1,0:T(8,128)S(1)}, u32[]{:S(2)}, u32[]{:S(2)}) collective-permute-start(f32[2,64,128]{2,1,0:T(8,128)S(1)} %get-tuple-element.50), channel_id=1, source_target_pairs={{0,1},{1,2},{2,3},{3,4},{4,5},{5,6},{6,7},{7,8},{8,9},{9,10},{10,1... | collective-permute-start | bytes 196616 | tf_op jit(solution)/shard_map/ppermute | solution.py:70
  51.7 2.9 %collective-permute-start.14 = (f32[4,32,128]{2,1,0:T(8,128)S(1)}, f32[4,32,128]{2,1,0:T(8,128)S(1)}, u32[]{:S(2)}, u32[]{:S(2)}) collective-permute-start(f32[4,32,128]{2,1,0:T(8,128)S(1)} %get-tuple-element.49), channel_id=1, source_target_pairs={{0,16},{1,17},{2,18},{3,19},{4,20},{5,21},{6,22},{7,23},{8,24},{9,... | collective-permute-start | bytes 196616 | tf_op jit(solution)/shard_map/ppermute | solution.py:70
  54.6 1.0 %collective-permute-done.15.own_lower_ref = f32[2,64,128]{2,1,0:T(8,128)S(1)} collective-permute-done((f32[2,64,128]{2,1,0:T(8,128)S(1)}, f32[2,64,128]{2,1,0:T(8,128)S(1)}, u32[]{:S(2)}, u32[]{:S(2)}) %collective-permute-start.15) | collective-permute-done | bytes 65568 | tf_op jit(solution)/shard_map/ppermute | solution.py:70
  55.6 5.0 %collective-permute-start.16 = (f32[2,64,128]{2,1,0:T(8,128)S(1)}, f32[2,64,128]{2,1,0:T(8,128)S(1)}, u32[]{:S(2)}, u32[]{:S(2)}) collective-permute-start(f32[2,64,128]{2,1,0:T(8,128)S(1)} %collective-permute-done.15.own_lower_ref), channel_id=1, source_target_pairs={{0,16},{1,17},{2,18},{3,19},{4,20},{5,21},{6,22},{7,23},{8,24},{9,... | collective-permute-start | bytes 196616 | tf_op jit(solution)/shard_map/ppermute | solution.py:70
  60.5 0.0 collective-permute-done.14.other_upper_ref
  60.5 0.9 %collective-permute-done.16.other_lower_ref = f32[2,64,128]{2,1,0:T(8,128)S(1)} collective-permute-done((f32[2,64,128]{2,1,0:T(8,128)S(1)}, f32[2,64,128]{2,1,0:T(8,128)S(1)}, u32[]{:S(2)}, u32[]{:S(2)}) %collective-permute-start.16) | collective-permute-done | bytes 65568 | tf_op jit(solution)/shard_map/ppermute | solution.py:70
  61.4 0.7 %shard_map.44 = f32[32,1152]{1,0:T(8,128)} custom-call(f32[32,1152]{1,0:T(8,128)S(1)} %get-tuple-element.31.mask_ref, f32[4,32,128]{2,1,0:T(8,128)S(1)} %get-tuple-element.48.own_upper_ref, f32[4,32,128]{2,1,0:T(8,128)S(1)} %collective-permute-done.14.other_upper_ref, f32[2,64,128]{2,1,0:T(8,128)S(1)} %collective-permute-done.15.own_lower_ref, ...), custom_call_target="tpu_custom_call" | custom-call | tf_op jit(solution)/shard_map/pallas_call | solution.py:352
  (1 shorter events, 0.0 us)
Async XLA Ops:
  0.0 8.1 %copy-start.1 = (s32[32]{0:T(128)S(1)}, s32[32]{0:T(128)}, u32[]{:S(2)}) copy-start(s32[32]{0:T(128)} %after_ref.1) | copy-start | bytes 388
  6.6 4.9 %collective-permute-start = (bf16[4,5,128,128]{3,2,1,0:T(8,128)(2,1)S(1)}, bf16[4,5,128,128]{3,2,1,0:T(8,128)(2,1)S(1)}, u32[]{:S(2)}, u32[]{:S(2)}) collective-permute-start(bf16[4,5,128,128]{3,2,1,0:T(8,128)(2,1)S(1)} %get-tuple-element.30), channel_id=1, source_target_pairs={{0,16},{1,17},{2,18},{3,19},{4,20},{5,21},{6,22},{7,23},{8,24},{9,... | collective-permute-start | bytes 1966088 | tf_op jit(solution)/shard_map/ppermute | solution.py:70
  11.3 3.2 %collective-permute-start.3 = (bf16[4,5,128,128]{3,2,1,0:T(8,128)(2,1)S(1)}, bf16[4,5,128,128]{3,2,1,0:T(8,128)(2,1)S(1)}, u32[]{:S(2)}, u32[]{:S(2)}) collective-permute-start(bf16[4,5,128,128]{3,2,1,0:T(8,128)(2,1)S(1)} %get-tuple-element.35), channel_id=1, source_target_pairs={{0,16},{1,17},{2,18},{3,19},{4,20},{5,21},{6,22},{7,23},{8,24},{9,... | collective-permute-start | bytes 1966088 | tf_op jit(solution)/shard_map/ppermute | solution.py:70
  11.7 12.0 %collective-permute-start.1 = (bf16[4,5,128,128]{3,2,1,0:T(8,128)(2,1)S(1)}, bf16[4,5,128,128]{3,2,1,0:T(8,128)(2,1)S(1)}, u32[]{:S(2)}, u32[]{:S(2)}) collective-permute-start(bf16[4,5,128,128]{3,2,1,0:T(8,128)(2,1)S(1)} %add_convert_fusion.2), channel_id=1, source_target_pairs={{0,8},{1,9},{2,10},{3,11},{4,12},{5,13},{6,14},{7,15},{8,0},{9,1},... | collective-permute-start | bytes 1966088 | tf_op jit(solution)/shard_map/ppermute | solution.py:70
  18.0 5.6 %copy-start = (s32[32,5]{0,1:T(8,128)S(1)}, s32[32,5]{0,1:T(8,128)}, u32[]{:S(2)}) copy-start(s32[32,5]{0,1:T(8,128)} %param.5) | copy-start | bytes 1924
  18.0 2.3 %collective-permute-start.5 = (bf16[2,5,128,128]{3,2,1,0:T(8,128)(2,1)S(1)}, bf16[2,5,128,128]{3,2,1,0:T(8,128)(2,1)S(1)}, u32[]{:S(2)}, u32[]{:S(2)}) collective-permute-start(bf16[2,5,128,128]{3,2,1,0:T(8,128)(2,1)S(1)} %get-tuple-element.37), channel_id=1, source_target_pairs={{0,16},{1,17},{2,18},{3,19},{4,20},{5,21},{6,22},{7,23},{8,24},{9,... | collective-permute-start | bytes 983048 | tf_op jit(solution)/shard_map/ppermute | solution.py:70
  19.0 1.7 %collective-permute-start.6 = (bf16[2,5,128,128]{3,2,1,0:T(8,128)(2,1)S(1)}, bf16[2,5,128,128]{3,2,1,0:T(8,128)(2,1)S(1)}, u32[]{:S(2)}, u32[]{:S(2)}) collective-permute-start(bf16[2,5,128,128]{3,2,1,0:T(8,128)(2,1)S(1)} %get-tuple-element.38), channel_id=1, source_target_pairs={{0,16},{1,17},{2,18},{3,19},{4,20},{5,21},{6,22},{7,23},{8,24},{9,... | collective-permute-start | bytes 983048 | tf_op jit(solution)/shard_map/ppermute | solution.py:70
  19.1 10.9 %collective-permute-start.4 = (bf16[4,5,128,128]{3,2,1,0:T(8,128)(2,1)S(1)}, bf16[4,5,128,128]{3,2,1,0:T(8,128)(2,1)S(1)}, u32[]{:S(2)}, u32[]{:S(2)}) collective-permute-start(bf16[4,5,128,128]{3,2,1,0:T(8,128)(2,1)S(1)} %add_convert_fusion.1.after_ref), channel_id=1, source_target_pairs={{0,4},{1,5},{2,6},{3,7},{4,8},{5,9},{6,10},{7,11},{8,12},{9,13},{1... | collective-permute-start | bytes 1966088 | tf_op jit(solution)/shard_map/ppermute | solution.py:70
  20.9 10.2 %collective-permute-start.7 = (bf16[4,5,128,128]{3,2,1,0:T(8,128)(2,1)S(1)}, bf16[4,5,128,128]{3,2,1,0:T(8,128)(2,1)S(1)}, u32[]{:S(2)}, u32[]{:S(2)}) collective-permute-start(bf16[4,5,128,128]{3,2,1,0:T(8,128)(2,1)S(1)} %add_convert_fusion), channel_id=1, source_target_pairs={{0,12},{1,13},{2,14},{3,15},{4,0},{5,1},{6,2},{7,3},{8,4},{9,5},{1... | collective-permute-start | bytes 1966088 | tf_op jit(solution)/shard_map/ppermute | solution.py:70
  27.5 3.7 %collective-permute-start.2 = (bf16[4,5,128,128]{3,2,1,0:T(8,128)(2,1)S(1)}, bf16[4,5,128,128]{3,2,1,0:T(8,128)(2,1)S(1)}, u32[]{:S(2)}, u32[]{:S(2)}) collective-permute-start(bf16[4,5,128,128]{3,2,1,0:T(8,128)(2,1)S(1)} %get-tuple-element.33), channel_id=1, source_target_pairs={{0,16},{1,17},{2,18},{3,19},{4,20},{5,21},{6,22},{7,23},{8,24},{9,... | collective-permute-start | bytes 1966088 | tf_op jit(solution)/shard_map/ppermute | solution.py:70
  31.6 5.7 %collective-permute-start.10 = (bf16[5,128,128]{2,1,0:T(8,128)(2,1)S(1)}, bf16[5,128,128]{2,1,0:T(8,128)(2,1)S(1)}, u32[]{:S(2)}, u32[]{:S(2)}) collective-permute-start(bf16[5,128,128]{2,1,0:T(8,128)(2,1)S(1)} %get-tuple-element.42), channel_id=1, source_target_pairs={{0,1},{1,2},{2,3},{3,0},{4,5},{5,6},{6,7},{7,4},{8,9},{9,10},{10,1... | collective-permute-start | bytes 491528 | tf_op jit(solution)/shard_map/ppermute | solution.py:70
  32.1 7.1 %collective-permute-start.8 = (bf16[5,128,128]{2,1,0:T(8,128)(2,1)S(1)}, bf16[5,128,128]{2,1,0:T(8,128)(2,1)S(1)}, u32[]{:S(2)}, u32[]{:S(2)}) collective-permute-start(bf16[5,128,128]{2,1,0:T(8,128)(2,1)S(1)} %get-tuple-element.40), channel_id=1, source_target_pairs={{0,2},{1,3},{2,0},{3,1},{4,6},{5,7},{6,4},{7,5},{8,10},{9,11},{10,... | collective-permute-start | bytes 491528 | tf_op jit(solution)/shard_map/ppermute | solution.py:70
  34.8 4.6 %collective-permute-start.9 = (bf16[5,128,128]{2,1,0:T(8,128)(2,1)S(1)}, bf16[5,128,128]{2,1,0:T(8,128)(2,1)S(1)}, u32[]{:S(2)}, u32[]{:S(2)}) collective-permute-start(bf16[5,128,128]{2,1,0:T(8,128)(2,1)S(1)} %get-tuple-element.41), channel_id=1, source_target_pairs={{0,3},{1,0},{2,1},{3,2},{4,7},{5,4},{6,5},{7,6},{8,11},{9,8},{10,9... | collective-permute-start | bytes 491528 | tf_op jit(solution)/shard_map/ppermute | solution.py:70
  39.7 5.8 %collective-permute-start.11 = (bf16[6,64,128]{2,1,0:T(8,128)(2,1)S(1)}, bf16[6,64,128]{2,1,0:T(8,128)(2,1)S(1)}, u32[]{:S(2)}, u32[]{:S(2)}) collective-permute-start(bf16[6,64,128]{2,1,0:T(8,128)(2,1)S(1)} %get-tuple-element.45), channel_id=1, source_target_pairs={{0,32},{1,33},{2,34},{3,35},{4,36},{5,37},{6,38},{7,39},{8,40},{9,... | collective-permute-start | bytes 294920 | tf_op jit(solution)/shard_map/ppermute | solution.py:70
  41.4 4.1 %collective-permute-start.12 = (bf16[6,64,128]{2,1,0:T(8,128)(2,1)S(1)}, bf16[6,64,128]{2,1,0:T(8,128)(2,1)S(1)}, u32[]{:S(2)}, u32[]{:S(2)}) collective-permute-start(bf16[6,64,128]{2,1,0:T(8,128)(2,1)S(1)} %get-tuple-element.46), channel_id=1, source_target_pairs={{0,96},{1,97},{2,98},{3,99},{4,100},{5,101},{6,102},{7,103},{8,104... | collective-permute-start | bytes 294920 | tf_op jit(solution)/shard_map/ppermute | solution.py:70
  43.6 5.1 %collective-permute-start.13 = (bf16[6,64,128]{2,1,0:T(8,128)(2,1)S(1)}, bf16[6,64,128]{2,1,0:T(8,128)(2,1)S(1)}, u32[]{:S(2)}, u32[]{:S(2)}) collective-permute-start(bf16[6,64,128]{2,1,0:T(8,128)(2,1)S(1)} %get-tuple-element.47), channel_id=1, source_target_pairs={{0,64},{1,65},{2,66},{3,67},{4,68},{5,69},{6,70},{7,71},{8,72},{9,... | collective-permute-start | bytes 294920 | tf_op jit(solution)/shard_map/ppermute | solution.py:70
  48.8 6.8 %collective-permute-start.15 = (f32[2,64,128]{2,1,0:T(8,128)S(1)}, f32[2,64,128]{2,1,0:T(8,128)S(1)}, u32[]{:S(2)}, u32[]{:S(2)}) collective-permute-start(f32[2,64,128]{2,1,0:T(8,128)S(1)} %get-tuple-element.50), channel_id=1, source_target_pairs={{0,1},{1,2},{2,3},{3,4},{4,5},{5,6},{6,7},{7,8},{8,9},{9,10},{10,1... | collective-permute-start | bytes 196616 | tf_op jit(solution)/shard_map/ppermute | solution.py:70
  51.7 8.9 %collective-permute-start.14 = (f32[4,32,128]{2,1,0:T(8,128)S(1)}, f32[4,32,128]{2,1,0:T(8,128)S(1)}, u32[]{:S(2)}, u32[]{:S(2)}) collective-permute-start(f32[4,32,128]{2,1,0:T(8,128)S(1)} %get-tuple-element.49), channel_id=1, source_target_pairs={{0,16},{1,17},{2,18},{3,19},{4,20},{5,21},{6,22},{7,23},{8,24},{9,... | collective-permute-start | bytes 196616 | tf_op jit(solution)/shard_map/ppermute | solution.py:70
  55.6 5.9 %collective-permute-start.16 = (f32[2,64,128]{2,1,0:T(8,128)S(1)}, f32[2,64,128]{2,1,0:T(8,128)S(1)}, u32[]{:S(2)}, u32[]{:S(2)}) collective-permute-start(f32[2,64,128]{2,1,0:T(8,128)S(1)} %collective-permute-done.15.own_lower_ref), channel_id=1, source_target_pairs={{0,16},{1,17},{2,18},{3,19},{4,20},{5,21},{6,22},{7,23},{8,24},{9,... | collective-permute-start | bytes 196616 | tf_op jit(solution)/shard_map/ppermute | solution.py:70
